TPU v7x, 32 devices: a whole 2x2x4 slice. The times are simulated.
32 devices in a mesh: wide: 16 (over z, y, x), narrow: 2 (over core).
Axes of the slice: x: 2, y: 2, z: 4, core: 2. Of those that a mesh axis runs over, the one named last changes fastest.
Arguments:
- tokens: bfloat16 [16, 12288, 512], P('narrow', 'wide')
- cotangent: bfloat16 [16, 12288, 512], P('narrow', 'wide'), may hold values from -6 to 6
- owner_list: int32 [12], replicated, may hold values from 0 to 15, as said below
- master: float32 [16, 512, 512], P('wide', 'narrow')
- moment_one: float32 [16, 512, 512], P('wide', 'narrow'), may hold values from -112 to 112
- moment_two: float32 [16, 512, 512], P('wide', 'narrow'), may hold values from 825.7536 to 13172.736
- small_params: float32 [4608], replicated
- small_one: float32 [4608], replicated, may hold values from -128 to 128
- small_two: float32 [4608], replicated, may hold values from 1297.6128 to 20643.84
Outputs:
- block_out: bfloat16 [16, 12288, 512], P('narrow', 'wide')
- grad_tokens: float32 [16, 12288, 512], P('narrow', 'wide')
- new_master: float32 [16, 512, 512], P('wide', 'narrow')
- new_one: float32 [16, 512, 512], P('wide', 'narrow')
- new_two: float32 [16, 512, 512], P('wide', 'narrow')
- small_new: float32 [4608], replicated
- small_one_new: float32 [4608], replicated
- small_two_new: float32 [4608], replicated
Inputs may be any that keep to these rules, and one draw needn't show every extreme that they name: `owner_list`: 12 different slot indices; 0 and 15 are always among them.
All inputs are finite; a program needn't handle non-finite values.
Results may differ from a plain program's by a relative error of at most 0.025.
Values may be sent and summed in bfloat16 or wider, within the bound.
No kernel may reach another device: no remote copies, remote signals or barrier semaphores. Data moves between devices by JAX's collectives and lax.ppermute only.
A program may use at most 512 MiB of HBM per device.

v0:
```python
import math

import jax
import jax.numpy as jnp
from jax import lax
from jax.sharding import PartitionSpec as P

D = 512
HEADS = 8
HD = 64
FF = 2048
ROW = 192
ROWS_IMG = 64
STEP = 10


RATE = 0.03
GAIN_RATE = 0.4


def layer_norm(values, gain, shift):
    centre = jnp.mean(values, -1, keepdims=True)
    centred = values - centre
    spread = jnp.mean(centred * centred, -1, keepdims=True)
    return centred * lax.rsqrt(spread + 1e-05) * gain + shift


def adamw_update(weight_now, gradient, first_moment, second_moment, decay_rate, step_rate):
    first_new = 0.9 * first_moment + 0.1 * gradient
    second_new = 0.95 * second_moment + 0.05 * gradient * gradient
    direction = first_new / (1.0 - 0.9**STEP) / (jnp.sqrt(second_new / (1.0 - 0.95**STEP)) + 1e-08)
    return (weight_now - step_rate * (direction + decay_rate * weight_now), first_new, second_new)


def fetch_blocks(master, owner_list):
    shard_low = master.astype(jnp.bfloat16)
    joined = lax.all_gather(shard_low.reshape(-1, D), ("wide", "narrow"), axis=0, tiled=True)
    return jnp.take(joined.reshape(-1, D, D), owner_list, axis=0)


def per_device(
    tokens,
    cotangent,
    owner_list,
    master,
    moment_one,
    moment_two,
    small_params,
    small_one,
    small_two,
):
    f32 = jnp.float32
    bf16 = jnp.bfloat16
    image_count = tokens.shape[0]
    wide_size = lax.axis_size("wide")
    rows_here = ROWS_IMG // wide_size
    ff_blocks = FF // D
    score_scale = 1.0 / math.sqrt(HD)
    five_shape = (image_count, rows_here, ROW, HEADS, HD)
    blocks = fetch_blocks(master, owner_list)
    gain_one = small_params[0:D]
    shift_one = small_params[D : 2 * D]
    gain_two = small_params[2 * D : 3 * D]
    shift_two = small_params[3 * D : 4 * D]
    bias_up = small_params[4 * D : 4 * D + FF]
    bias_down = small_params[4 * D + FF :]
    inputs = tokens.astype(f32).reshape(-1, D)
    normed_one, norm_back_one = jax.vjp(layer_norm, inputs, gain_one, shift_one)
    low_one = normed_one.astype(bf16)
    projected = jnp.einsum("nd,jde->nje", low_one, blocks[0:3], preferred_element_type=f32).astype(
        bf16
    )
    queries = projected[:, 0].reshape(five_shape)
    key_heads = projected[:, 1].reshape(five_shape)
    value_heads = projected[:, 2].reshape(five_shape)
    sum_keys = jnp.mean(
        projected[:, 1].reshape(image_count, rows_here, ROW, D), axis=2, dtype=f32
    ).astype(bf16)
    sum_values = jnp.mean(
        projected[:, 2].reshape(image_count, rows_here, ROW, D), axis=2, dtype=f32
    ).astype(bf16)
    all_keys, all_values = (
        lax.all_gather(sum_keys, "wide", axis=1, tiled=True),
        lax.all_gather(sum_values, "wide", axis=1, tiled=True),
    )
    summ_key_heads = all_keys.reshape(image_count, ROWS_IMG, HEADS, HD)
    summ_value_heads = all_values.reshape(image_count, ROWS_IMG, HEADS, HD)
    columns = jnp.arange(ROW, dtype=jnp.int32)
    causal = columns[None, :] <= columns[:, None]
    query_rows = lax.axis_index("wide") * rows_here + jnp.arange(rows_here, dtype=jnp.int32)
    earlier = jnp.arange(ROWS_IMG, dtype=jnp.int32)[None, :] < query_rows[:, None]
    local_scores = (
        jnp.einsum("irqhd,irkhd->irhqk", queries, key_heads, preferred_element_type=f32)
        * score_scale
    )
    local_scores = jnp.where(causal, local_scores, -1e30)
    summ_scores = jnp.einsum(
        "irqhd,ishd->irhqs", queries, summ_key_heads, preferred_element_type=f32
    ) * score_scale + math.log(ROW)
    summ_scores = jnp.where(earlier[None, :, None, None, :], summ_scores, -1e30)
    log_total = jnp.logaddexp(jax.nn.logsumexp(local_scores, -1), jax.nn.logsumexp(summ_scores, -1))
    local_probs = jnp.exp(local_scores - log_total[..., None])
    summ_probs = jnp.exp(summ_scores - log_total[..., None])
    local_low = local_probs.astype(bf16)
    summ_low = summ_probs.astype(bf16)
    attended = jnp.einsum("irhqk,irkhd->irqhd", local_low, value_heads, preferred_element_type=f32)
    attended = attended + jnp.einsum(
        "irhqs,ishd->irqhd", summ_low, summ_value_heads, preferred_element_type=f32
    )
    attended = attended.astype(bf16).reshape(-1, D)
    hidden_one = inputs + jnp.dot(attended, blocks[3], preferred_element_type=f32)
    normed_two, norm_back_two = jax.vjp(layer_norm, hidden_one, gain_two, shift_two)
    low_two = normed_two.astype(bf16)
    pre_act = (
        jnp.einsum(
            "nd,jde->nje", low_two, blocks[4 : 4 + ff_blocks], preferred_element_type=f32
        ).reshape(-1, FF)
        + bias_up
    )
    activated, gelu_back = jax.vjp(jax.nn.gelu, pre_act)
    act_low = activated.astype(bf16)
    w_down = blocks[4 + ff_blocks :].reshape(FF, D)
    block_out = (
        (hidden_one + jnp.dot(act_low, w_down, preferred_element_type=f32) + bias_down)
        .astype(bf16)
        .reshape(tokens.shape)
    )
    back_blocks = fetch_blocks(master, owner_list)
    cot_rows = cotangent.reshape(-1, D)
    cot_float = cot_rows.astype(f32)
    grad_act = jnp.einsum(
        "nd,fd->nf",
        cot_rows,
        back_blocks[4 + ff_blocks :].reshape(FF, D),
        preferred_element_type=f32,
    )
    grad_pre = gelu_back(grad_act)[0].astype(bf16)
    grad_pre_blocks = grad_pre.reshape(-1, ff_blocks, D)
    grad_down = jnp.einsum("nf,nd->fd", act_low, cot_rows, preferred_element_type=f32)
    grad_up = jnp.einsum("nd,nje->jde", low_two, grad_pre_blocks, preferred_element_type=f32)
    bias_down_grad = jnp.sum(cot_float, 0)
    bias_up_grad = jnp.sum(grad_pre, 0, dtype=f32)
    grad_low_two = jnp.einsum(
        "nje,jde->nd", grad_pre_blocks, back_blocks[4 : 4 + ff_blocks], preferred_element_type=f32
    )
    grad_hidden, gain_two_grad, shift_two_grad = norm_back_two(grad_low_two)
    grad_hidden = grad_hidden + cot_float
    grad_branch = grad_hidden.astype(bf16)
    grad_wout = jnp.einsum("nd,ne->de", attended, grad_branch, preferred_element_type=f32)
    grad_attended = (
        jnp.einsum("ne,de->nd", grad_branch, back_blocks[3], preferred_element_type=f32)
        .astype(bf16)
        .reshape(five_shape)
    )
    local_dp = jnp.einsum(
        "irqhd,irkhd->irhqk", grad_attended, value_heads, preferred_element_type=f32
    )
    summ_dp = jnp.einsum(
        "irqhd,ishd->irhqs", grad_attended, summ_value_heads, preferred_element_type=f32
    )
    value_grad_local = jnp.einsum(
        "irhqk,irqhd->irkhd", local_low, grad_attended, preferred_element_type=f32
    )
    summ_value_grad = jnp.einsum(
        "irhqs,irqhd->ishd", summ_low, grad_attended, preferred_element_type=f32
    )
    centre_term = jnp.sum(local_probs * local_dp, -1) + jnp.sum(summ_probs * summ_dp, -1)
    local_ds = (local_probs * (local_dp - centre_term[..., None])).astype(bf16)
    summ_ds = (summ_probs * (summ_dp - centre_term[..., None])).astype(bf16)
    query_grad = jnp.einsum("irhqk,irkhd->irqhd", local_ds, key_heads, preferred_element_type=f32)
    query_grad = (
        score_scale
        * (
            query_grad
            + jnp.einsum("irhqs,ishd->irqhd", summ_ds, summ_key_heads, preferred_element_type=f32)
        )
    ).astype(bf16)
    key_grad_local = score_scale * jnp.einsum(
        "irhqk,irqhd->irkhd", local_ds, queries, preferred_element_type=f32
    )
    summ_key_grad = score_scale * jnp.einsum(
        "irhqs,irqhd->ishd", summ_ds, queries, preferred_element_type=f32
    )
    own_key_grad, own_value_grad = (
        lax.psum_scatter(
            summ_key_grad.reshape(image_count, ROWS_IMG, D).astype(jnp.bfloat16),
            "wide",
            scatter_dimension=1,
            tiled=True,
        ).astype(jnp.float32),
        lax.psum_scatter(
            summ_value_grad.reshape(image_count, ROWS_IMG, D).astype(jnp.bfloat16),
            "wide",
            scatter_dimension=1,
            tiled=True,
        ).astype(jnp.float32),
    )
    key_grad = (
        key_grad_local.reshape(image_count, rows_here, ROW, D) + own_key_grad[:, :, None, :] / ROW
    ).astype(bf16)
    value_grad = (
        value_grad_local.reshape(image_count, rows_here, ROW, D)
        + own_value_grad[:, :, None, :] / ROW
    ).astype(bf16)
    grad_proj = jnp.stack(
        [query_grad.reshape(-1, D), key_grad.reshape(-1, D), value_grad.reshape(-1, D)], axis=1
    )
    grad_qkv = jnp.einsum("nd,nje->jde", low_one, grad_proj, preferred_element_type=f32)
    grad_low_one = jnp.einsum(
        "nje,jde->nd", grad_proj, back_blocks[0:3], preferred_element_type=f32
    )
    grad_inputs, gain_one_grad, shift_one_grad = norm_back_one(grad_low_one)
    grad_tokens = (grad_hidden + grad_inputs).reshape(tokens.shape)
    grad_blocks = jnp.concatenate(
        [grad_qkv, grad_wout[None], grad_up, grad_down.reshape(ff_blocks, D, D)], axis=0
    )
    row_sums = lax.psum_scatter(
        grad_blocks.astype(jnp.bfloat16), "narrow", scatter_dimension=1, tiled=True
    ).astype(jnp.float32)
    slotted = jnp.zeros((wide_size,) + row_sums.shape[1:], f32).at[owner_list].set(row_sums)
    own_grad = lax.psum_scatter(
        slotted.astype(jnp.bfloat16), "wide", scatter_dimension=0, tiled=True
    ).astype(jnp.float32)
    small_grad = lax.psum(
        jnp.concatenate(
            [
                gain_one_grad,
                shift_one_grad,
                gain_two_grad,
                shift_two_grad,
                bias_up_grad,
                bias_down_grad,
            ]
        ),
        ("wide", "narrow"),
    )
    owns_slot = jnp.any(owner_list == lax.axis_index("wide"))
    slot_weight, slot_first, slot_second = adamw_update(
        master, own_grad, moment_one, moment_two, 0.1, RATE
    )
    new_master = jnp.where(owns_slot, slot_weight, master)
    new_one = jnp.where(owns_slot, slot_first, moment_one)
    new_two = jnp.where(owns_slot, slot_second, moment_two)
    small_new, small_one_new, small_two_new = adamw_update(
        small_params, small_grad, small_one, small_two, 0.0, GAIN_RATE
    )
    return (
        block_out,
        grad_tokens,
        new_master,
        new_one,
        new_two,
        small_new,
        small_one_new,
        small_two_new,
    )


def solution(mesh):
    in_specs = (
        P("narrow", "wide", None),
        P("narrow", "wide", None),
        P(),
        P("wide", "narrow", None),
        P("wide", "narrow", None),
        P("wide", "narrow", None),
        P(),
        P(),
        P(),
    )
    out_specs = (
        P("narrow", "wide", None),
        P("narrow", "wide", None),
        P("wide", "narrow", None),
        P("wide", "narrow", None),
        P("wide", "narrow", None),
        P(),
        P(),
        P(),
    )
    return jax.shard_map(
        per_device, mesh=mesh, in_specs=in_specs, out_specs=out_specs, check_vma=False
    )
```

profile of v0, /device:TPU:0, one launch (start us, length us, event | category | flops | bytes accessed | tf_op | source)
XLA Modules:
  0.0 1282.7 jit_solution(14555857946981295142)
XLA Ops:
  29.7 62.0 %all-gather.3.cloned.1.call-done = bf16[1,8192,512]{2,1,0:T(8,128)(2,1)} async-done(((bf16[1,256,512]{2,1,0:T(8,128)(2,1)}), bf16[1,8192,512]{2,1,0:T(8,128)(2,1)}) %all-gather.3.cloned.1.call-update) | async-done | bytes 8388624 | tf_op jit(solution)/shard_map/all_gather | solution.py:37
  105.3 16.1 %convolution_convert_fusion = bf16[6144,3,512]{2,0,1:T(8,128)(2,1)} fusion(bf16[6144,512]{1,0:T(8,128)(2,1)} %fusion.38, bf16[12,512,512]{2,1,0:T(8,128)(2,1)} %copy-done.7), kind=kOutput, calls=%fused_computation.53 | convolution fusion | flops 9673113600 | bytes 26738688 | tf_op jit(solution)/shard_map/nd,jde->nje/dot_general | solution.py:70
  121.4 13.9 %fusion.113 = (bf16[6144,1,512]{2,0,1:T(8,128)(2,1)}, bf16[6144,1,512]{2,0,1:T(8,128)(2,1)}, bf16[6144,1,512]{2,0,1:T(8,128)(2,1)}) fusion(bf16[6144,3,512]{2,0,1:T(8,128)(2,1)} %convolution_convert_fusion), kind=kLoop, calls=%fused_computation.192 | loop fusion | bytes 37748736 | tf_op jit(solution)/shard_map/slice | solution.py:73
  144.1 16.2 %reshape.337 = bf16[8,4,192,8,64]{4,3,2,1,0:T(8,128)(2,1)} reshape(bf16[6144,1,512]{2,0,1:T(8,128)(2,1)} %get-tuple-element.23) | data formatting | bytes 12582912 | tf_op jit(solution)/shard_map/reshape;squeeze | solution.py:75
  164.2 16.5 %reshape.338 = bf16[8,4,192,8,64]{4,3,2,1,0:T(8,128)(2,1)} reshape(bf16[6144,1,512]{2,0,1:T(8,128)(2,1)} %get-tuple-element.22) | data formatting | bytes 12582912 | tf_op jit(solution)/shard_map/reshape;squeeze | solution.py:74
  184.7 41.5 %all_gather.11 = bf16[8,64,512]{2,0,1:T(8,128)(2,1)S(1)} all-gather(bf16[8,4,512]{2,0,1:T(8,128)(2,1)S(1)} %fusion.94), channel_id=1, replica_groups=mesh['wide'=16,'narrow'=2] {'wide'}, dimensions={1}, use_global_device_ids=true | all-gather | bytes 557056 | tf_op jit(solution)/shard_map/all_gather | solution.py:83
  226.3 38.3 %all_gather.12 = bf16[8,64,512]{2,0,1:T(8,128)(2,1)S(1)} all-gather(bf16[8,4,512]{2,0,1:T(8,128)(2,1)S(1)} %fusion.93), channel_id=1, replica_groups=mesh['wide'=16,'narrow'=2] {'wide'}, dimensions={1}, use_global_device_ids=true | all-gather | bytes 557056 | tf_op jit(solution)/shard_map/all_gather | solution.py:84
  266.6 17.5 %reshape_squeeze.12 = bf16[8,4,192,8,64]{2,1,0,4,3:T(4,128)(2,1)} reshape(bf16[6144,1,512]{0,2,1:T(8,128)(2,1)} %copy.196) | data formatting | bytes 12582912 | tf_op jit(solution)/shard_map/reshape;squeeze | solution.py:73
  284.0 15.4 %copy.199 = bf16[8,4,192,8,64]{2,4,3,1,0:T(8,128)(2,1)} copy(bf16[8,4,192,8,64]{4,3,2,1,0:T(8,128)(2,1)} %reshape.338) | data formatting | bytes 12582912 | tf_op jit(solution)/shard_map/reshape;squeeze | solution.py:74
  299.4 15.4 %copy.208 = bf16[8,4,192,8,64]{2,4,3,1,0:T(8,128)(2,1)} copy(bf16[8,4,192,8,64]{4,3,2,1,0:T(8,128)(2,1)} %reshape.337) | data formatting | bytes 12582912 | tf_op jit(solution)/shard_map/reshape;squeeze | solution.py:75
  314.7 13.7 %fusion.115 = (f32[8,4,8,192]{3,1,2,0:T(4,128)S(1)}, f32[8,4,8,192,64]{3,4,1,2,0:T(8,128)}) fusion(bf16[8,4,192,8,64]{2,1,0,4,3:T(4,128)(2,1)} %reshape_squeeze.12, bf16[8,64,8,64,1]{1,3,2,4,0:T(8,128)(2,1)S(1)} %copy.257, pred[4,64]{1,0:T(4,128)(4,1)S(1)} %iota_compare_fusion.1), kind=kOutput, calls=%fused_computation.194 | convolution fusion | flops 415186944 | bytes 19595520 | tf_op jit(solution)/shard_map/irqhd,ishd->irhqs/dot_general | solution.py:97
  328.6 25.5 %fusion.18 = (f32[8,4,8,192]{3,2,1,0:T(8,128)S(1)}, f32[8,4,8,192,192]{3,4,2,1,0:T(8,128)}) fusion(pred[192,192]{0,1:T(8,128)(4,1)S(1)} %iota_compare_fusion, bf16[8,4,192,8,64]{2,4,3,1,0:T(8,128)(2,1)} %copy.199, bf16[8,4,192,8,64]{2,1,0,4,3:T(4,128)(2,1)} %reshape_squeeze.12), kind=kOutput, calls=%fused_computation.33 | convolution fusion | flops 1236221952 | bytes 50565120 | tf_op jit(solution)/shard_map/irqhd,irkhd->irhqk/dot_general | solution.py:93
  354.2 10.8 exponential_reduce_fusion.1
  365.0 23.4 %exponential_reduce_fusion = f32[8,4,8,192]{3,2,1,0:T(8,128)S(1)} fusion(f32[8,4,8,192,192]{3,4,2,1,0:T(8,128)} %get-tuple-element.35, f32[8,4,8,192]{3,2,1,0:T(8,128)S(1)} %is-finite_select_fusion.1, pred[192,192]{0,1:T(8,128)(4,1)S(1)} %iota_compare_fusion), kind=kLoop, calls=%fused_computation.31 | loop fusion | flops 37699584 | bytes 38178816 | tf_op jit(solution)/shard_map/reduce_sum | solution.py:101
  388.8 26.6 %fusion.89 = f32[8,4,8,64,192]{4,3,2,1,0:T(8,128)} fusion(bf16[8,4,192,8,64]{2,4,3,1,0:T(8,128)(2,1)} %copy.208, f32[8,4,8,192,192]{3,4,2,1,0:T(8,128)} %get-tuple-element.35, f32[8,4,8,192]{3,2,1,0:T(8,128)S(1)} %add_select_fusion, pred[192,192]{0,1:T(8,128)(4,1)S(1)} %iota_compare_fusion), kind=kOutput, calls=%fused_computation.140 | convolution fusion | flops 1245708288 | bytes 56856576 | tf_op jit(solution)/shard_map/irhqk,irkhd->irqhd/dot_general | solution.py:106
  415.4 15.6 %fusion.27 = bf16[8,4,192,8,64]{2,4,3,1,0:T(8,128)(2,1)} fusion(f32[8,4,8,64,192]{4,3,2,1,0:T(8,128)} %fusion.89, bf16[8,64,8,64,1]{1,3,2,4,0:T(8,128)(2,1)S(1)} %bitcast.234, f32[8,4,8,192,64]{3,4,1,2,0:T(8,128)} %get-tuple-element.37, f32[8,4,8,192]{3,1,2,0:T(4,128)S(1)} %copy.212), kind=kOutput, calls=%fused_computation.48 | convolution fusion | flops 415236096 | bytes 32178176 | tf_op jit(solution)/shard_map/irhqs,ishd->irqhd/dot_general | solution.py:107
  431.0 12.4 copy.214
  443.4 15.7 %reshape.288 = bf16[6144,512]{0,1:T(8,128)(2,1)} reshape(bf16[8,4,192,8,64]{2,1,0,4,3:T(4,128)(2,1)} %copy.214) | data formatting | bytes 12582912 | tf_op jit(solution)/shard_map/reshape | solution.py:110
  475.0 25.8 %fusion.68 = f32[6144,4,512]{0,2,1:T(8,128)} fusion(bf16[12,512,512]{2,1,0:T(8,128)(2,1)} %copy-done.7, f32[6144,512]{1,0:T(8,128)} %copy-done.1, f32[512]{0:T(512)S(1)} %copy-done.43, f32[512]{0:T(512)S(1)} %copy-done.38, f32[6144]{0:T(1024)S(1)} %fusion.95, f32[6144]{0:T(1024)S(1)} %broadcast_multiply_fusion), kind=kOutput, calls=%fused_computation.121 | convolution fusion | flops 12900630528 | bytes 65064960 | tf_op jit(solution)/shard_map/nd,jde->nje/dot_general | solution.py:115
  500.8 33.6 %multiply_convert_fusion = bf16[6144,2048]{0,1:T(8,128)(2,1)} fusion(f32[6144,4,512]{0,2,1:T(8,128)} %fusion.68, f32[2048]{0:T(1024)S(1)} %copy-done.32), kind=kLoop, calls=%fused_computation.27 | loop fusion | flops 125829120 | bytes 75505664 | tf_op jit(solution)/shard_map/convert_element_type | solution.py:121
  534.5 48.0 %convert_reduce_fusion = (f32[2048]{0:T(1024)}, bf16[6144,2048]{0,1:T(8,128)(2,1)}) fusion(f32[2048]{0:T(1024)S(1)} %copy-done.32, f32[6144,4,512]{0,2,1:T(8,128)} %fusion.68, bf16[2048,512]{1,0:T(8,128)(2,1)S(1)} %bitcast.233, bf16[6144,512]{1,0:T(8,128)(2,1)} %bitcast.225), kind=kOutput, calls=%fused_computation.26 | convolution fusion | flops 13174306816 | bytes 83902464 | tf_op jit(solution)/shard_map/nd,fd->nf/dot_general | solution.py:131
  582.4 20.5 %convert_bitcast_fusion = bf16[4,512,512]{1,2,0:T(8,128)(2,1)} fusion(bf16[6144,4,512]{0,2,1:T(8,128)(2,1)} %bitcast.242, f32[6144,512]{1,0:T(8,128)} %copy-done.1, f32[512]{0:T(512)S(1)} %copy-done.43, f32[512]{0:T(512)S(1)} %copy-done.38, f32[6144]{0:T(1024)S(1)} %fusion.95, f32[6144]{0:T(1024)S(1)} %broadcast_multiply_fusion), kind=kOutput, calls=%fused_computation.117 | convolution fusion | flops 12901679104 | bytes 39899136 | tf_op jit(solution)/shard_map/nd,nje->jde/dot_general | solution.py:140
  602.9 26.0 %fusion.30 = (f32[512]{0:T(512)}, f32[6144]{0:T(1024)S(1)}, f32[512]{0:T(512)}, f32[6144,512,1]{1,0,2:T(8,128)}) fusion(f32[6144,512]{1,0:T(8,128)} %copy-done.1, f32[6144]{0:T(1024)S(1)} %fusion.95, f32[6144]{0:T(1024)S(1)} %broadcast_multiply_fusion, f32[512]{0:T(512)S(1)} %copy-done.38, bf16[6144,4,512]{0,2,1:T(8,128)(2,1)} %bitcast.243, ...), kind=kOutput, calls=%fused_computation.64 | convolution fusion | flops 12910061568 | bytes 52508672 | tf_op jit(solution)/shard_map/nje,jde->nd/dot_general | solution.py:143
  666.3 17.1 %reshape.294 = bf16[8,4,192,8,64]{2,1,0,4,3:T(4,128)(2,1)} reshape(bf16[6144,512]{0,1:T(8,128)(2,1)} %copy.218) | data formatting | bytes 12582912 | tf_op jit(solution)/shard_map/reshape | solution.py:153
  683.3 10.9 bitcast_convert_fusion
  694.3 29.7 %convolution_bitcast_fusion = f32[8,4,192,8,64]{2,4,3,1,0:T(8,128)} fusion(bf16[8,4,192,8,64]{2,1,0,4,3:T(4,128)(2,1)} %reshape.294, f32[8,4,8,192,192]{3,4,2,1,0:T(8,128)} %get-tuple-element.35, f32[8,4,8,192]{3,2,1,0:T(8,128)S(1)} %copy-done.10, pred[192,192]{0,1:T(8,128)(4,1)S(1)} %copy-done.4), kind=kOutput, calls=%fused_computation.90 | convolution fusion | flops 1245708288 | bytes 56856576 | tf_op jit(solution)/shard_map/irhqk,irqhd->irkhd/dot_general | solution.py:161
  724.0 45.9 %multiply_reduce_fusion = (f32[8,4,8,192]{3,2,1,0:T(8,128)S(1)}, f32[8,4,8,192,192]{3,4,2,1,0:T(8,128)}) fusion(f32[8,4,8,192,192]{3,4,2,1,0:T(8,128)} %get-tuple-element.35, f32[8,4,8,192]{3,2,1,0:T(8,128)S(1)} %copy-done.10, pred[192,192]{0,1:T(8,128)(4,1)S(1)} %copy-done.4, bf16[8,4,192,8,64]{2,4,3,1,0:T(8,128)(2,1)} %copy.208, ...), kind=kOutput, calls=%fused_computation.29 | convolution fusion | flops 1255096320 | bytes 88510464 | tf_op jit(solution)/shard_map/irqhd,irkhd->irhqk/dot_general | solution.py:155
  769.9 15.1 %fusion.24 = (f32[8,4,8,192]{3,1,2,0:T(4,128)S(1)}, f32[8,8,64,4,192]{4,2,3,1,0:T(8,128)}) fusion(f32[8,4,8,192,64]{3,4,1,2,0:T(8,128)} %get-tuple-element.37, f32[8,4,8,192]{3,1,2,0:T(4,128)S(1)} %copy-done.14, bf16[8,64,8,64,1]{1,3,4,2,0:T(8,128)(2,1)S(1)} %bitcast.235, bf16[8,4,192,8,64]{2,1,0,4,3:T(4,128)(2,1)} %reshape.294), kind=kOutput, calls=%fused_computation.44 | convolution fusion | flops 412041216 | bytes 32374784 | tf_op jit(solution)/shard_map/irqhd,ishd->irhqs/dot_general | solution.py:158
  785.3 41.1 %multiply_convert_fusion.1 = bf16[8,4,8,192,192]{3,4,2,1,0:T(8,128)(2,1)} fusion(f32[8,4,8,192,192]{3,4,2,1,0:T(8,128)} %get-tuple-element.42, f32[8,4,8,192,192]{3,4,2,1,0:T(8,128)} %get-tuple-element.35, f32[8,4,8,192]{3,2,1,0:T(8,128)S(1)} %copy_add_fusion, f32[8,4,8,192]{3,2,1,0:T(8,128)S(1)} %copy-done.10, pred[192,192]{0,1:T(8,128)(4,1)S(1)} %copy-done.4), kind=kLoop, calls=%fused_computation.28 | loop fusion | flops 56623104 | bytes 94801920 | tf_op jit(solution)/shard_map/convert_element_type | solution.py:168
  826.3 20.9 %multiply_bitcast_fusion = f32[8,4,192,8,64]{2,4,3,1,0:T(8,128)} fusion(bf16[8,4,8,192,192]{3,4,2,1,0:T(8,128)(2,1)} %multiply_convert_fusion.1, bf16[8,4,192,8,64]{2,1,0,4,3:T(4,128)(2,1)} %reshape_squeeze.12), kind=kOutput, calls=%fused_computation.50 | convolution fusion | flops 1211105280 | bytes 37748736 | tf_op jit(solution)/shard_map/irhqk,irqhd->irkhd/dot_general | solution.py:178
  847.3 19.5 %fusion.117 = f32[8,4,8,64,192]{4,3,2,1,0:T(8,128)} fusion(bf16[8,4,192,8,64]{2,4,3,1,0:T(8,128)(2,1)} %copy.199, bf16[8,4,8,192,192]{3,4,2,1,0:T(8,128)(2,1)} %multiply_convert_fusion.1), kind=kOutput, calls=%fused_computation.196 | convolution fusion | flops 1207959552 | bytes 37748736 | tf_op jit(solution)/shard_map/irhqk,irkhd->irqhd/dot_general | solution.py:170
  868.5 19.5 %convolution_convert_fusion.2 = bf16[4,512,512]{1,2,0:T(8,128)(2,1)} fusion(bf16[4,512,6144]{2,1,0:T(8,128)(2,1)} %bitcast.231, bf16[6144,512,1]{1,0,2:T(8,128)(2,1)} %bitcast.226), kind=kOutput, calls=%fused_computation.118 | convolution fusion | flops 12885950464 | bytes 33554432 | tf_op jit(solution)/shard_map/nf,nd->fd/dot_general | solution.py:139
  887.9 15.1 %fusion.26 = bf16[8,4,8,192,64]{3,4,1,2,0:T(8,128)(2,1)} fusion(f32[8,8,64,4,192]{4,2,3,1,0:T(8,128)} %get-tuple-element.44, f32[8,4,8,192,64]{3,4,1,2,0:T(8,128)} %get-tuple-element.37, f32[8,4,8,192]{3,1,2,0:T(4,128)S(1)} %copy.226, f32[8,4,8,192]{3,1,2,0:T(4,128)S(1)} %copy-done.14), kind=kLoop, calls=%fused_computation.46 | loop fusion | flops 12582912 | bytes 31850496 | tf_op jit(solution)/shard_map/convert_element_type | solution.py:169
  903.0 12.1 fusion.23
  915.2 15.3 %fusion.65 = bf16[8,8,64,64]{3,2,1,0:T(8,128)(2,1)S(1)} fusion(bf16[8,4,8,192,64]{3,4,1,2,0:T(8,128)(2,1)} %fusion.26, bf16[8,4,192,8,64]{2,1,0,4,3:T(4,128)(2,1)} %reshape_squeeze.12), kind=kOutput, calls=%fused_computation.116 | convolution fusion | flops 403177472 | bytes 13107200 | tf_op jit(solution)/shard_map/irhqs,irqhd->ishd/dot_general | solution.py:181
  940.5 22.0 %copy.272 = f32[8,4,192,8,64]{4,3,2,1,0:T(8,128)} copy(f32[8,4,192,8,64]{2,4,3,1,0:T(8,128)} %convolution_bitcast_fusion) | data formatting | bytes 25165824 | tf_op jit(solution)/shard_map/reshape | solution.py:202
  962.5 20.9 %reshape.336 = f32[6144,1,512]{2,0,1:T(8,128)} reshape(f32[8,4,192,8,64]{4,3,2,1,0:T(8,128)} %copy.272) | data formatting | bytes 25165824 | tf_op jit(solution)/shard_map/reshape | solution.py:202
  983.4 15.2 %copy.270 = bf16[8,4,192,8,64]{4,3,2,1,0:T(8,128)(2,1)} copy(bf16[8,4,192,8,64]{2,4,3,1,0:T(8,128)(2,1)} %fusion.23) | data formatting | bytes 12582912 | tf_op jit(solution)/shard_map/stack;reshape | solution.py:205
  998.6 17.1 %reshape.334 = bf16[6144,1,512]{2,0,1:T(8,128)(2,1)} reshape(bf16[8,4,192,8,64]{4,3,2,1,0:T(8,128)(2,1)} %copy.270) | data formatting | bytes 12582912 | tf_op jit(solution)/shard_map/stack;reshape | solution.py:205
  1015.7 21.5 %copy.271 = f32[8,4,192,8,64]{4,3,2,1,0:T(8,128)} copy(f32[8,4,192,8,64]{2,4,3,1,0:T(8,128)} %multiply_bitcast_fusion) | data formatting | bytes 25165824 | tf_op jit(solution)/shard_map/reshape | solution.py:199
  1037.2 20.9 %reshape.335 = f32[6144,1,512]{2,0,1:T(8,128)} reshape(f32[8,4,192,8,64]{4,3,2,1,0:T(8,128)} %copy.271) | data formatting | bytes 25165824 | tf_op jit(solution)/shard_map/reshape | solution.py:199
  1071.9 22.3 %add_convert_fusion = (bf16[6144,1,512]{2,0,1:T(8,128)(2,1)}, bf16[6144,1,512]{2,0,1:T(8,128)(2,1)}) fusion(f32[6144,1,512]{2,0,1:T(8,128)} %reshape.336, f32[6144,1,512]{2,0,1:T(8,128)} %bitcast.229, f32[6144,1,512]{2,0,1:T(8,128)} %reshape.335, f32[6144,1,512]{2,0,1:T(8,128)} %bitcast.230), kind=kLoop, calls=%fused_computation.83 | loop fusion | flops 12582912 | bytes 62914560 | tf_op jit(solution)/shard_map/convert_element_type | solution.py:204
  1094.2 14.2 %fusion.77 = bf16[3,512,512]{1,2,0:T(8,128)(2,1)S(1)} fusion(bf16[6144,512]{1,0:T(8,128)(2,1)S(1)} %bitcast.237, bf16[6144,1,512]{2,0,1:T(8,128)(2,1)} %get-tuple-element.48, bf16[6144,1,512]{2,0,1:T(8,128)(2,1)} %get-tuple-element.49, bf16[6144,1,512]{2,0,1:T(8,128)(2,1)} %reshape.334), kind=kOutput, calls=%fused_computation.124 | convolution fusion | flops 9683337216 | bytes 26738688 | tf_op jit(solution)/shard_map/nd,nje->jde/dot_general | solution.py:208
  1118.1 32.6 %fusion.32 = bf16[6144,512]{1,0:T(8,128)(2,1)} fusion(f32[6144,512]{1,0:T(8,128)} %copy-done.1, f32[6144,4,512]{0,2,1:T(8,128)} %fusion.68, f32[4,512]{1,0:T(4,128)S(1)} %slice.64, f32[512]{0:T(512)S(1)} %copy-done.42, bf16[12,512,512]{2,1,0:T(8,128)(2,1)} %copy-done.7), kind=kOutput, calls=%fused_computation.67 | convolution fusion | flops 13020168192 | bytes 71313408 | tf_op jit(solution)/shard_map/dot_general | solution.py:124
  1160.5 11.6 scatter_fusion
  1178.3 18.0 %bitcast_reduce_fusion = (f32[512]{0:T(512)S(1)}, f32[6144]{0:T(1024)S(1)}, f32[6144,512,1]{1,0,2:T(8,128)S(1)}) fusion(f32[512]{0:T(512)S(1)} %copy-done.35, f32[6144]{0:T(1024)S(1)} %copy-done.21, bf16[8,768,512]{2,1,0:T(8,128)(2,1)} %param.11, bf16[12,512,512]{2,1,0:T(8,128)(2,1)} %copy-done.7, bf16[6144,1,512]{2,0,1:T(8,128)(2,1)} %get-tuple-element.48, ...), kind=kOutput, calls=%fused_computation.57 | convolution fusion | flops 9701419008 | bytes 39374848 | tf_op jit(solution)/shard_map/nje,jde->nd/dot_general | solution.py:209
  1203.4 40.9 %psum.7 = f32[4608]{0:T(1024)S(1)} all-reduce(f32[4608]{0:T(1024)S(1)} %constant_dynamic-update-slice_fusion), channel_id=1, replica_groups=mesh['wide'=16,'narrow'=2] {'wide','narrow'}, use_global_device_ids=true, to_apply=%region_28.30 | all-reduce | flops 4608 | bytes 36864 | tf_op jit(solution)/shard_map/psum | solution.py:224
  1244.9 19.0 %add_add_fusion.2 = f32[6144,512]{1,0:T(8,128)} fusion(f32[6144,512]{1,0:T(8,128)} %copy-done, f32[6144]{0:T(1024)S(1)} %negate_multiply_fusion, f32[6144]{0:T(1024)S(1)} %copy-done.25, bf16[8,768,512]{2,1,0:T(8,128)(2,1)} %param.12, f32[6144]{0:T(1024)S(1)} %multiply_multiply_fusion.5, f32[6144]{0:T(1024)S(1)} %copy-done.21, ...), kind=kLoop, calls=%fused_computation.82 | loop fusion | flops 37748736 | bytes 50456576 | tf_op jit(solution)/shard_map/add | solution.py:213
  (198 shorter events, 179.4 us)
Async XLA Ops:
  7.2 13.8 %copy-start.30 = (f32[4608]{0:T(1024)S(1)}, f32[4608]{0:T(1024)}, u32[]{:S(2)}) copy-start(f32[4608]{0:T(1024)} %param.17) | copy-start | bytes 55300
  7.2 11.9 copy-start.46
  7.2 84.5 %all-gather.3.cloned.1.call-start = ((), (), s32[]{:S(2)}) async-start(), calls=%async_computation.8 | async-start | bytes 8650752 | tf_op jit(solution)/shard_map/all_gather | solution.py:37
  9.0 1049.0 %reduce-scatter.7.cloned.1.call-start = ((), (), s32[]{:S(2)}) async-start(), calls=%async_computation.5 | async-start | bytes 557056 | tf_op jit(solution)/shard_map/reduce_scatter | solution.py:191
  14.1 85.2 %copy-start.20 = (f32[6144]{0:T(1024)}, f32[6144]{0:T(1024)S(1)}, u32[]{:S(2)}) copy-start(f32[6144]{0:T(1024)S(1)} %div.81) | copy-start | bytes 73732
  19.0 80.3 %copy-start.22 = (f32[6144]{0:T(1024)}, f32[6144]{0:T(1024)S(1)}, u32[]{:S(2)}) copy-start(f32[6144]{0:T(1024)S(1)} %rsqrt.20) | copy-start | bytes 73732
  20.2 368.6 %copy-start.3 = (pred[192,192]{0,1:T(8,128)(4,1)}, pred[192,192]{0,1:T(8,128)(4,1)S(1)}, u32[]{:S(2)}) copy-start(pred[192,192]{0,1:T(8,128)(4,1)S(1)} %iota_compare_fusion) | copy-start | bytes 110596
  265.2 150.2 %copy-start.11 = (bf16[8,64,512]{1,2,0:T(8,128)(2,1)}, bf16[8,64,512]{1,2,0:T(8,128)(2,1)S(1)}, u32[]{:S(2)}) copy-start(bf16[8,64,512]{1,2,0:T(8,128)(2,1)S(1)} %copy.211) | copy-start | bytes 1572868
  266.5 48.2 %copy-start.5 = (bf16[8,64,8,64,1]{1,3,2,4,0:T(8,128)(2,1)}, bf16[8,64,8,64,1]{1,3,2,4,0:T(8,128)(2,1)S(1)}, u32[]{:S(2)}) copy-start(bf16[8,64,8,64,1]{1,3,2,4,0:T(8,128)(2,1)S(1)} %copy.257) | copy-start | bytes 1572868
  388.7 26.7 %copy-start.9 = (f32[8,4,8,192]{3,2,1,0:T(8,128)}, f32[8,4,8,192]{3,2,1,0:T(8,128)S(1)}, u32[]{:S(2)}) copy-start(f32[8,4,8,192]{3,2,1,0:T(8,128)S(1)} %add_select_fusion) | copy-start | bytes 589828
  388.8 26.6 %copy-start.13 = (f32[8,4,8,192]{3,1,2,0:T(4,128)}, f32[8,4,8,192]{3,1,2,0:T(4,128)S(1)}, u32[]{:S(2)}) copy-start(f32[8,4,8,192]{3,1,2,0:T(4,128)S(1)} %copy.212) | copy-start | bytes 589828
  467.5 7.5 copy-start.38
  467.5 7.5 copy-start.43
  475.0 25.8 %copy-start.32 = (f32[2048]{0:T(1024)S(1)}, f32[2048]{0:T(1024)}, u32[]{:S(2)}) copy-start(f32[2048]{0:T(1024)} %slice.63) | copy-start | bytes 24580
  500.8 33.6 %slice-start.4 = ((bf16[12,512,512]{2,1,0:T(8,128)(2,1)}), bf16[4,512,512]{2,1,0:T(8,128)(2,1)S(1)}, s32[]{:S(2)}) async-start(bf16[12,512,512]{2,1,0:T(8,128)(2,1)} %copy-done.7), calls=%async_computation.13 | async-start | bytes 4194304 | tf_op jit(solution)/shard_map/slice | solution.py:122
  582.4 61.8 %slice-start.2 = ((s8[6291456]{0:T(1024)(128)(4,1)}), s8[4194304]{0:T(1024)(128)(4,1)S(1)}, s32[]{:S(2)}) async-start(s8[6291456]{0:T(1024)(128)(4,1)} %bitcast.227), calls=%async_computation.11 | async-start | bytes 8388608
  602.9 26.0 %copy-start.27 = (f32[6144]{0:T(1024)S(1)}, f32[6144]{0:T(1024)}, u32[]{:S(2)}) copy-start(f32[6144]{0:T(1024)} %copy-done.26) | copy-start | bytes 73732
  602.9 41.3 %slice-start.3 = ((s8[6291456]{0:T(1024)(128)(4,1)}), s8[2097152]{0:T(1024)(128)(4,1)S(1)}, s32[]{:S(2)}) async-start(s8[6291456]{0:T(1024)(128)(4,1)} %bitcast.227), calls=%async_computation.12 | async-start | bytes 4194304
  639.7 8.3 copy-start.24
  657.5 25.8 %copy-start.14 = (f32[8,4,8,192]{3,1,2,0:T(4,128)S(1)}, f32[8,4,8,192]{3,1,2,0:T(4,128)}, u32[]{:S(2)}) copy-start(f32[8,4,8,192]{3,1,2,0:T(4,128)} %copy-done.13) | copy-start | bytes 589828
  683.3 11.0 copy-start.4
  683.3 11.0 copy-start.10
  724.0 45.9 %copy-start.12 = (bf16[8,64,512]{1,2,0:T(8,128)(2,1)S(1)}, bf16[8,64,512]{1,2,0:T(8,128)(2,1)}, u32[]{:S(2)}) copy-start(bf16[8,64,512]{1,2,0:T(8,128)(2,1)} %copy-done.11) | copy-start | bytes 1572868
  868.4 190.5 %reduce-scatter.5.cloned.1.call-start = ((), (), s32[]{:S(2)}) async-start(), calls=%async_computation.4 | async-start | bytes 557056 | tf_op jit(solution)/shard_map/reduce_scatter | solution.py:185
  887.9 15.1 %copy-start.6 = (bf16[8,64,8,64,1]{1,3,2,4,0:T(8,128)(2,1)S(1)}, bf16[8,64,8,64,1]{1,3,2,4,0:T(8,128)(2,1)}, u32[]{:S(2)}) copy-start(bf16[8,64,8,64,1]{1,3,2,4,0:T(8,128)(2,1)} %copy-done.5) | copy-start | bytes 1572868
  932.2 218.5 %reduce-scatter.9.cloned.1.call-start = ((), (), s32[]{:S(2)}) async-start(), calls=%async_computation.6 | async-start | bytes 9437184 | tf_op jit(solution)/shard_map/reduce_scatter | solution.py:217
  1065.8 28.4 %slice-start.5 = ((s8[6291456]{0:T(1024)(128)(4,1)}), s8[4194304]{0:T(1024)(128)(4,1)S(1)}, s32[]{:S(2)}) async-start(s8[6291456]{0:T(1024)(128)(4,1)} %bitcast.236), calls=%async_computation.14 | async-start | bytes 8388608
  1071.9 22.3 %slice-start.6 = ((s8[6291456]{0:T(1024)(128)(4,1)}), s8[2097152]{0:T(1024)(128)(4,1)S(1)}, s32[]{:S(2)}) async-start(s8[6291456]{0:T(1024)(128)(4,1)} %bitcast.236), calls=%async_computation.15 | async-start | bytes 4194304
  1094.2 14.2 %copy-start.16 = (bf16[4,512,512]{1,2,0:T(8,128)(2,1)S(1)}, bf16[4,512,512]{1,2,0:T(8,128)(2,1)}, u32[]{:S(2)}) copy-start(bf16[4,512,512]{1,2,0:T(8,128)(2,1)} %convert_bitcast_fusion) | copy-start | bytes 6291460
  1094.2 14.2 %copy-start.17 = (bf16[4,512,512]{1,2,0:T(8,128)(2,1)S(1)}, bf16[4,512,512]{1,2,0:T(8,128)(2,1)}, u32[]{:S(2)}) copy-start(bf16[4,512,512]{1,2,0:T(8,128)(2,1)} %convolution_convert_fusion.2) | copy-start | bytes 6291460
  1108.5 9.6 copy-start.42
  1114.3 158.4 %reduce-scatter.11.cloned.1.call-start = ((), (), s32[]{:S(2)}) async-start(), calls=%async_computation.7 | async-start | bytes 4456448 | tf_op jit(solution)/shard_map/reduce_scatter | solution.py:221
  1150.7 9.9 copy-start.41
  1172.1 24.3 %slice-start = ((s8[6291456]{0:T(1024)(128)(4,1)}), s8[2097152]{0:T(1024)(128)(4,1)S(1)}, s32[]{:S(2)}) async-start(s8[6291456]{0:T(1024)(128)(4,1)} %bitcast.221), calls=%async_computation.9 | async-start | bytes 4194304
  1178.2 18.1 %copy-start.29 = (f32[6144]{0:T(1024)S(1)}, f32[6144]{0:T(1024)}, u32[]{:S(2)}) copy-start(f32[6144]{0:T(1024)} %copy-done.28) | copy-start | bytes 73732
  1178.3 18.1 %slice-start.1 = ((s8[6291456]{0:T(1024)(128)(4,1)}), s8[4194304]{0:T(1024)(128)(4,1)S(1)}, s32[]{:S(2)}) async-start(s8[6291456]{0:T(1024)(128)(4,1)} %bitcast.221), calls=%async_computation.10 | async-start | bytes 8388608
  1178.3 18.1 %copy-start.23 = (f32[6144]{0:T(1024)S(1)}, f32[6144]{0:T(1024)}, u32[]{:S(2)}) copy-start(f32[6144]{0:T(1024)} %copy-done.22) | copy-start | bytes 73732
  1196.2 7.0 copy-start.2
  1196.3 7.0 copy-start.45
  1196.3 7.0 copy-start.44
  1196.3 7.0 copy-start.39
  1196.3 47.9 %copy-start.31 = (f32[4608]{0:T(1024)S(1)}, f32[4608]{0:T(1024)}, u32[]{:S(2)}) copy-start(f32[4608]{0:T(1024)} %param.17) | copy-start | bytes 55300
  1196.3 47.9 %copy-start.36 = (f32[4608]{0:T(1024)S(1)}, f32[4608]{0:T(1024)}, u32[]{:S(2)}) copy-start(f32[4608]{0:T(1024)} %param.18) | copy-start | bytes 55300
  1196.3 47.9 %copy-start.37 = (f32[4608]{0:T(1024)S(1)}, f32[4608]{0:T(1024)}, u32[]{:S(2)}) copy-start(f32[4608]{0:T(1024)} %param.19) | copy-start | bytes 55300
  1196.3 48.6 %copy-start.25 = (f32[6144]{0:T(1024)S(1)}, f32[6144]{0:T(1024)}, u32[]{:S(2)}) copy-start(f32[6144]{0:T(1024)} %copy-done.24) | copy-start | bytes 73732
  1244.9 27.8 %copy-start.15 = (f32[1,256,512]{2,1,0:T(8,128)S(1)}, f32[1,256,512]{2,1,0:T(8,128)}, u32[]{:S(2)}) copy-start(f32[1,256,512]{2,1,0:T(8,128)} %param.14) | copy-start | bytes 1572868
  1244.9 27.8 %copy-start.18 = (f32[1,256,512]{2,1,0:T(8,128)S(1)}, f32[1,256,512]{2,1,0:T(8,128)}, u32[]{:S(2)}) copy-start(f32[1,256,512]{2,1,0:T(8,128)} %param.16) | copy-start | bytes 1572868
  1244.9 27.8 %copy-start.19 = (f32[1,256,512]{2,1,0:T(8,128)S(1)}, f32[1,256,512]{2,1,0:T(8,128)}, u32[]{:S(2)}) copy-start(f32[1,256,512]{2,1,0:T(8,128)} %param.15) | copy-start | bytes 1572868
  (11 other events, 37.4 us)
Sparse Core Ops, SparseCore 0:
  11.5 80.1 all-gather.2
  868.5 74.4 reduce-scatter.6
  945.9 72.8 reduce-scatter.4
  1114.4 12.2 reduce-scatter.8
  1178.3 94.3 reduce-scatter.10
where the time goes:
time: 1300 us; the launch traced here: 1280 us
  matrix products  496 us (38%)
  local copies, waits for them, and re-layouts  340 us (26%)
  other arithmetic  240 us (18%)
  blocking collectives  121 us (9%)
  waiting for transfers between devices  70.8 us (5%)
  between operations  14.9 us (1%)
    all_gather x1, waiting for transfers between devices, fetch_blocks(): lax.all_gather(shard_low.reshape(-1, D), ('wide', 'narrow'), axis=0, tile...  62 us
    dot_general x1, matrix products, per_device(): jnp.einsum('nd,fd->nf', cot_rows, back_blocks[4 + ff_blocks:].reshape(FF,...  48 us
    dot_general x1, matrix products, per_device(): jnp.einsum('irqhd,irkhd->irhqk', grad_attended, value_heads, preferred_el...  45.9 us
    reshape x2, local copies, waits for them, and re-layouts, per_device(): value_grad_local.reshape(image_count, rows_here, ROW, D)  42.9 us
    reshape x2, local copies, waits for them, and re-layouts, per_device(): key_grad_local.reshape(image_count, rows_here, ROW, D)  42.4 us
    all_gather x1, blocking collectives, per_device(): lax.all_gather(sum_keys, 'wide', axis=1, tiled=True)  41.5 us
    convert_element_type x1, other arithmetic, per_device(): local_ds = (local_probs * (local_dp - centre_term[..., None])).astype(bf16)  41.1 us
    psum x1, blocking collectives, per_device(): lax.psum(jnp.concatenate([gain_one_grad, shift_one_grad, gain_two_grad, s...  40.9 us
  transfers between devices with their start and end apart: 5, of which 2 were waited for; matrix products, arithmetic and copies ran while one was open for 23% of the time, Pallas kernels for 0%

commit v1 on v0

v1 whole, which is shorter than its diff:
```python
import functools
import math

import jax
import jax.numpy as jnp
from jax import lax
from jax.experimental import pallas as pl
from jax.experimental.pallas import tpu as pltpu
from jax.sharding import PartitionSpec as P

D = 512
HEADS = 8
HD = 64
PAIR = 2 * HD
PAIRS = HEADS // 2
FF = 2048
NF = FF // D
ROW = 192
ROWS_IMG = 64
KEYS = ROW + ROWS_IMG
STEP = 10
RATE = 0.03
GAIN_RATE = 0.4
EPS = 1e-05
LOG2E = math.log2(math.e)
F32 = jnp.float32
BF16 = jnp.bfloat16
MIB = 1024 * 1024


def dot(left, right):
    return jnp.dot(left, right, preferred_element_type=F32)


def dot_nt(left, right):
    return lax.dot_general(left, right, (((1,), (1,)), ((), ())), preferred_element_type=F32)


def normalize(values):
    centred = values - jnp.mean(values, -1, keepdims=True)
    scale = lax.rsqrt(jnp.mean(centred * centred, -1, keepdims=True) + EPS)
    return centred * scale, scale


def head_masks(dtype):
    lane = lax.broadcasted_iota(jnp.int32, (1, PAIR), 1)
    first = (lane < HD).astype(F32)
    return first.astype(dtype), (1.0 - first).astype(dtype)


def tile_spec(*tail, buffers=None):
    zeros = (0,) * len(tail)
    return pl.BlockSpec((1,) + tail, lambda step, *_: (step,) + zeros)


def whole_spec(shape):
    zeros = (0,) * len(shape)
    return pl.BlockSpec(shape, lambda step, *_: zeros, pipeline_mode=pl.Buffered(1))


def weight_spec(block):
    return pl.BlockSpec(
        (1, D, D), lambda step, owner, *_: (owner[block], 0, 0), pipeline_mode=pl.Buffered(1)
    )


def out_whole(shape):
    zeros = (0,) * len(shape)
    return pl.BlockSpec(shape, lambda step, *_: zeros)


def norm_kernel(x_ref, cot_ref, g_ref, s_ref, a_ref, xh_ref, mean_ref, csum_ref):
    normal, _ = normalize(x_ref[0].astype(F32))
    a_ref[0] = (normal * g_ref[...] + s_ref[...]).astype(BF16)
    xh_ref[0] = normal.astype(BF16)
    for row in range(mean_ref.shape[1]):
        part = normal[row * ROW : (row + 1) * ROW]
        mean_ref[0, row : row + 1, :] = jnp.mean(part, 0, keepdims=True)
    total = jnp.sum(cot_ref[0].astype(F32), 0, keepdims=True)

    @pl.when(pl.program_id(0) == 0)
    def _():
        csum_ref[...] = total

    @pl.when(pl.program_id(0) > 0)
    def _():
        csum_ref[...] += total


def norm_call(tokens, cotangent, gain, shift):
    images, count, _ = tokens.shape
    rows = count // ROW
    return pl.pallas_call(
        norm_kernel,
        grid=(images,),
        in_specs=[tile_spec(count, D), tile_spec(count, D), whole_spec((1, D)), whole_spec((1, D))],
        out_specs=[tile_spec(count, D), tile_spec(count, D), tile_spec(rows, D), out_whole((1, D))],
        out_shape=[
            jax.ShapeDtypeStruct((images, count, D), BF16),
            jax.ShapeDtypeStruct((images, count, D), BF16),
            jax.ShapeDtypeStruct((images, rows, D), F32),
            jax.ShapeDtypeStruct((1, D), F32),
        ],
        compiler_params=pltpu.CompilerParams(vmem_limit_bytes=40 * MIB),
        cost_estimate=pl.CostEstimate(
            flops=images * count * D * 20, bytes_accessed=images * count * D * 8, transcendentals=0
        ),
        name="norm_one",
    )(tokens, cotangent, gain, shift)


def attend_kernel(
    owner, first_row, a_ref, mean_ref, g_ref, s_ref, wq_ref, wk_ref, wv_ref,
    q_ref, k_ref, v_ref, e_ref, o_ref, li_ref, bias_ref, sk_ref, sv_ref,
):
    rows = a_ref.shape[1] // ROW

    @pl.when(pl.program_id(0) == 0)
    def _():
        query = lax.broadcasted_iota(jnp.int32, (ROW, KEYS), 0)
        key = lax.broadcasted_iota(jnp.int32, (ROW, KEYS), 1)
        for row in range(rows):
            own = jnp.where(key <= query, 0.0, -1e30)
            earlier = jnp.where(key - ROW < first_row[0] + row, math.log2(ROW), -1e30)
            bias_ref[row] = jnp.where(key < ROW, own, earlier)

    a1 = a_ref[0]
    q_ref[0] = dot(a1, wq_ref[0]).astype(BF16)
    k_ref[0] = dot(a1, wk_ref[0]).astype(BF16)
    v_ref[0] = dot(a1, wv_ref[0]).astype(BF16)
    mean_a = (mean_ref[0].astype(F32) * g_ref[...] + s_ref[...]).astype(BF16)
    sk_ref[...] = dot(mean_a, wk_ref[0]).astype(BF16)
    sv_ref[...] = dot(mean_a, wv_ref[0]).astype(BF16)
    masks = head_masks(BF16)
    ones = [jnp.broadcast_to(mask, (KEYS, PAIR)) for mask in masks]
    scale = LOG2E / math.sqrt(HD)

    def one_row(row, carry):
        here = pl.ds(pl.multiple_of(row * ROW, ROW), ROW)
        for pair in range(PAIRS):
            lanes = slice(pair * PAIR, (pair + 1) * PAIR)
            query = q_ref[0, here, lanes]
            keys = jnp.concatenate([k_ref[0, here, lanes], sk_ref[:, lanes]], 0)
            values = jnp.concatenate([v_ref[0, here, lanes], sv_ref[:, lanes]], 0)
            total = None
            for half in range(2):
                score = dot_nt(query, keys * masks[half]) * scale + bias_ref[row]
                weight = jnp.exp2(score - jnp.max(score, -1, keepdims=True)).astype(BF16)
                e_ref[0, row, 2 * pair + half] = weight
                part = dot(weight, jnp.concatenate([values * masks[half], ones[half]], 1))
                total = part if total is None else total + part
            inverse = 1.0 / total[:, PAIR:]
            o_ref[0, here, lanes] = (total[:, :PAIR] * inverse).astype(BF16)
            li_ref[0, here, lanes] = inverse.astype(BF16)
        return carry

    lax.fori_loop(0, rows, one_row, 0)


def attend_call(owner, first_row, a1, mean_all, gain, shift, slots):
    images, count, _ = a1.shape
    rows = count // ROW
    tokens_shape = jax.ShapeDtypeStruct((images, count, D), BF16)
    return pl.pallas_call(
        attend_kernel,
        grid_spec=pltpu.PrefetchScalarGridSpec(
            num_scalar_prefetch=2,
            grid=(images,),
            in_specs=[
                tile_spec(count, D), tile_spec(ROWS_IMG, D), whole_spec((1, D)), whole_spec((1, D)),
                weight_spec(0), weight_spec(1), weight_spec(2),
            ],
            out_specs=[tile_spec(count, D)] * 3
            + [tile_spec(rows, HEADS, ROW, KEYS)]
            + [tile_spec(count, D)] * 2,
            scratch_shapes=[
                pltpu.VMEM((rows, ROW, KEYS), F32),
                pltpu.VMEM((ROWS_IMG, D), BF16),
                pltpu.VMEM((ROWS_IMG, D), BF16),
            ],
        ),
        out_shape=[tokens_shape] * 3
        + [jax.ShapeDtypeStruct((images, rows, HEADS, ROW, KEYS), BF16)]
        + [tokens_shape] * 2,
        compiler_params=pltpu.CompilerParams(vmem_limit_bytes=56 * MIB),
        cost_estimate=pl.CostEstimate(
            flops=images * count * D * D * 10, bytes_accessed=images * count * D * 20, transcendentals=0
        ),
        name="attend",
    )(owner, first_row, a1, mean_all, gain, shift, slots, slots, slots)


def ff_kernel(
    owner, x_ref, o_ref, cot_ref, li_ref, g_ref, s_ref, bu_ref, bd_ref,
    wo_ref, u0_ref, u1_ref, u2_ref, u3_ref, d0_ref, d1_ref, d2_ref, d3_ref,
    out_ref, dr_ref, do_ref, grads_ref, gg_ref, gs_ref, gbu_ref,
    acc_ref, h_ref, xh_ref, da_ref,
):
    step = pl.program_id(0)
    ups = (u0_ref, u1_ref, u2_ref, u3_ref)
    downs = (d0_ref, d1_ref, d2_ref, d3_ref)

    @pl.when(step == 0)
    def _():
        acc_ref[...] = jnp.zeros_like(acc_ref)
        gg_ref[...] = jnp.zeros_like(gg_ref)
        gs_ref[...] = jnp.zeros_like(gs_ref)
        gbu_ref[...] = jnp.zeros_like(gbu_ref)

    hidden = x_ref[0].astype(F32) + dot(o_ref[0], wo_ref[0])
    normal, spread = normalize(hidden)
    xh_ref[...] = normal
    h_ref[...] = hidden + bd_ref[...]
    a2 = (normal * g_ref[...] + s_ref[...]).astype(BF16)
    a2_t = a2.T
    cot = cot_ref[0]
    cot_t = cot.T
    c_one = math.sqrt(2.0 / math.pi)
    c_two = c_one * 0.044715
    for block in range(NF):
        w_up = ups[block][0]
        w_down = downs[block][0]
        pre = dot(a2, w_up) + bu_ref[:, block * D : (block + 1) * D]
        d_act = dot_nt(cot, w_down)
        square = pre * pre
        half = 0.5 + 0.5 * jnp.tanh(pre * (c_one + c_two * square))
        act = pre * half
        slope = half + act * (1.0 - half) * (2.0 * c_one + (6.0 * c_two) * square)
        act = act.astype(BF16)
        d_pre = d_act * slope
        gbu_ref[:, block * D : (block + 1) * D] += jnp.sum(d_pre, 0, keepdims=True)
        d_pre = d_pre.astype(BF16)
        h_ref[...] += dot(act, w_down)
        part = dot_nt(d_pre, w_up)
        if block == 0:
            da_ref[...] = part
        else:
            da_ref[...] += part
        acc_ref[1 + block] += dot(a2_t, d_pre)
        acc_ref[1 + NF + block] += dot(cot_t, act)
    out_ref[0] = h_ref[...].astype(BF16)
    d_a2 = da_ref[...]
    normal = xh_ref[...]
    gs_ref[...] += jnp.sum(d_a2, 0, keepdims=True)
    gg_ref[...] += jnp.sum(d_a2 * normal, 0, keepdims=True)
    d_normal = d_a2 * g_ref[...]
    middle = jnp.mean(d_normal, -1, keepdims=True)
    along = jnp.mean(d_normal * normal, -1, keepdims=True)
    d_hidden = cot.astype(F32) + spread * (d_normal - middle - normal * along)
    branch = d_hidden.astype(BF16)
    dr_ref[0] = branch
    acc_ref[0] += dot(o_ref[0].T, branch)
    do_ref[0] = (dot_nt(branch, wo_ref[0]) * li_ref[0].astype(F32)).astype(BF16)

    @pl.when(step == pl.num_programs(0) - 1)
    def _():
        for block in range(1 + NF):
            grads_ref[block] = acc_ref[block].astype(BF16)
        for block in range(1 + NF, 1 + 2 * NF):
            grads_ref[block] = acc_ref[block].T.astype(BF16)


def ff_call(owner, tokens, attended, cotangent, inverse, gain, shift, bias_up, bias_down, slots):
    images, count, _ = tokens.shape
    tokens_shape = jax.ShapeDtypeStruct((images, count, D), BF16)
    blocks = 1 + 2 * NF
    return pl.pallas_call(
        ff_kernel,
        grid_spec=pltpu.PrefetchScalarGridSpec(
            num_scalar_prefetch=1,
            grid=(images,),
            in_specs=[tile_spec(count, D)] * 4
            + [whole_spec((1, D)), whole_spec((1, D)), whole_spec((1, FF)), whole_spec((1, D))]
            + [weight_spec(3 + block) for block in range(blocks)],
            out_specs=[tile_spec(count, D)] * 3
            + [out_whole((blocks, D, D)), out_whole((1, D)), out_whole((1, D)), out_whole((1, FF))],
            scratch_shapes=[
                pltpu.VMEM((blocks, D, D), F32),
                pltpu.VMEM((count, D), F32),
                pltpu.VMEM((count, D), F32),
                pltpu.VMEM((count, D), F32),
            ],
        ),
        out_shape=[tokens_shape] * 3
        + [
            jax.ShapeDtypeStruct((blocks, D, D), BF16),
            jax.ShapeDtypeStruct((1, D), F32),
            jax.ShapeDtypeStruct((1, D), F32),
            jax.ShapeDtypeStruct((1, FF), F32),
        ],
        compiler_params=pltpu.CompilerParams(vmem_limit_bytes=60 * MIB),
        cost_estimate=pl.CostEstimate(
            flops=images * count * D * D * 54, bytes_accessed=images * count * D * 14, transcendentals=0
        ),
        name="feed_forward",
    )(owner, tokens, attended, cotangent, inverse, gain, shift, bias_up, bias_down, *([slots] * blocks))


def back_kernel(
    owner, q_ref, k_ref, v_ref, o_ref, do_ref, e_ref, xh_ref, mean_ref, g_ref, s_ref,
    wq_ref, wk_ref, wv_ref,
    dlow_ref, dm_ref, grads_ref, gg_ref, gs_ref,
    acc_ref, dt_ref, sk_ref, sv_ref, dsk_ref, dsv_ref, skt_ref,
):
    step = pl.program_id(0)
    rows = q_ref.shape[1] // ROW
    scale = 1.0 / math.sqrt(HD)

    @pl.when(step == 0)
    def _():
        acc_ref[...] = jnp.zeros_like(acc_ref)
        gg_ref[...] = jnp.zeros_like(gg_ref)
        gs_ref[...] = jnp.zeros_like(gs_ref)

    mean_x = mean_ref[0].astype(F32)
    mean_a = (mean_x * g_ref[...] + s_ref[...]).astype(BF16)
    sum_k = dot(mean_a, wk_ref[0]).astype(BF16)
    sk_ref[...] = sum_k
    skt_ref[...] = (sum_k * scale).T
    sv_ref[...] = dot(mean_a, wv_ref[0]).astype(BF16)
    dsk_ref[...] = jnp.zeros_like(dsk_ref)
    dsv_ref[...] = jnp.zeros_like(dsv_ref)
    masks = head_masks(BF16)
    minus = [jnp.broadcast_to(-mask, (KEYS, PAIR)) for mask in masks]

    def one_row(row, carry):
        here = pl.ds(pl.multiple_of(row * ROW, ROW), ROW)
        d_out = do_ref[0, here, :]
        d_out_o = d_out * o_ref[0, here, :]
        q_t = (q_ref[0, here, :] * scale).T
        d_out_t = d_out.T
        k_t = jnp.concatenate([(k_ref[0, here, :] * scale).T, skt_ref[...]], 1)
        for pair in range(PAIRS):
            lanes = slice(pair * PAIR, (pair + 1) * PAIR)
            values = jnp.concatenate([v_ref[0, here, lanes], sv_ref[:, lanes]], 0)
            left = jnp.concatenate([d_out[:, lanes], d_out_o[:, lanes]], 1)
            for half in range(2):
                head = 2 * pair + half
                mine = slice(head * HD, (head + 1) * HD)
                right = jnp.concatenate([values * masks[half], minus[half]], 1)
                weight = e_ref[0, row, head]
                d_score = weight * dot_nt(left, right).astype(BF16)
                d_v = dot(d_out_t[mine], weight)
                d_k = dot(q_t[mine], d_score)
                d_q = dot_nt(k_t[mine], d_score)
                dt_ref[mine, :] = d_q.astype(BF16)
                dt_ref[D + head * HD : D + (head + 1) * HD, :] = d_k[:, :ROW].astype(BF16)
                dt_ref[2 * D + head * HD : 2 * D + (head + 1) * HD, :] = d_v[:, :ROW].astype(BF16)
                dsk_ref[mine, :] += d_k[:, PAIR:]
                dsv_ref[mine, :] += d_v[:, PAIR:]
        normal = xh_ref[0, here, :].astype(F32)
        a1 = (normal * g_ref[...] + s_ref[...]).astype(BF16)
        acc_ref[...] += dot(dt_ref[...], a1)
        low = (
            dot(wq_ref[0], dt_ref[0:D, :])
            + dot(wk_ref[0], dt_ref[D : 2 * D, :])
            + dot(wv_ref[0], dt_ref[2 * D : 3 * D, :])
        ).T
        dlow_ref[0, here, :] = low.astype(BF16)
        gs_ref[...] += jnp.sum(low, 0, keepdims=True)
        gg_ref[...] += jnp.sum(low * normal, 0, keepdims=True)
        return carry

    lax.fori_loop(0, rows, one_row, 0)
    d_sum_k = dsk_ref[:, ROW - PAIR :].astype(BF16)
    d_sum_v = dsv_ref[:, ROW - PAIR :].astype(BF16)
    acc_ref[D : 2 * D, :] += dot(d_sum_k, mean_a)
    acc_ref[2 * D : 3 * D, :] += dot(d_sum_v, mean_a)
    d_mean = (dot(wk_ref[0], d_sum_k) + dot(wv_ref[0], d_sum_v)).T
    dm_ref[0] = d_mean.astype(BF16)
    gs_ref[...] += jnp.sum(d_mean, 0, keepdims=True)
    gg_ref[...] += jnp.sum(d_mean * mean_x, 0, keepdims=True)

    @pl.when(step == pl.num_programs(0) - 1)
    def _():
        for block in range(3):
            grads_ref[block] = acc_ref[block * D : (block + 1) * D, :].T.astype(BF16)


def back_call(owner, queries, keys, values, attended, d_out, weights, normal, mean_all, gain, shift, slots):
    images, count, _ = queries.shape
    rows = count // ROW
    return pl.pallas_call(
        back_kernel,
        grid_spec=pltpu.PrefetchScalarGridSpec(
            num_scalar_prefetch=1,
            grid=(images,),
            in_specs=[tile_spec(count, D)] * 5
            + [tile_spec(rows, HEADS, ROW, KEYS), tile_spec(count, D), tile_spec(ROWS_IMG, D)]
            + [whole_spec((1, D)), whole_spec((1, D))]
            + [weight_spec(block) for block in range(3)],
            out_specs=[
                tile_spec(count, D), tile_spec(ROWS_IMG, D), out_whole((3, D, D)),
                out_whole((1, D)), out_whole((1, D)),
            ],
            scratch_shapes=[
                pltpu.VMEM((3 * D, D), F32),
                pltpu.VMEM((3 * D, ROW), BF16),
                pltpu.VMEM((ROWS_IMG, D), BF16),
                pltpu.VMEM((ROWS_IMG, D), BF16),
                pltpu.VMEM((D, PAIR), F32),
                pltpu.VMEM((D, PAIR), F32),
                pltpu.VMEM((D, ROWS_IMG), BF16),
            ],
        ),
        out_shape=[
            jax.ShapeDtypeStruct((images, count, D), BF16),
            jax.ShapeDtypeStruct((images, ROWS_IMG, D), BF16),
            jax.ShapeDtypeStruct((3, D, D), BF16),
            jax.ShapeDtypeStruct((1, D), F32),
            jax.ShapeDtypeStruct((1, D), F32),
        ],
        compiler_params=pltpu.CompilerParams(vmem_limit_bytes=56 * MIB),
        cost_estimate=pl.CostEstimate(
            flops=images * count * D * D * 20, bytes_accessed=images * count * D * 24, transcendentals=0
        ),
        name="attend_back",
    )(owner, queries, keys, values, attended, d_out, weights, normal, mean_all, gain, shift, slots, slots, slots)


def last_kernel(x_ref, low_ref, dr_ref, dm_ref, g_ref, out_ref):
    for row in range(dm_ref.shape[1]):
        here = slice(row * ROW, (row + 1) * ROW)
        normal, spread = normalize(x_ref[0, here, :].astype(F32))
        total = low_ref[0, here, :].astype(F32) + dm_ref[0, row : row + 1, :] * (1.0 / ROW)
        d_normal = total * g_ref[...]
        middle = jnp.mean(d_normal, -1, keepdims=True)
        along = jnp.mean(d_normal * normal, -1, keepdims=True)
        out_ref[0, here, :] = dr_ref[0, here, :].astype(F32) + spread * (d_normal - middle - normal * along)


def last_call(tokens, d_low, d_branch, d_mean, gain):
    images, count, _ = tokens.shape
    return pl.pallas_call(
        last_kernel,
        grid=(images,),
        in_specs=[tile_spec(count, D)] * 3 + [tile_spec(count // ROW, D), whole_spec((1, D))],
        out_specs=tile_spec(count, D),
        out_shape=jax.ShapeDtypeStruct((images, count, D), F32),
        compiler_params=pltpu.CompilerParams(vmem_limit_bytes=40 * MIB),
        cost_estimate=pl.CostEstimate(
            flops=images * count * D * 20, bytes_accessed=images * count * D * 10, transcendentals=0
        ),
        name="norm_one_back",
    )(tokens, d_low, d_branch, d_mean, gain)


def adamw_update(weight_now, gradient, first_moment, second_moment, decay_rate, step_rate):
    first_new = 0.9 * first_moment + 0.1 * gradient
    second_new = 0.95 * second_moment + 0.05 * gradient * gradient
    direction = first_new / (1.0 - 0.9**STEP) / (jnp.sqrt(second_new / (1.0 - 0.95**STEP)) + 1e-08)
    return (weight_now - step_rate * (direction + decay_rate * weight_now), first_new, second_new)


def sum_everywhere(value):
    for axis in ("narrow", "wide"):
        size = lax.axis_size(axis)
        bit = 1
        while bit < size:
            value = value + lax.ppermute(value, axis, [(index, index ^ bit) for index in range(size)])
            bit *= 2
    return value


def share_sums(grads):
    blocks = grads.shape[0]
    narrow = lax.axis_size("narrow")
    wide = lax.axis_size("wide")
    parts = lax.all_to_all(grads.reshape(blocks, narrow, D // narrow, D), "narrow", 1, 1, tiled=True)
    rows = jnp.sum(parts.astype(F32), 1).astype(BF16)
    pieces = rows.reshape(blocks, wide, -1, D).swapaxes(0, 1)
    parts = lax.all_to_all(pieces, "wide", 0, 0, tiled=True)
    return jnp.sum(parts.astype(F32), 0).astype(BF16)


def to_slots(shares, owner_list):
    wide = lax.axis_size("wide")
    slotted = jnp.zeros((wide,) + shares.shape[1:], BF16).at[owner_list].set(shares)
    parts = lax.all_to_all(slotted, "wide", 0, 0, tiled=True)
    return parts.reshape(1, -1, D).astype(F32)


def per_device(
    tokens, cotangent, owner_list, master, moment_one, moment_two, small_params, small_one, small_two
):
    images, count, _ = tokens.shape
    rows = count // ROW
    wide = lax.axis_size("wide")
    small = small_params.reshape(1, -1)
    gain_one = small[:, 0:D]
    shift_one = small[:, D : 2 * D]
    gain_two = small[:, 2 * D : 3 * D]
    shift_two = small[:, 3 * D : 4 * D]
    bias_up = small[:, 4 * D : 4 * D + FF]
    bias_down = small[:, 4 * D + FF :]
    low_master = master.astype(BF16)
    slots = lax.all_gather(low_master.reshape(-1, D), ("wide", "narrow"), axis=0, tiled=True)
    slots = slots.reshape(-1, D, D)
    a1, normal, means, bias_down_grad = norm_call(tokens, cotangent, gain_one, shift_one)
    gathered = lax.all_gather(means.astype(BF16).reshape(-1, D), "wide", axis=0, tiled=True)
    mean_all = gathered.reshape(wide, images, rows, D).swapaxes(0, 1).reshape(images, ROWS_IMG, D)
    first_row = (lax.axis_index("wide") * rows).astype(jnp.int32).reshape(1)
    queries, keys, values, weights, attended, inverse = attend_call(
        owner_list, first_row, a1, mean_all, gain_one, shift_one, slots
    )
    block_out, d_branch, d_out, grads_late, gain_two_grad, shift_two_grad, bias_up_grad = ff_call(
        owner_list, tokens, attended, cotangent, inverse, gain_two, shift_two, bias_up, bias_down, slots
    )
    d_low, d_mean, grads_early, gain_one_grad, shift_one_grad = back_call(
        owner_list, queries, keys, values, attended, d_out, weights, normal, mean_all, gain_one, shift_one, slots
    )
    pieces = d_mean.reshape(images, wide, rows, D).swapaxes(0, 1)
    own_mean = jnp.sum(lax.all_to_all(pieces, "wide", 0, 0, tiled=True).astype(F32), 0)
    grad_tokens = last_call(tokens, d_low, d_branch, own_mean, gain_one)
    own_grad = to_slots(share_sums(grads_late), owner_list[3:]) + to_slots(
        share_sums(grads_early), owner_list[:3]
    )
    small_grad = sum_everywhere(
        jnp.concatenate(
            [gain_one_grad, shift_one_grad, gain_two_grad, shift_two_grad, bias_up_grad, bias_down_grad], 1
        )
    ).reshape(-1)
    owns_slot = jnp.any(owner_list == lax.axis_index("wide"))
    slot_weight, slot_first, slot_second = adamw_update(
        master, own_grad, moment_one, moment_two, 0.1, RATE
    )
    new_master = jnp.where(owns_slot, slot_weight, master)
    new_one = jnp.where(owns_slot, slot_first, moment_one)
    new_two = jnp.where(owns_slot, slot_second, moment_two)
    small_new, small_one_new, small_two_new = adamw_update(
        small_params, small_grad, small_one, small_two, 0.0, GAIN_RATE
    )
    return (block_out, grad_tokens, new_master, new_one, new_two, small_new, small_one_new, small_two_new)


def solution(mesh):
    split = P("narrow", "wide", None)
    slot = P("wide", "narrow", None)
    return jax.shard_map(
        per_device,
        mesh=mesh,
        in_specs=(split, split, P(), slot, slot, slot, P(), P(), P()),
        out_specs=(split, split, slot, slot, slot, P(), P(), P()),
        check_vma=False,
    )
```

time: 1300 us -> 560 us (0.43); the launches traced: 1280 us -> 558 us
  matrix products: 496 us -> 0 us
  local copies, waits for them, and re-layouts: 340 us -> 32.1 us
  Pallas kernels: 0 us -> 300 us
  other arithmetic: 240 us -> 12 us
  blocking collectives: 121 us -> 60.6 us
  starting transfers between devices: 0.21 us -> 39.8 us
  waiting for transfers between devices: 70.8 us -> 98.6 us
    dot_general x24 -> x0, matrix products: 496 us -> none  [the longest x1 48 us: per_device(): jnp.einsum('nd,fd->nf', cot_rows, back_blocks[4 + ff_blocks:].reshape(FF,...]
    pallas_call x0 -> x5, Pallas kernels: none -> 300 us  [the longest x1 119 us: ff_call(): pl.pallas_call(ff_kernel, grid_spec=pltpu.PrefetchScalarGridSpec(num_scal...]
    convert_element_type x10 -> x2, other arithmetic: 131 us -> 1.79 us  [the longest x1 1.78 us: per_device(): low_master = master.astype(BF16)]
    another operation x7 -> x2, local copies, waits for them, and re-layouts: 113 us -> 1.46 us  [the longest x2 32.3 us: per_device(): jnp.stack([query_grad.reshape(-1, D), key_grad.reshape(-1, D), value_grad...]
    reshape x8, local copies, waits for them, and re-layouts: 119 us -> 10.7 us  [the longest x2 7.7 us: share_sums(): grads.reshape(blocks, narrow, D // narrow, D)]
    all_to_all x0 -> x6, waiting for transfers between devices: none -> 71.1 us  [the longest x2 57.4 us: share_sums(): parts = lax.all_to_all(pieces, 'wide', 0, 0, tiled=True)]
    reduce_sum x10 -> x5, other arithmetic: 73.9 us -> 6.26 us  [the longest x2 4.39 us: share_sums(): rows = jnp.sum(parts.astype(F32), 1).astype(BF16)]
    all_gather x1, waiting for transfers between devices: 62 us -> 19.1 us  [per_device(): lax.all_gather(low_master.reshape(-1, D), ('wide', 'narrow'), axis=0, til...]
  transfers between devices with their start and end apart: 5 -> 12, of which waited for: 2 -> 8; matrix products, arithmetic and copies ran while one was open for 23% -> 5% of each run, Pallas kernels for 0% -> 4%
where the time goes in v1:
time: 560 us; the launch traced here: 558 us
  Pallas kernels  300 us (54%)
  waiting for transfers between devices  98.6 us (18%)
  blocking collectives  60.6 us (11%)
  starting transfers between devices  39.8 us (7%)
  local copies, waits for them, and re-layouts  32.1 us (6%)
  between operations  14.4 us (3%)
  other arithmetic  12 us (2%)
    pallas_call x1, Pallas kernels, ff_call(): pl.pallas_call(ff_kernel, grid_spec=pltpu.PrefetchScalarGridSpec(num_scal...  119 us
    pallas_call x1, Pallas kernels, back_call(): pl.pallas_call(back_kernel, grid_spec=pltpu.PrefetchScalarGridSpec(num_sc...  112 us
    all_to_all x2, waiting for transfers between devices, share_sums(): parts = lax.all_to_all(pieces, 'wide', 0, 0, tiled=True)  57.4 us
    all_gather x1, blocking collectives, per_device(): lax.all_gather(means.astype(BF16).reshape(-1, D), 'wide', axis=0, tiled=T...  47.9 us
    pallas_call x1, Pallas kernels, attend_call(): pl.pallas_call(attend_kernel, grid_spec=pltpu.PrefetchScalarGridSpec(num_...  46.3 us
    all_gather x1, waiting for transfers between devices, per_device(): lax.all_gather(low_master.reshape(-1, D), ('wide', 'narrow'), axis=0, til...  19.1 us
    all_to_all x2, starting transfers between devices, to_slots(): parts = lax.all_to_all(slotted, 'wide', 0, 0, tiled=True)  15.4 us
    all_to_all x1, waiting for transfers between devices, per_device(): lax.all_to_all(pieces, 'wide', 0, 0, tiled=True).astype(F32)  13.7 us
  transfers between devices with their start and end apart: 12, of which 8 were waited for; matrix products, arithmetic and copies ran while one was open for 5% of the time, Pallas kernels for 4%

profile of v1, /device:TPU:0, one launch (start us, length us, event | category | flops | bytes accessed | tf_op | source)
XLA Modules:
  0.0 557.9 jit_solution(11818917637441649972)
XLA Ops:
  7.2 1.8 convert_element_type.50
  9.0 0.7 reshape.109
  11.0 10.0 %norm_one.1 = (bf16[8,768,512]{2,1,0:T(8,128)(2,1)S(1)}, bf16[8,768,512]{2,1,0:T(8,128)(2,1)S(1)}, f32[8,4,512]{2,1,0:T(4,128)S(1)}, f32[1,512]{1,0:T(1,128)S(1)}) custom-call(bf16[8,768,512]{2,1,0:T(8,128)(2,1)} %x_ref.5, bf16[8,768,512]{2,1,0:T(8,128)(2,1)} %cot_ref.3, f32[1,512]{1,0:T(1,128)S(1)} %get-tuple-element.62.g_ref, ...), custom_call_target="tpu_custom_call" | custom-call | flops 62914560 | bytes 25165824 | tf_op jit(solution)/shard_map/norm_one/pallas_call | solution.py:93
  21.0 2.6 copy-done.5
  23.5 2.7 copy-done.6
  26.3 47.9 %all_gather.6 = bf16[512,512]{1,0:T(8,128)(2,1)S(1)} all-gather(bf16[32,512]{1,0:T(8,128)(2,1)S(1)} %reshape.110), channel_id=1, replica_groups=mesh['wide'=16,'narrow'=2] {'wide'}, dimensions={0}, use_global_device_ids=true | all-gather | bytes 557056 | tf_op jit(solution)/shard_map/all_gather | solution.py:500
  74.5 0.9 reshape.112.mean_ref
  75.4 19.1 %all-gather.3.cloned.1.call-done = bf16[1,8192,512]{2,1,0:T(8,128)(2,1)} async-done(((bf16[1,256,512]{2,1,0:T(8,128)(2,1)}), bf16[1,8192,512]{2,1,0:T(8,128)(2,1)}) %all-gather.3.cloned.1.call-update) | async-done | bytes 8388624 | tf_op jit(solution)/shard_map/all_gather | solution.py:497
  94.6 46.3 %attend.1 = (bf16[8,768,512]{2,1,0:T(8,128)(2,1)}, bf16[8,768,512]{2,1,0:T(8,128)(2,1)}, bf16[8,768,512]{2,1,0:T(8,128)(2,1)}, bf16[8,4,8,192,256]{4,3,2,1,0:T(8...) custom-call(s32[12]{0:T(128)} %owner.5, s32[1]{0:T(128)} %bitcast.first_row, ...), custom_call_target="tpu_custom_call" | custom-call | flops 16106127360 | bytes 62914560 | tf_op jit(solution)/shard_map/attend/pallas_call | solution.py:164
  140.9 118.6 %feed_forward.1 = (bf16[8,768,512]{2,1,0:T(8,128)(2,1)}, bf16[8,768,512]{2,1,0:T(8,128)(2,1)}, bf16[8,768,512]{2,1,0:T(8,128)(2,1)}, bf16[9,512,512]{2,1,0:T(8,1...) custom-call(s32[12]{0:T(128)} %owner.5, bf16[8,768,512]{2,1,0:T(8,128)(2,1)} %x_ref.5, ...), custom_call_target="tpu_custom_call" | custom-call | flops 86973087744 | bytes 44040192 | tf_op jit(solution)/shard_map/feed_forward/pallas_call | solution.py:267
  259.5 112.2 %attend_back.1 = (bf16[8,768,512]{2,1,0:T(8,128)(2,1)}, bf16[8,64,512]{2,1,0:T(8,128)(2,1)}, bf16[3,512,512]{2,1,0:T(8,128)(2,1)}, f32[1,512]{1,0:T(1,128)}, f32[1,512]{1,0:T(1,128)}) custom-call(s32[12]{0:T(128)} %owner.5, bf16[8,768,512]{2,1,0:T(8,128)(2,1)} %get-tuple-element.35.q_ref, bf16[8,768,512]{2,1,0:T(8,128)(2,1)} %get-tuple-element.36.k_ref, ...), custom_call_target="tpu_custom_call" | custom-call | flops 32212254720 | bytes 75497472 | tf_op jit(solution)/shard_map/attend_back/pallas_call | solution.py:383
  371.8 2.8 copy.26
  374.5 3.8 all-to-all-start.4
  378.4 4.9 copy.24
  383.4 1.0 copy.29
  384.5 12.7 %all_to_all.35 = bf16[9,2,256,512]{3,2,0,1:T(8,128)(2,1)} all-to-all(bf16[9,2,256,512]{3,2,0,1:T(8,128)(2,1)} %copy.24), channel_id=1, replica_groups=mesh['wide'=16,'narrow'=2] {'narrow'}, dimensions={1} | all-to-all | bytes 9437184 | tf_op jit(solution)/shard_map/all_to_all | solution.py:469
  397.2 4.5 all-to-all-start
  401.7 0.8 reduce_sum.60
  402.5 0.9 copy.27
  403.4 13.7 %all-to-all-done = bf16[16,8,4,512]{3,2,1,0:T(4,128)(2,1)S(1)} async-done(((bf16[16,8,4,512]{3,2,1,0:T(4,128)(2,1)}), bf16[16,8,4,512]{3,2,1,0:T(4,128)(2,1)S(1)}, u32[]{:S(2)}, u32[]{:S(2)}) %all-to-all-start) | async-done | bytes 524320 | tf_op jit(solution)/shard_map/all_to_all | solution.py:513
  417.1 0.8 copy-done.7
  417.9 3.9 all-to-all-start.5
  421.8 3.6 reduce_sum.58
  425.5 1.6 copy.25
  427.1 13.7 %all-to-all-done.5 = bf16[16,3,16,512]{3,2,1,0:T(8,128)(2,1)S(1)} async-done(((bf16[16,3,16,512]{3,2,1,0:T(8,128)(2,1)}), bf16[16,3,16,512]{3,2,1,0:T(8,128)(2,1)S(1)}, u32[]{:S(2)}, u32[]{:S(2)}) %all-to-all-start.5) | async-done | bytes 786464 | tf_op jit(solution)/shard_map/all_to_all | solution.py:472
  440.8 4.9 all-to-all-start.2
  446.0 0.7 broadcast.38.clone
  446.7 1.9 scatter_fusion.1
  448.7 43.7 %all-to-all-done.2 = bf16[16,9,16,512]{3,2,1,0:T(8,128)(2,1)S(1)} async-done(((bf16[16,9,16,512]{3,2,1,0:T(8,128)(2,1)}), bf16[16,9,16,512]{3,2,1,0:T(8,128)(2,1)S(1)}, u32[]{:S(2)}, u32[]{:S(2)}) %all-to-all-start.2) | async-done | bytes 2359328 | tf_op jit(solution)/shard_map/all_to_all | solution.py:472
  492.4 10.8 %all-to-all-start.6 = ((bf16[16,16,512]{2,1,0:T(8,128)(2,1)}), bf16[16,16,512]{2,1,0:T(8,128)(2,1)S(1)}, u32[]{:S(2)}, u32[]{:S(2)}) async-start(bf16[16,16,512]{2,1,0:T(8,128)(2,1)} %scatter_fusion.1), calls=%async_computation.6 | async-start | bytes 524288 | tf_op jit(solution)/shard_map/all_to_all | solution.py:479
  503.3 1.2 collective-permute-done
  504.5 2.0 collective-permute-start.1
  506.5 2.6 collective-permute-done.1
  509.1 1.5 collective-permute-start.2
  510.7 2.3 collective-permute-done.2
  513.0 1.5 collective-permute-start.3
  514.5 2.3 collective-permute-done.3
  516.8 2.2 collective-permute-start.4
  519.0 0.7 compare_reduce_fusion
  520.2 0.7 broadcast.38.clone.1
  520.9 2.4 scatter_fusion
  523.3 4.6 all-to-all-start.3
  528.0 0.6 multiply_subtract_fusion
  528.6 1.3 convert_reduce_fusion.dm_ref
  529.9 2.8 copy-done
  532.7 2.8 copy-done.1
  535.5 13.1 %norm_one_back.1 = f32[8,768,512]{2,1,0:T(8,128)} custom-call(bf16[8,768,512]{2,1,0:T(8,128)(2,1)S(1)} %copy-done, bf16[8,768,512]{2,1,0:T(8,128)(2,1)S(1)} %copy-done.1, bf16[8,768,512]{2,1,0:T(8,128)(2,1)} %get-tuple-element.42.dr_ref, f32[8,4,512]{2,1,0:T(4,128)S(1)} %convert_reduce_fusion.dm_ref, f32[1,512]{1,0:T(1,128)S(1)} %copy-done.3), custom_call_target="tpu_custom_call" | custom-call | flops 62914560 | bytes 31457280 | tf_op jit(solution)/shard_map/norm_one_back/pallas_call | solution.py:434
  548.7 2.4 fusion.3
  (67 shorter events, 2.8 us)
Async XLA Ops:
  7.2 87.4 %all-gather.3.cloned.1.call-start = ((), (), s32[]{:S(2)}) async-start(), calls=%async_computation.7 | async-start | bytes 8650752 | tf_op jit(solution)/shard_map/all_gather | solution.py:497
  11.0 10.0 %copy-start.2 = (f32[1,512]{1,0:T(1,128)}, f32[1,512]{1,0:T(1,128)S(1)}, u32[]{:S(2)}) copy-start(f32[1,512]{1,0:T(1,128)S(1)} %get-tuple-element.62.g_ref) | copy-start | bytes 6148
  11.0 10.0 %copy-start.4 = (f32[1,512]{1,0:T(1,128)}, f32[1,512]{1,0:T(1,128)S(1)}, u32[]{:S(2)}) copy-start(f32[1,512]{1,0:T(1,128)S(1)} %get-tuple-element.61.s_ref) | copy-start | bytes 6148
  20.9 2.6 copy-start.5
  23.5 2.7 copy-start.6
  374.5 8.7 %copy-start.9 = (bf16[8,64,512]{2,1,0:T(8,128)(2,1)S(1)}, bf16[8,64,512]{2,1,0:T(8,128)(2,1)}, u32[]{:S(2)}) copy-start(bf16[8,64,512]{2,1,0:T(8,128)(2,1)} %get-tuple-element.43) | copy-start | bytes 1572868
  374.5 9.9 %all-to-all-start.4 = ((bf16[3,2,256,512]{3,2,0,1:T(8,128)(2,1)}), bf16[3,2,256,512]{3,2,0,1:T(8,128)(2,1)S(1)}, u32[]{:S(2)}, u32[]{:S(2)}) async-start(bf16[3,2,256,512]{3,2,0,1:T(8,128)(2,1)} %copy.26), calls=%async_computation.4 | async-start | bytes 3145728 | tf_op jit(solution)/shard_map/all_to_all | solution.py:469
  397.2 19.9 %all-to-all-start = ((bf16[16,8,4,512]{3,2,1,0:T(4,128)(2,1)}), bf16[16,8,4,512]{3,2,1,0:T(4,128)(2,1)S(1)}, u32[]{:S(2)}, u32[]{:S(2)}) async-start(bf16[16,8,4,512]{3,2,1,0:T(4,128)(2,1)} %bitcast.26), calls=%async_computation | async-start | bytes 1048576 | tf_op jit(solution)/shard_map/all_to_all | solution.py:513
  417.1 0.8 copy-start.7
  417.9 23.0 %all-to-all-start.5 = ((bf16[16,3,16,512]{3,2,1,0:T(8,128)(2,1)}), bf16[16,3,16,512]{3,2,1,0:T(8,128)(2,1)S(1)}, u32[]{:S(2)}, u32[]{:S(2)}) async-start(bf16[16,3,16,512]{3,2,1,0:T(8,128)(2,1)} %copy.27), calls=%async_computation.5 | async-start | bytes 1572864 | tf_op jit(solution)/shard_map/all_to_all | solution.py:472
  425.4 20.3 %copy-start.20 = (s32[12]{0:T(128)S(1)}, s32[12]{0:T(128)}, u32[]{:S(2)}) copy-start(s32[12]{0:T(128)} %owner.5) | copy-start | bytes 148
  425.4 20.3 %copy-start.19 = (f32[1,512]{1,0:T(1,128)S(1)}, f32[1,512]{1,0:T(1,128)}, u32[]{:S(2)}) copy-start(f32[1,512]{1,0:T(1,128)} %get-tuple-element.46) | copy-start | bytes 6148
  425.5 20.3 %copy-start.18 = (f32[1,512]{1,0:T(1,128)S(1)}, f32[1,512]{1,0:T(1,128)}, u32[]{:S(2)}) copy-start(f32[1,512]{1,0:T(1,128)} %get-tuple-element.47) | copy-start | bytes 6148
  425.5 20.3 %copy-start.17 = (f32[1,512]{1,0:T(1,128)S(1)}, f32[1,512]{1,0:T(1,128)}, u32[]{:S(2)}) copy-start(f32[1,512]{1,0:T(1,128)} %get-tuple-element.48) | copy-start | bytes 6148
  425.5 20.3 %copy-start.16 = (f32[1,512]{1,0:T(1,128)S(1)}, f32[1,512]{1,0:T(1,128)}, u32[]{:S(2)}) copy-start(f32[1,512]{1,0:T(1,128)} %get-tuple-element.49) | copy-start | bytes 6148
  425.5 20.3 %copy-start.15 = (f32[1,2048]{1,0:T(1,128)S(1)}, f32[1,2048]{1,0:T(1,128)}, u32[]{:S(2)}) copy-start(f32[1,2048]{1,0:T(1,128)} %get-tuple-element.50) | copy-start | bytes 24580
  427.1 100.8 %copy-start.12 = (f32[4608]{0:T(1024)S(1)}, f32[4608]{0:T(1024)}, u32[]{:S(2)}) copy-start(f32[4608]{0:T(1024)} %param.15) | copy-start | bytes 55300
  427.1 100.8 %copy-start.13 = (f32[4608]{0:T(1024)S(1)}, f32[4608]{0:T(1024)}, u32[]{:S(2)}) copy-start(f32[4608]{0:T(1024)} %param.16) | copy-start | bytes 55300
  427.1 100.8 %copy-start.14 = (f32[4608]{0:T(1024)S(1)}, f32[4608]{0:T(1024)}, u32[]{:S(2)}) copy-start(f32[4608]{0:T(1024)} %param.17) | copy-start | bytes 55300
  427.1 102.8 %copy-start.3 = (f32[1,512]{1,0:T(1,128)S(1)}, f32[1,512]{1,0:T(1,128)}, u32[]{:S(2)}) copy-start(f32[1,512]{1,0:T(1,128)} %copy-done.2) | copy-start | bytes 6148
  440.8 51.6 %all-to-all-start.2 = ((bf16[16,9,16,512]{3,2,1,0:T(8,128)(2,1)}), bf16[16,9,16,512]{3,2,1,0:T(8,128)(2,1)S(1)}, u32[]{:S(2)}, u32[]{:S(2)}) async-start(bf16[16,9,16,512]{3,2,1,0:T(8,128)(2,1)} %copy.25), calls=%async_computation.2 | async-start | bytes 4718592 | tf_op jit(solution)/shard_map/all_to_all | solution.py:472
  492.4 30.9 %all-to-all-start.6 = ((bf16[16,16,512]{2,1,0:T(8,128)(2,1)}), bf16[16,16,512]{2,1,0:T(8,128)(2,1)S(1)}, u32[]{:S(2)}, u32[]{:S(2)}) async-start(bf16[16,16,512]{2,1,0:T(8,128)(2,1)} %scatter_fusion.1), calls=%async_computation.6 | async-start | bytes 524288 | tf_op jit(solution)/shard_map/all_to_all | solution.py:479
  503.2 1.3 collective-permute-start
  504.5 4.6 collective-permute-start.1
  509.1 3.8 collective-permute-start.2
  513.0 3.8 collective-permute-start.3
  516.8 11.1 %collective-permute-start.4 = (f32[1,4608]{1,0:T(1,128)S(1)}, f32[1,4608]{1,0:T(1,128)S(1)}, u32[]{:S(2)}, u32[]{:S(2)}) collective-permute-start(f32[1,4608]{1,0:T(1,128)S(1)} %add.81), channel_id=1, source_target_pairs={{0,16},{2,18},{4,20},{6,22},{8,24},{10,26},{12,28},{14,30},{16,0},... | collective-permute-start | bytes 55304 | tf_op jit(solution)/shard_map/ppermute | solution.py:460
  523.3 25.3 %all-to-all-start.3 = ((bf16[16,16,512]{2,1,0:T(8,128)(2,1)}), bf16[16,16,512]{2,1,0:T(8,128)(2,1)S(1)}, u32[]{:S(2)}, u32[]{:S(2)}) async-start(bf16[16,16,512]{2,1,0:T(8,128)(2,1)} %scatter_fusion), calls=%async_computation.3 | async-start | bytes 524288 | tf_op jit(solution)/shard_map/all_to_all | solution.py:479
  529.9 2.8 copy-start
  532.7 2.8 copy-start.1
  535.5 13.2 %copy-start.8 = (f32[1,256,512]{2,1,0:T(8,128)S(1)}, f32[1,256,512]{2,1,0:T(8,128)}, u32[]{:S(2)}) copy-start(f32[1,256,512]{2,1,0:T(8,128)} %param.12) | copy-start | bytes 1572868
  535.5 13.2 %copy-start.10 = (f32[1,256,512]{2,1,0:T(8,128)S(1)}, f32[1,256,512]{2,1,0:T(8,128)}, u32[]{:S(2)}) copy-start(f32[1,256,512]{2,1,0:T(8,128)} %param.14) | copy-start | bytes 1572868
  535.5 13.2 %copy-start.11 = (f32[1,256,512]{2,1,0:T(8,128)S(1)}, f32[1,256,512]{2,1,0:T(8,128)}, u32[]{:S(2)}) copy-start(f32[1,256,512]{2,1,0:T(8,128)} %param.13) | copy-start | bytes 1572868
Sparse Core Ops, SparseCore 0:
  11.4 83.0 all-gather.2

commit v2 on v1

--- a/solution.py
+++ b/solution.py
@@ -1,3 +1,4 @@
+import functools
 import functools
 import math
 
@@ -64,6 +65,10 @@
     )
 
 
+def plain_weight_spec(block):
+    return pl.BlockSpec((1, D, D), lambda step, *_: (block, 0, 0), pipeline_mode=pl.Buffered(1))
+
+
 def out_whole(shape):
     zeros = (0,) * len(shape)
     return pl.BlockSpec(shape, lambda step, *_: zeros)
@@ -110,7 +115,7 @@
 
 
 def attend_kernel(
-    owner, first_row, a_ref, mean_ref, g_ref, s_ref, wq_ref, wk_ref, wv_ref,
+    first_row, a_ref, mean_ref, g_ref, s_ref, wq_ref, wk_ref, wv_ref,
     q_ref, k_ref, v_ref, e_ref, o_ref, li_ref, bias_ref, sk_ref, sv_ref,
 ):
     rows = a_ref.shape[1] // ROW
@@ -157,19 +162,19 @@
     lax.fori_loop(0, rows, one_row, 0)
 
 
-def attend_call(owner, first_row, a1, mean_all, gain, shift, slots):
+def attend_call(first_row, a1, mean_all, gain, shift, blocks):
     images, count, _ = a1.shape
     rows = count // ROW
     tokens_shape = jax.ShapeDtypeStruct((images, count, D), BF16)
     return pl.pallas_call(
         attend_kernel,
         grid_spec=pltpu.PrefetchScalarGridSpec(
-            num_scalar_prefetch=2,
+            num_scalar_prefetch=1,
             grid=(images,),
             in_specs=[
                 tile_spec(count, D), tile_spec(ROWS_IMG, D), whole_spec((1, D)), whole_spec((1, D)),
-                weight_spec(0), weight_spec(1), weight_spec(2),
-            ],
+            ]
+            + [plain_weight_spec(block) for block in range(3)],
             out_specs=[tile_spec(count, D)] * 3
             + [tile_spec(rows, HEADS, ROW, KEYS)]
             + [tile_spec(count, D)] * 2,
@@ -187,7 +192,7 @@
             flops=images * count * D * D * 10, bytes_accessed=images * count * D * 20, transcendentals=0
         ),
         name="attend",
-    )(owner, first_row, a1, mean_all, gain, shift, slots, slots, slots)
+    )(first_row, a1, mean_all, gain, shift, blocks, blocks, blocks)
 
 
 def ff_kernel(
@@ -296,21 +301,27 @@
     )(owner, tokens, attended, cotangent, inverse, gain, shift, bias_up, bias_down, *([slots] * blocks))
 
 
-def back_kernel(
-    owner, q_ref, k_ref, v_ref, o_ref, do_ref, e_ref, xh_ref, mean_ref, g_ref, s_ref,
-    wq_ref, wk_ref, wv_ref,
-    dlow_ref, dm_ref, grads_ref, gg_ref, gs_ref,
-    acc_ref, dt_ref, sk_ref, sv_ref, dsk_ref, dsv_ref, skt_ref,
-):
+def back_kernel(first, last, owner, *refs):
+    (q_ref, k_ref, v_ref, o_ref, do_ref, e_ref, xh_ref, mean_ref, g_ref, s_ref, wq_ref, wk_ref, wv_ref) = refs[:13]
+    refs = refs[13:]
+    if not first:
+        old_acc_ref, old_gg_ref, old_gs_ref = refs[:3]
+        refs = refs[4:]
+    dlow_ref, dm_ref, acc_ref, gg_ref, gs_ref = refs[:5]
+    refs = refs[5:]
+    if last:
+        grads_ref = refs[0]
+        refs = refs[1:]
+    dt_ref, sk_ref, sv_ref, dsk_ref, dsv_ref, skt_ref = refs
     step = pl.program_id(0)
     rows = q_ref.shape[1] // ROW
     scale = 1.0 / math.sqrt(HD)
 
     @pl.when(step == 0)
     def _():
-        acc_ref[...] = jnp.zeros_like(acc_ref)
-        gg_ref[...] = jnp.zeros_like(gg_ref)
-        gs_ref[...] = jnp.zeros_like(gs_ref)
+        acc_ref[...] = jnp.zeros_like(acc_ref) if first else old_acc_ref[...]
+        gg_ref[...] = jnp.zeros_like(gg_ref) if first else old_gg_ref[...]
+        gs_ref[...] = jnp.zeros_like(gs_ref) if first else old_gs_ref[...]
 
     mean_x = mean_ref[0].astype(F32)
     mean_a = (mean_x * g_ref[...] + s_ref[...]).astype(BF16)
@@ -371,30 +382,48 @@
     gs_ref[...] += jnp.sum(d_mean, 0, keepdims=True)
     gg_ref[...] += jnp.sum(d_mean * mean_x, 0, keepdims=True)
 
+    if not last:
+        return
+
     @pl.when(step == pl.num_programs(0) - 1)
     def _():
         for block in range(3):
             grads_ref[block] = acc_ref[block * D : (block + 1) * D, :].T.astype(BF16)
 
 
-def back_call(owner, queries, keys, values, attended, d_out, weights, normal, mean_all, gain, shift, slots):
-    images, count, _ = queries.shape
+def back_call(start, stop, before, owner, operands, gain, shift, slots):
+    images, count, _ = operands[0].shape
     rows = count // ROW
+    first, last = start == 0, stop == images
+
+    def at(*tail):
+        zeros = (0,) * len(tail)
+        return pl.BlockSpec((1,) + tail, lambda step, *_: (start + step,) + zeros)
+
+    in_specs = (
+        [at(count, D)] * 5
+        + [at(rows, HEADS, ROW, KEYS), at(count, D), at(ROWS_IMG, D)]
+        + [whole_spec((1, D)), whole_spec((1, D))]
+        + [weight_spec(block) for block in range(3)]
+    )
+    inputs = [owner, *operands, gain, shift, slots, slots, slots]
+    aliases = {}
+    if not first:
+        d_low, *sums = before
+        in_specs += [whole_spec((3 * D, D)), whole_spec((1, D)), whole_spec((1, D)), pl.BlockSpec(memory_space=pl.ANY)]
+        inputs += [*sums, d_low]
+        aliases = {len(inputs) - 1: 0}
     return pl.pallas_call(
-        back_kernel,
+        functools.partial(back_kernel, first, last),
         grid_spec=pltpu.PrefetchScalarGridSpec(
             num_scalar_prefetch=1,
-            grid=(images,),
-            in_specs=[tile_spec(count, D)] * 5
-            + [tile_spec(rows, HEADS, ROW, KEYS), tile_spec(count, D), tile_spec(ROWS_IMG, D)]
-            + [whole_spec((1, D)), whole_spec((1, D))]
-            + [weight_spec(block) for block in range(3)],
+            grid=(stop - start,),
+            in_specs=in_specs,
             out_specs=[
-                tile_spec(count, D), tile_spec(ROWS_IMG, D), out_whole((3, D, D)),
-                out_whole((1, D)), out_whole((1, D)),
-            ],
+                at(count, D), tile_spec(ROWS_IMG, D), out_whole((3 * D, D)), out_whole((1, D)), out_whole((1, D)),
+            ]
+            + [out_whole((3, D, D))] * last,
             scratch_shapes=[
-                pltpu.VMEM((3 * D, D), F32),
                 pltpu.VMEM((3 * D, ROW), BF16),
                 pltpu.VMEM((ROWS_IMG, D), BF16),
                 pltpu.VMEM((ROWS_IMG, D), BF16),
@@ -405,17 +434,21 @@
         ),
         out_shape=[
             jax.ShapeDtypeStruct((images, count, D), BF16),
-            jax.ShapeDtypeStruct((images, ROWS_IMG, D), BF16),
-            jax.ShapeDtypeStruct((3, D, D), BF16),
+            jax.ShapeDtypeStruct((stop - start, ROWS_IMG, D), BF16),
+            jax.ShapeDtypeStruct((3 * D, D), F32),
             jax.ShapeDtypeStruct((1, D), F32),
             jax.ShapeDtypeStruct((1, D), F32),
-        ],
+        ]
+        + [jax.ShapeDtypeStruct((3, D, D), BF16)] * last,
+        input_output_aliases=aliases,
         compiler_params=pltpu.CompilerParams(vmem_limit_bytes=56 * MIB),
         cost_estimate=pl.CostEstimate(
-            flops=images * count * D * D * 20, bytes_accessed=images * count * D * 24, transcendentals=0
+            flops=(stop - start) * count * D * D * 20,
+            bytes_accessed=(stop - start) * count * D * 24,
+            transcendentals=0,
         ),
         name="attend_back",
-    )(owner, queries, keys, values, attended, d_out, weights, normal, mean_all, gain, shift, slots, slots, slots)
+    )(*inputs)
 
 
 def last_kernel(x_ref, low_ref, dr_ref, dm_ref, g_ref, out_ref):
@@ -452,32 +485,100 @@
     return (weight_now - step_rate * (direction + decay_rate * weight_now), first_new, second_new)
 
 
+def swap(value, axis, bit):
+    size = lax.axis_size(axis)
+    return lax.ppermute(value, axis, [(index, index ^ bit) for index in range(size)])
+
+
 def sum_everywhere(value):
     for axis in ("narrow", "wide"):
-        size = lax.axis_size(axis)
         bit = 1
-        while bit < size:
-            value = value + lax.ppermute(value, axis, [(index, index ^ bit) for index in range(size)])
+        while bit < lax.axis_size(axis):
+            value = value + swap(value, axis, bit)
             bit *= 2
     return value
 
 
-def share_sums(grads):
+def join(value, axis, inner):
+    size = lax.axis_size(axis)
+    near = jnp.stack([value] + [swap(value, axis, inner * step) for step in range(1, size // inner)])
+    far = jnp.stack([near] + [swap(near, axis, step) for step in range(1, inner)], 1)
+    return jnp.take(far.reshape((size,) + value.shape), lax.axis_index(axis) ^ jnp.arange(size), axis=0)
+
+
+def fetch_blocks(low_master, owners, means):
+    wide = lax.axis_size("wide")
+    narrow = lax.axis_size("narrow")
+    pieces = lax.all_to_all(low_master.reshape(wide, -1, D), "wide", 0, 0, tiled=True)
+    mine = jnp.take(pieces, owners, axis=0)
+    count = owners.shape[0]
+    depth = mine.shape[1]
+    joined = join(jnp.concatenate([mine.reshape(-1, D), means.reshape(-1, D)], 0), "wide", near_size())
+    halves = join(joined[:, : count * depth], "narrow", 1)
+    blocks = halves.reshape(narrow, wide, count, depth, D).transpose(2, 0, 1, 3, 4).reshape(count, D, D)
+    mean_all = joined[:, count * depth :].reshape((wide,) + means.shape).swapaxes(0, 1)
+    return blocks, mean_all.reshape(means.shape[0], -1, D)
+
+
+def sum_narrow(grads):
     blocks = grads.shape[0]
     narrow = lax.axis_size("narrow")
+    me = lax.axis_index("narrow")
+    parts = grads.reshape(blocks, narrow, D // narrow, D)
+    total = lax.dynamic_index_in_dim(parts, me, 1, False).astype(F32)
+    for step in range(1, narrow):
+        total += swap(lax.dynamic_index_in_dim(parts, me ^ step, 1, False), "narrow", step).astype(F32)
+    return total.astype(BF16)
+
+
+def sum_group(pieces, stride):
+    size = pieces.shape[0]
+    me = lax.axis_index("wide") // stride % size
+    total = lax.dynamic_index_in_dim(pieces, me, 0, False).astype(F32)
+    for step in range(1, size):
+        part = lax.dynamic_index_in_dim(pieces, me ^ step, 0, False)
+        total += swap(part, "wide", step * stride).astype(F32)
+    return total
+
+
+def near_size():
+    return min(4, lax.axis_size("wide"))
+
+
+def to_pieces(rows):
     wide = lax.axis_size("wide")
-    parts = lax.all_to_all(grads.reshape(blocks, narrow, D // narrow, D), "narrow", 1, 1, tiled=True)
-    rows = jnp.sum(parts.astype(F32), 1).astype(BF16)
-    pieces = rows.reshape(blocks, wide, -1, D).swapaxes(0, 1)
-    parts = lax.all_to_all(pieces, "wide", 0, 0, tiled=True)
-    return jnp.sum(parts.astype(F32), 0).astype(BF16)
-
-
-def to_slots(shares, owner_list):
+    pieces = rows.reshape(rows.shape[0], wide, -1, D).swapaxes(0, 1)
+    return pieces.reshape(wide, -1, D)
+
+
+def sum_near(pieces):
+    inner = near_size()
+    parts = pieces.reshape((-1, inner) + pieces.shape[1:]).swapaxes(0, 1)
+    return sum_group(parts, 1).astype(BF16)
+
+
+def sum_far(pieces):
+    return sum_group(pieces, near_size())
+
+
+def to_slots(shares, owner_list, beside):
     wide = lax.axis_size("wide")
-    slotted = jnp.zeros((wide,) + shares.shape[1:], BF16).at[owner_list].set(shares)
-    parts = lax.all_to_all(slotted, "wide", 0, 0, tiled=True)
-    return parts.reshape(1, -1, D).astype(F32)
+    inner = near_size()
+    outer = wide // inner
+    me = lax.axis_index("wide")
+    far, near = me // inner, me % inner
+    slotted = jnp.zeros((wide,) + shares.shape[1:], BF16).at[owner_list].set(shares.astype(BF16))
+    slotted = slotted.reshape((outer, inner) + shares.shape[1:])
+    parts = [lax.dynamic_index_in_dim(slotted, far, 0, False)]
+    for step in range(1, outer):
+        parts.append(swap(lax.dynamic_index_in_dim(slotted, far ^ step, 0, False), "wide", step * inner))
+    parts, beside = lax.optimization_barrier((jnp.stack(parts, 1), beside))
+    pieces = [lax.dynamic_index_in_dim(parts, near, 0, False)]
+    for step in range(1, inner):
+        pieces.append(swap(lax.dynamic_index_in_dim(parts, near ^ step, 0, False), "wide", step))
+    pieces = jnp.stack(pieces, 1).reshape((wide,) + shares.shape[1:])
+    ordered = jnp.take(pieces, me ^ jnp.arange(wide), axis=0)
+    return ordered.reshape(1, -1, D).astype(F32), beside
 
 
 def per_device(
@@ -497,24 +598,36 @@
     slots = lax.all_gather(low_master.reshape(-1, D), ("wide", "narrow"), axis=0, tiled=True)
     slots = slots.reshape(-1, D, D)
     a1, normal, means, bias_down_grad = norm_call(tokens, cotangent, gain_one, shift_one)
-    gathered = lax.all_gather(means.astype(BF16).reshape(-1, D), "wide", axis=0, tiled=True)
-    mean_all = gathered.reshape(wide, images, rows, D).swapaxes(0, 1).reshape(images, ROWS_IMG, D)
+    blocks, mean_all = fetch_blocks(low_master, owner_list[:3], means.astype(BF16))
     first_row = (lax.axis_index("wide") * rows).astype(jnp.int32).reshape(1)
     queries, keys, values, weights, attended, inverse = attend_call(
-        owner_list, first_row, a1, mean_all, gain_one, shift_one, slots
+        first_row, a1, mean_all, gain_one, shift_one, blocks
     )
     block_out, d_branch, d_out, grads_late, gain_two_grad, shift_two_grad, bias_up_grad = ff_call(
         owner_list, tokens, attended, cotangent, inverse, gain_two, shift_two, bias_up, bias_down, slots
     )
-    d_low, d_mean, grads_early, gain_one_grad, shift_one_grad = back_call(
-        owner_list, queries, keys, values, attended, d_out, weights, normal, mean_all, gain_one, shift_one, slots
-    )
-    pieces = d_mean.reshape(images, wide, rows, D).swapaxes(0, 1)
-    own_mean = jnp.sum(lax.all_to_all(pieces, "wide", 0, 0, tiled=True).astype(F32), 0)
+    operands = (queries, keys, values, attended, d_out, weights, normal, mean_all)
+    quarter = images // 4
+    cuts = (0, quarter, images - quarter, images)
+    state = None
+    d_means = []
+    late = grads_late
+    stages = (sum_narrow, lambda sums: sum_near(to_pieces(sums)), sum_far)
+    for start, stop, stage in zip(cuts[:-1], cuts[1:], stages):
+        moved = stage(late)
+        d_low, d_mean, *state = back_call(
+            start, stop, state, owner_list, operands, gain_one, shift_one, slots
+        )
+        late, *state = lax.optimization_barrier((moved, d_low, *state))
+        d_means.append(d_mean)
+    d_low, _, gain_one_grad, shift_one_grad, grads_early = state
+    early = to_pieces(sum_narrow(grads_early))
+    depth = early.shape[1] // 3
+    last = sum_far(sum_near(jnp.concatenate([early] + [to_pieces(d_mean) for d_mean in d_means], 1)))
+    own_mean = last[3 * depth :].reshape(images, rows, D)
     grad_tokens = last_call(tokens, d_low, d_branch, own_mean, gain_one)
-    own_grad = to_slots(share_sums(grads_late), owner_list[3:]) + to_slots(
-        share_sums(grads_early), owner_list[:3]
-    )
+    shares = jnp.concatenate([last[: 3 * depth], late], 0).reshape(-1, depth, D)
+    own_grad, grad_tokens = to_slots(shares, owner_list, grad_tokens)
     small_grad = sum_everywhere(
         jnp.concatenate(
             [gain_one_grad, shift_one_grad, gain_two_grad, shift_two_grad, bias_up_grad, bias_down_grad], 1

time: 560 us -> 464 us (0.83)
  blocking collectives: 60.6 us -> 0 us
  waiting for transfers between devices: 98.6 us -> 45.6 us
  Pallas kernels: 300 us -> 317 us
    all_to_all x6 -> x1, waiting for transfers between devices: 71.1 us -> 0.01 us  [fetch_blocks(): lax.all_to_all(low_master.reshape(wide, -1, D), 'wide', 0, 0, tiled=True)]
    all_gather x1 -> x0, blocking collectives: 47.9 us -> none  [per_device(): lax.all_gather(means.astype(BF16).reshape(-1, D), 'wide', axis=0, tiled=T...]
    ppermute x5 -> x32, waiting for transfers between devices: 8.34 us -> 45.6 us  [swap(): lax.ppermute(value, axis, [(index, index ^ bit) for index in range(size)])]
    ppermute x5 -> x32, starting transfers between devices: 7.24 us -> 36.9 us  [swap(): lax.ppermute(value, axis, [(index, index ^ bit) for index in range(size)])]
    all_to_all x6 -> x1, starting transfers between devices: 32.6 us -> 8.32 us  [fetch_blocks(): lax.all_to_all(low_master.reshape(wide, -1, D), 'wide', 0, 0, tiled=True)]
    all_gather x1, waiting for transfers between devices: 19.1 us -> 0.01 us  [per_device(): lax.all_gather(low_master.reshape(-1, D), ('wide', 'narrow'), axis=0, til...]
    pallas_call x1 -> x3, Pallas kernels: 112 us -> 130 us  [back_call(): pl.pallas_call(functools.partial(back_kernel, first, last), grid_spec=plt...]
    all_to_all x1 -> x0, blocking collectives: 12.7 us -> none  [share_sums(): lax.all_to_all(grads.reshape(blocks, narrow, D // narrow, D), 'narrow', 1...]
  transfers between devices with their start and end apart: 12 -> 34, of which waited for: 8 -> 14; matrix products, arithmetic and copies ran while one was open for 5% -> 3% of each run, Pallas kernels for 4% -> 43%
where the time goes in v2:
time: 464 us; the launch traced here: 458 us
  Pallas kernels  317 us (68%)
  waiting for transfers between devices  45.6 us (10%)
  starting transfers between devices  45.2 us (10%)
  local copies, waits for them, and re-layouts  27.1 us (6%)
  between operations  15.3 us (3%)
  other arithmetic  8.33 us (2%)
    pallas_call x3, Pallas kernels, back_call(): pl.pallas_call(functools.partial(back_kernel, first, last), grid_spec=plt...  130 us
    pallas_call x1, Pallas kernels, ff_call(): pl.pallas_call(ff_kernel, grid_spec=pltpu.PrefetchScalarGridSpec(num_scal...  118 us
    ppermute x32, waiting for transfers between devices, swap(): lax.ppermute(value, axis, [(index, index ^ bit) for index in range(size)])  45.6 us
    pallas_call x1, Pallas kernels, attend_call(): pl.pallas_call(attend_kernel, grid_spec=pltpu.PrefetchScalarGridSpec(num_...  45 us
    ppermute x32, starting transfers between devices, swap(): lax.ppermute(value, axis, [(index, index ^ bit) for index in range(size)])  36.9 us
    pallas_call x1, Pallas kernels, last_call(): pl.pallas_call(last_kernel, grid=(images,), in_specs=[tile_spec(count, D)...  13 us
    unnamed x63, local copies, waits for them, and re-layouts  11.5 us
    pallas_call x1, Pallas kernels, norm_call(): pl.pallas_call(norm_kernel, grid=(images,), in_specs=[tile_spec(count, D)...  10 us
  transfers between devices with their start and end apart: 34, of which 14 were waited for; matrix products, arithmetic and copies ran while one was open for 3% of the time, Pallas kernels for 43%

profile of v2, /device:TPU:0, one launch (start us, length us, event | category | flops | bytes accessed | tf_op | source)
XLA Modules:
  0.0 458.4 jit_solution(1817832322767936960)
XLA Ops:
  7.2 1.8 convert_element_type.115
  9.0 8.3 %all-to-all-start = ((bf16[16,16,512]{2,1,0:T(8,128)(2,1)}), bf16[16,16,512]{2,1,0:T(8,128)(2,1)S(1)}, u32[]{:S(2)}, u32[]{:S(2)}) async-start(bf16[16,16,512]{2,1,0:T(8,128)(2,1)} %bitcast.174), calls=%async_computation | async-start | bytes 524288 | tf_op jit(solution)/shard_map/all_to_all | solution.py:512
  18.0 10.0 %norm_one.1 = (bf16[8,768,512]{2,1,0:T(8,128)(2,1)S(1)}, bf16[8,768,512]{2,1,0:T(8,128)(2,1)S(1)}, f32[8,4,512]{2,1,0:T(4,128)S(1)}, f32[1,512]{1,0:T(1,128)S(1)}) custom-call(bf16[8,768,512]{2,1,0:T(8,128)(2,1)} %x_ref.5, bf16[8,768,512]{2,1,0:T(8,128)(2,1)} %cot_ref.3, f32[1,512]{1,0:T(1,128)S(1)} %get-tuple-element.144.g_ref.refs_8_, ...), custom_call_target="tpu_custom_call" | custom-call | flops 62914560 | bytes 25165824 | tf_op jit(solution)/shard_map/norm_one/pallas_call | solution.py:98
  28.0 2.7 copy-done
  30.7 2.7 copy-done.6
  34.3 3.8 collective-permute-start.2
  38.8 2.7 collective-permute-done.2
  41.5 5.9 %collective-permute-done.1 = bf16[80,512]{1,0:T(8,128)(2,1)S(1)} collective-permute-done((bf16[80,512]{1,0:T(8,128)(2,1)S(1)}, bf16[80,512]{1,0:T(8,128)(2,1)S(1)}, u32[]{:S(2)}, u32[]{:S(2)}) %collective-permute-start.1) | collective-permute-done | bytes 81952 | tf_op jit(solution)/shard_map/ppermute | solution.py:490
  47.5 2.4 collective-permute-start.5
  51.1 8.2 %collective-permute-done.5 = bf16[4,80,512]{2,1,0:T(8,128)(2,1)S(1)} collective-permute-done((bf16[4,80,512]{2,1,0:T(8,128)(2,1)S(1)}, bf16[4,80,512]{2,1,0:T(8,128)(2,1)S(1)}, u32[]{:S(2)}, u32[]{:S(2)}) %collective-permute-start.5) | collective-permute-done | bytes 327712 | tf_op jit(solution)/shard_map/ppermute | solution.py:490
  59.3 4.0 collective-permute-done.4
  63.3 1.0 collective-permute-done.3
  65.3 1.0 slice_bitcast_fusion
  67.7 0.9 reshape.272.mean_ref.refs_7_
  70.0 1.3 copy.37
  71.3 45.0 %attend.1 = (bf16[8,768,512]{2,1,0:T(8,128)(2,1)}, bf16[8,768,512]{2,1,0:T(8,128)(2,1)}, bf16[8,768,512]{2,1,0:T(8,128)(2,1)}, bf16[8,4,8,192,256]{4,3,2,1,0:T(8...) custom-call(s32[1]{0:T(128)} %bitcast.first_row, bf16[8,768,512]{2,1,0:T(8,128)(2,1)} %copy-done.6, ...), custom_call_target="tpu_custom_call" | custom-call | flops 16106127360 | bytes 62914560 | tf_op jit(solution)/shard_map/attend/pallas_call | solution.py:169
  116.3 118.5 %feed_forward.1 = (bf16[8,768,512]{2,1,0:T(8,128)(2,1)}, bf16[8,768,512]{2,1,0:T(8,128)(2,1)}, bf16[8,768,512]{2,1,0:T(8,128)(2,1)}, bf16[9,512,512]{2,1,0:T(8,1...) custom-call(s32[12]{0:T(128)} %owner.7, bf16[8,768,512]{2,1,0:T(8,128)(2,1)} %x_ref.5, ...), custom_call_target="tpu_custom_call" | custom-call | flops 86973087744 | bytes 44040192 | tf_op jit(solution)/shard_map/feed_forward/pallas_call | solution.py:272
  234.8 3.3 dynamic-slice_bitcast_fusion
  238.2 33.8 %attend_back.3 = (bf16[8,768,512]{2,1,0:T(8,128)(2,1)}, bf16[2,64,512]{2,1,0:T(8,128)(2,1)}, f32[1536,512]{1,0:T(8,128)}, f32[1,512]{1,0:T(1,128)}, f32[1,512]{1,0:T(1,128)}) custom-call(s32[12]{0:T(128)} %owner.7, bf16[8,768,512]{2,1,0:T(8,128)(2,1)} %get-tuple-element.63.refs_0_, bf16[8,768,512]{2,1,0:T(8,128)(2,1)} %get-tuple-element.64.refs_1_, ...), custom_call_target="tpu_custom_call" | custom-call | flops 8053063680 | bytes 18874368 | tf_op jit(solution)/shard_map/attend_back/pallas_call | solution.py:416
  273.2 2.4 collective-permute-start.10
  276.7 60.4 %attend_back.4 = (bf16[8,768,512]{2,1,0:T(8,128)(2,1)}, bf16[4,64,512]{2,1,0:T(8,128)(2,1)}, f32[1536,512]{1,0:T(8,128)}, f32[1,512]{1,0:T(1,128)}, f32[1,512]{1,0:T(1,128)}) custom-call(s32[12]{0:T(128)} %owner.7, bf16[8,768,512]{2,1,0:T(8,128)(2,1)} %get-tuple-element.63.refs_0_, ...), custom_call_target="tpu_custom_call", output_to_operand_aliasing={{0}: (17, {})} | custom-call | flops 16106127360 | bytes 37748736 | tf_op jit(solution)/shard_map/attend_back/pallas_call | solution.py:416
  337.5 3.8 collective-permute-start.13
  342.0 36.2 %attend_back.5 = (bf16[8,768,512]{2,1,0:T(8,128)(2,1)}, bf16[2,64,512]{2,1,0:T(8,128)(2,1)}, f32[1536,512]{1,0:T(8,128)}, f32[1,512]{1,0:T(1,128)}, f32[1,512]{1,0:T(1,128)}, /*index=5*/bf16[3,512,512]{2,1,0:T(8,128)(2,1)}) custom-call(s32[12]{0:T(128)} %owner.7, bf16[8,768,512]{2,1,0:T(8,128)(2,1)} %get-tuple-element.63.refs_0_, ...), custom_call_target="tpu_custom_call", output_to_operand_aliasing={{0}: (17, {})} | custom-call | flops 8053063680 | bytes 18874368 | tf_op jit(solution)/shard_map/attend_back/pallas_call | solution.py:416
  378.4 2.1 dynamic-slice_bitcast_fusion.1
  381.6 1.4 collective-permute-done.14
  383.4 2.4 collective-permute-start.17
  386.2 0.8 collective-permute-start.15
  387.0 1.2 collective-permute-done.27
  388.2 1.3 collective-permute-start.28
  389.5 12.5 %collective-permute-done.28 = f32[1,4608]{1,0:T(1,128)S(1)} collective-permute-done((f32[1,4608]{1,0:T(1,128)S(1)}, f32[1,4608]{1,0:T(1,128)S(1)}, u32[]{:S(2)}, u32[]{:S(2)}) %collective-permute-start.28) | collective-permute-done | bytes 18464 | tf_op jit(solution)/shard_map/ppermute | solution.py:490
  402.3 3.6 collective-permute-done.29
  405.9 1.1 collective-permute-start.30
  407.2 2.5 collective-permute-start.20
  410.2 1.4 collective-permute-start.18
  412.5 2.1 collective-permute-start.31
  414.6 2.1 collective-permute-done.19
  416.8 1.0 scatter_fusion
  417.8 2.3 collective-permute-start.23
  420.1 2.1 collective-permute-start.21
  422.4 2.8 copy-done.1
  425.2 2.8 copy-done.2
  428.0 13.0 %norm_one_back.1 = f32[8,768,512]{2,1,0:T(8,128)} custom-call(bf16[8,768,512]{2,1,0:T(8,128)(2,1)S(1)} %copy-done.2, bf16[8,768,512]{2,1,0:T(8,128)(2,1)S(1)} %copy-done.1, bf16[8,768,512]{2,1,0:T(8,128)(2,1)} %get-tuple-element.97.dr_ref, f32[8,4,512]{2,1,0:T(4,128)S(1)} %reshape.284.dm_ref, f32[1,512]{1,0:T(1,128)S(1)} %copy-done.4), custom_call_target="tpu_custom_call" | custom-call | flops 62914560 | bytes 31457280 | tf_op jit(solution)/shard_map/norm_one_back/pallas_call | solution.py:467
  441.1 1.2 collective-permute-start.26
  442.2 1.3 collective-permute-start.25
  443.6 1.0 collective-permute-start.24
  445.3 1.1 collective-permute-done.26
  447.0 0.9 collective-permute-done.24
  448.6 2.5 fusion.10
  (170 shorter events, 16.8 us)
Async XLA Ops:
  7.2 10.2 %copy-start.15 = (f32[4608]{0:T(1024)S(1)}, f32[4608]{0:T(1024)}, u32[]{:S(2)}) copy-start(f32[4608]{0:T(1024)} %param.15) | copy-start | bytes 55300
  7.2 109.1 %all-gather.3.cloned.1.call-start = ((), (), s32[]{:S(2)}) async-start(), calls=%async_computation.1 | async-start | bytes 8650752 | tf_op jit(solution)/shard_map/all_gather | solution.py:598
  9.0 24.6 %all-to-all-start = ((bf16[16,16,512]{2,1,0:T(8,128)(2,1)}), bf16[16,16,512]{2,1,0:T(8,128)(2,1)S(1)}, u32[]{:S(2)}, u32[]{:S(2)}) async-start(bf16[16,16,512]{2,1,0:T(8,128)(2,1)} %bitcast.174), calls=%async_computation | async-start | bytes 524288 | tf_op jit(solution)/shard_map/all_to_all | solution.py:512
  18.0 10.0 %copy-start.3 = (f32[1,512]{1,0:T(1,128)}, f32[1,512]{1,0:T(1,128)S(1)}, u32[]{:S(2)}) copy-start(f32[1,512]{1,0:T(1,128)S(1)} %get-tuple-element.144.g_ref.refs_8_) | copy-start | bytes 6148
  18.0 10.0 %copy-start.5 = (f32[1,512]{1,0:T(1,128)}, f32[1,512]{1,0:T(1,128)S(1)}, u32[]{:S(2)}) copy-start(f32[1,512]{1,0:T(1,128)S(1)} %get-tuple-element.143.s_ref.refs_9_) | copy-start | bytes 6148
  18.0 15.5 %copy-start.21 = (s32[12]{0:T(128)S(1)}, s32[12]{0:T(128)}, u32[]{:S(2)}) copy-start(s32[12]{0:T(128)} %owner.7) | copy-start | bytes 148
  34.3 7.2 %collective-permute-start.2 = (bf16[80,512]{1,0:T(8,128)(2,1)S(1)}, bf16[80,512]{1,0:T(8,128)(2,1)S(1)}, u32[]{:S(2)}, u32[]{:S(2)}) collective-permute-start(bf16[80,512]{1,0:T(8,128)(2,1)S(1)} %get-tuple-element.139), channel_id=1, source_target_pairs={{0,24},{2,26},{4,28},{6,30},{8,16},{10,18},{12,20},{14,22},{16,8},... | collective-permute-start | bytes 245768 | tf_op jit(solution)/shard_map/ppermute | solution.py:490
  38.1 9.3 %collective-permute-start.1 = (bf16[80,512]{1,0:T(8,128)(2,1)S(1)}, bf16[80,512]{1,0:T(8,128)(2,1)S(1)}, u32[]{:S(2)}, u32[]{:S(2)}) collective-permute-start(bf16[80,512]{1,0:T(8,128)(2,1)S(1)} %get-tuple-element.139), channel_id=1, source_target_pairs={{0,16},{2,18},{4,20},{6,22},{8,24},{10,26},{12,28},{14,30},{16,0},... | collective-permute-start | bytes 245768 | tf_op jit(solution)/shard_map/ppermute | solution.py:490
  38.1 9.3 %collective-permute-start = (bf16[80,512]{1,0:T(8,128)(2,1)S(1)}, bf16[80,512]{1,0:T(8,128)(2,1)S(1)}, u32[]{:S(2)}, u32[]{:S(2)}) collective-permute-start(bf16[80,512]{1,0:T(8,128)(2,1)S(1)} %get-tuple-element.139), channel_id=1, source_target_pairs={{0,8},{2,10},{4,12},{6,14},{8,0},{10,2},{12,4},{14,6},{16,24},{18,... | collective-permute-start | bytes 245768 | tf_op jit(solution)/shard_map/ppermute | solution.py:490
  47.5 11.8 %collective-permute-start.5 = (bf16[4,80,512]{2,1,0:T(8,128)(2,1)S(1)}, bf16[4,80,512]{2,1,0:T(8,128)(2,1)S(1)}, u32[]{:S(2)}, u32[]{:S(2)}) collective-permute-start(bf16[4,80,512]{2,1,0:T(8,128)(2,1)S(1)} %get-tuple-element.129), channel_id=1, source_target_pairs={{0,6},{2,4},{4,2},{6,0},{8,14},{10,12},{12,10},{14,8},{16,22},{18,... | collective-permute-start | bytes 983048 | tf_op jit(solution)/shard_map/ppermute | solution.py:490
  49.9 13.3 %collective-permute-start.4 = (bf16[4,80,512]{2,1,0:T(8,128)(2,1)S(1)}, bf16[4,80,512]{2,1,0:T(8,128)(2,1)S(1)}, u32[]{:S(2)}, u32[]{:S(2)}) collective-permute-start(bf16[4,80,512]{2,1,0:T(8,128)(2,1)S(1)} %get-tuple-element.129), channel_id=1, source_target_pairs={{0,4},{2,6},{4,0},{6,2},{8,12},{10,14},{12,8},{14,10},{16,20},{18,... | collective-permute-start | bytes 983048 | tf_op jit(solution)/shard_map/ppermute | solution.py:490
  50.5 13.7 %collective-permute-start.3 = (bf16[4,80,512]{2,1,0:T(8,128)(2,1)S(1)}, bf16[4,80,512]{2,1,0:T(8,128)(2,1)S(1)}, u32[]{:S(2)}, u32[]{:S(2)}) collective-permute-start(bf16[4,80,512]{2,1,0:T(8,128)(2,1)S(1)} %get-tuple-element.129), channel_id=1, source_target_pairs={{0,2},{2,0},{4,6},{6,4},{8,10},{10,8},{12,14},{14,12},{16,18},{18,... | collective-permute-start | bytes 983048 | tf_op jit(solution)/shard_map/ppermute | solution.py:490
  51.1 14.0 %copy-start.27 = (pred[16]{0:T(512)(128)(4,1)}, pred[16]{0:T(512)(128)(4,1)S(1)}, u32[]{:S(2)}) copy-start(pred[16]{0:T(512)(128)(4,1)S(1)} %compare_and_fusion.2) | copy-start | bytes 52
  51.1 14.0 %copy-start.20 = (s32[1024]{0:T(1024)}, s32[1024]{0:T(1024)S(1)}, u32[]{:S(2)}) copy-start(s32[1024]{0:T(1024)S(1)} %pad_clamp_fusion.1) | copy-start | bytes 12292
  66.3 2.7 collective-permute-start.6
  238.1 34.0 %collective-permute-start.7 = (bf16[9,256,512]{2,1,0:T(8,128)(2,1)}, bf16[9,256,512]{2,1,0:T(8,128)(2,1)S(1)}, u32[]{:S(2)}, u32[]{:S(2)}) collective-permute-start(bf16[9,256,512]{2,1,0:T(8,128)(2,1)} %dynamic-slice_bitcast_fusion), channel_id=1, source_target_pairs={{0,1},{1,0},{2,3},{3,2},{4,5},{5,4},{6,7},{7,6},{8,9},{9,8},{10,11... | collective-permute-start | bytes 7077896 | tf_op jit(solution)/shard_map/ppermute | solution.py:490
  238.2 33.9 %copy-start.7 = (bf16[9,512,512]{2,1,0:T(8,128)(2,1)S(1)}, bf16[9,512,512]{2,1,0:T(8,128)(2,1)}, u32[]{:S(2)}) copy-start(bf16[9,512,512]{2,1,0:T(8,128)(2,1)} %get-tuple-element.62) | copy-start | bytes 14155780
  273.2 63.9 %collective-permute-start.10 = (bf16[4,144,512]{2,1,0:T(8,128)(2,1)S(1)}, bf16[4,144,512]{2,1,0:T(8,128)(2,1)S(1)}, u32[]{:S(2)}, u32[]{:S(2)}) collective-permute-start(bf16[4,144,512]{2,1,0:T(8,128)(2,1)S(1)} %get-tuple-element.112), channel_id=1, source_target_pairs={{0,6},{2,4},{4,2},{6,0},{8,14},{10,12},{12,10},{14,8},{16,22},{18,... | collective-permute-start | bytes 1769480 | tf_op jit(solution)/shard_map/ppermute | solution.py:490
  275.6 61.5 %collective-permute-start.9 = (bf16[4,144,512]{2,1,0:T(8,128)(2,1)S(1)}, bf16[4,144,512]{2,1,0:T(8,128)(2,1)S(1)}, u32[]{:S(2)}, u32[]{:S(2)}) collective-permute-start(bf16[4,144,512]{2,1,0:T(8,128)(2,1)S(1)} %get-tuple-element.113), channel_id=1, source_target_pairs={{0,4},{2,6},{4,0},{6,2},{8,12},{10,14},{12,8},{14,10},{16,20},{18,... | collective-permute-start | bytes 1769480 | tf_op jit(solution)/shard_map/ppermute | solution.py:490
  275.9 61.2 %collective-permute-start.8 = (bf16[4,144,512]{2,1,0:T(8,128)(2,1)S(1)}, bf16[4,144,512]{2,1,0:T(8,128)(2,1)S(1)}, u32[]{:S(2)}, u32[]{:S(2)}) collective-permute-start(bf16[4,144,512]{2,1,0:T(8,128)(2,1)S(1)} %get-tuple-element.111), channel_id=1, source_target_pairs={{0,2},{2,0},{4,6},{6,4},{8,10},{10,8},{12,14},{14,12},{16,18},{18,... | collective-permute-start | bytes 1769480 | tf_op jit(solution)/shard_map/ppermute | solution.py:490
  337.5 40.7 %collective-permute-start.13 = (bf16[144,512]{1,0:T(8,128)(2,1)S(1)}, bf16[144,512]{1,0:T(8,128)(2,1)S(1)}, u32[]{:S(2)}, u32[]{:S(2)}) collective-permute-start(bf16[144,512]{1,0:T(8,128)(2,1)S(1)} %get-tuple-element.123), channel_id=1, source_target_pairs={{0,24},{2,26},{4,28},{6,30},{8,16},{10,18},{12,20},{14,22},{16,8},... | collective-permute-start | bytes 442376 | tf_op jit(solution)/shard_map/ppermute | solution.py:490
  341.3 36.9 %collective-permute-start.12 = (bf16[144,512]{1,0:T(8,128)(2,1)S(1)}, bf16[144,512]{1,0:T(8,128)(2,1)S(1)}, u32[]{:S(2)}, u32[]{:S(2)}) collective-permute-start(bf16[144,512]{1,0:T(8,128)(2,1)S(1)} %get-tuple-element.124), channel_id=1, source_target_pairs={{0,16},{2,18},{4,20},{6,22},{8,24},{10,26},{12,28},{14,30},{16,0},... | collective-permute-start | bytes 442376 | tf_op jit(solution)/shard_map/ppermute | solution.py:490
  341.3 37.0 %collective-permute-start.11 = (bf16[144,512]{1,0:T(8,128)(2,1)S(1)}, bf16[144,512]{1,0:T(8,128)(2,1)S(1)}, u32[]{:S(2)}, u32[]{:S(2)}) collective-permute-start(bf16[144,512]{1,0:T(8,128)(2,1)S(1)} %get-tuple-element.122), channel_id=1, source_target_pairs={{0,8},{2,10},{4,12},{6,14},{8,0},{10,2},{12,4},{14,6},{16,24},{18,... | collective-permute-start | bytes 442376 | tf_op jit(solution)/shard_map/ppermute | solution.py:490
  380.4 2.5 collective-permute-start.14
  383.3 18.9 %copy-start.22 = (s32[12]{0:T(128)S(1)}, s32[12]{0:T(128)}, u32[]{:S(2)}) copy-start(s32[12]{0:T(128)} %owner.7) | copy-start | bytes 148
  383.4 28.9 %copy-start.28 = (pred[16]{0:T(512)(128)(4,1)S(1)}, pred[16]{0:T(512)(128)(4,1)}, u32[]{:S(2)}) copy-start(pred[16]{0:T(512)(128)(4,1)} %copy-done.27) | copy-start | bytes 52
  383.4 23.5 %collective-permute-start.17 = (bf16[4,80,512]{2,1,0:T(8,128)(2,1)S(1)}, bf16[4,80,512]{2,1,0:T(8,128)(2,1)S(1)}, u32[]{:S(2)}, u32[]{:S(2)}) collective-permute-start(bf16[4,80,512]{2,1,0:T(8,128)(2,1)S(1)} %get-tuple-element.116), channel_id=1, source_target_pairs={{0,6},{2,4},{4,2},{6,0},{8,14},{10,12},{12,10},{14,8},{16,22},{18,... | collective-permute-start | bytes 983048 | tf_op jit(solution)/shard_map/ppermute | solution.py:490
  385.9 21.1 %collective-permute-start.16 = (bf16[4,80,512]{2,1,0:T(8,128)(2,1)S(1)}, bf16[4,80,512]{2,1,0:T(8,128)(2,1)S(1)}, u32[]{:S(2)}, u32[]{:S(2)}) collective-permute-start(bf16[4,80,512]{2,1,0:T(8,128)(2,1)S(1)} %get-tuple-element.115), channel_id=1, source_target_pairs={{0,4},{2,6},{4,0},{6,2},{8,12},{10,14},{12,8},{14,10},{16,20},{18,... | collective-permute-start | bytes 983048 | tf_op jit(solution)/shard_map/ppermute | solution.py:490
  386.2 20.8 %collective-permute-start.15 = (bf16[4,80,512]{2,1,0:T(8,128)(2,1)S(1)}, bf16[4,80,512]{2,1,0:T(8,128)(2,1)S(1)}, u32[]{:S(2)}, u32[]{:S(2)}) collective-permute-start(bf16[4,80,512]{2,1,0:T(8,128)(2,1)S(1)} %get-tuple-element.114), channel_id=1, source_target_pairs={{0,2},{2,0},{4,6},{6,4},{8,10},{10,8},{12,14},{14,12},{16,18},{18,... | collective-permute-start | bytes 983048 | tf_op jit(solution)/shard_map/ppermute | solution.py:490
  387.0 1.2 collective-permute-start.27
  388.2 13.8 %collective-permute-start.28 = (f32[1,4608]{1,0:T(1,128)S(1)}, f32[1,4608]{1,0:T(1,128)S(1)}, u32[]{:S(2)}, u32[]{:S(2)}) collective-permute-start(f32[1,4608]{1,0:T(1,128)S(1)} %add.242), channel_id=1, source_target_pairs={{0,2},{2,0},{4,6},{6,4},{8,10},{10,8},{12,14},{14,12},{16,18},{18,... | collective-permute-start | bytes 55304 | tf_op jit(solution)/shard_map/ppermute | solution.py:490
  402.0 3.8 collective-permute-start.29
  405.9 6.6 %collective-permute-start.30 = (f32[1,4608]{1,0:T(1,128)S(1)}, f32[1,4608]{1,0:T(1,128)S(1)}, u32[]{:S(2)}, u32[]{:S(2)}) collective-permute-start(f32[1,4608]{1,0:T(1,128)S(1)} %add.244), channel_id=1, source_target_pairs={{0,8},{2,10},{4,12},{6,14},{8,0},{10,2},{12,4},{14,6},{16,24},{18,... | collective-permute-start | bytes 55304 | tf_op jit(solution)/shard_map/ppermute | solution.py:490
  407.1 15.3 %copy-start.4 = (f32[1,512]{1,0:T(1,128)S(1)}, f32[1,512]{1,0:T(1,128)}, u32[]{:S(2)}) copy-start(f32[1,512]{1,0:T(1,128)} %copy-done.3) | copy-start | bytes 6148
  407.2 7.4 %collective-permute-start.20 = (bf16[80,512]{1,0:T(8,128)(2,1)S(1)}, bf16[80,512]{1,0:T(8,128)(2,1)S(1)}, u32[]{:S(2)}, u32[]{:S(2)}) collective-permute-start(bf16[80,512]{1,0:T(8,128)(2,1)S(1)} %get-tuple-element.126), channel_id=1, source_target_pairs={{0,24},{2,26},{4,28},{6,30},{8,16},{10,18},{12,20},{14,22},{16,8},... | collective-permute-start | bytes 245768 | tf_op jit(solution)/shard_map/ppermute | solution.py:490
  409.6 7.1 %collective-permute-start.19 = (bf16[80,512]{1,0:T(8,128)(2,1)S(1)}, bf16[80,512]{1,0:T(8,128)(2,1)S(1)}, u32[]{:S(2)}, u32[]{:S(2)}) collective-permute-start(bf16[80,512]{1,0:T(8,128)(2,1)S(1)} %get-tuple-element.127), channel_id=1, source_target_pairs={{0,16},{2,18},{4,20},{6,22},{8,24},{10,26},{12,28},{14,30},{16,0},... | collective-permute-start | bytes 245768 | tf_op jit(solution)/shard_map/ppermute | solution.py:490
  410.2 6.5 %collective-permute-start.18 = (bf16[80,512]{1,0:T(8,128)(2,1)S(1)}, bf16[80,512]{1,0:T(8,128)(2,1)S(1)}, u32[]{:S(2)}, u32[]{:S(2)}) collective-permute-start(bf16[80,512]{1,0:T(8,128)(2,1)S(1)} %get-tuple-element.125), channel_id=1, source_target_pairs={{0,8},{2,10},{4,12},{6,14},{8,0},{10,2},{12,4},{14,6},{16,24},{18,... | collective-permute-start | bytes 245768 | tf_op jit(solution)/shard_map/ppermute | solution.py:490
  412.5 9.8 %collective-permute-start.31 = (f32[1,4608]{1,0:T(1,128)S(1)}, f32[1,4608]{1,0:T(1,128)S(1)}, u32[]{:S(2)}, u32[]{:S(2)}) collective-permute-start(f32[1,4608]{1,0:T(1,128)S(1)} %add.245), channel_id=1, source_target_pairs={{0,16},{2,18},{4,20},{6,22},{8,24},{10,26},{12,28},{14,30},{16,0},... | collective-permute-start | bytes 55304 | tf_op jit(solution)/shard_map/ppermute | solution.py:490
  417.8 23.1 %collective-permute-start.23 = (bf16[4,16,512]{2,1,0:T(8,128)(2,1)S(1)}, bf16[4,16,512]{2,1,0:T(8,128)(2,1)S(1)}, u32[]{:S(2)}, u32[]{:S(2)}) collective-permute-start(bf16[4,16,512]{2,1,0:T(8,128)(2,1)S(1)} %get-tuple-element.135), channel_id=1, source_target_pairs={{0,24},{2,26},{4,28},{6,30},{8,16},{10,18},{12,20},{14,22},{16,8},... | collective-permute-start | bytes 196616 | tf_op jit(solution)/shard_map/ppermute | solution.py:490
  420.1 20.8 %collective-permute-start.22 = (bf16[4,16,512]{2,1,0:T(8,128)(2,1)S(1)}, bf16[4,16,512]{2,1,0:T(8,128)(2,1)S(1)}, u32[]{:S(2)}, u32[]{:S(2)}) collective-permute-start(bf16[4,16,512]{2,1,0:T(8,128)(2,1)S(1)} %get-tuple-element.136), channel_id=1, source_target_pairs={{0,16},{2,18},{4,20},{6,22},{8,24},{10,26},{12,28},{14,30},{16,0},... | collective-permute-start | bytes 196616 | tf_op jit(solution)/shard_map/ppermute | solution.py:490
  420.1 20.8 %collective-permute-start.21 = (bf16[4,16,512]{2,1,0:T(8,128)(2,1)S(1)}, bf16[4,16,512]{2,1,0:T(8,128)(2,1)S(1)}, u32[]{:S(2)}, u32[]{:S(2)}) collective-permute-start(bf16[4,16,512]{2,1,0:T(8,128)(2,1)S(1)} %get-tuple-element.137), channel_id=1, source_target_pairs={{0,8},{2,10},{4,12},{6,14},{8,0},{10,2},{12,4},{14,6},{16,24},{18,... | collective-permute-start | bytes 196616 | tf_op jit(solution)/shard_map/ppermute | solution.py:490
  428.0 16.6 %copy-start.16 = (f32[4608]{0:T(1024)S(1)}, f32[4608]{0:T(1024)}, u32[]{:S(2)}) copy-start(f32[4608]{0:T(1024)} %param.15) | copy-start | bytes 55300
  428.0 16.6 %copy-start.17 = (f32[4608]{0:T(1024)S(1)}, f32[4608]{0:T(1024)}, u32[]{:S(2)}) copy-start(f32[4608]{0:T(1024)} %param.16) | copy-start | bytes 55300
  428.0 16.6 %copy-start.18 = (f32[4608]{0:T(1024)S(1)}, f32[4608]{0:T(1024)}, u32[]{:S(2)}) copy-start(f32[4608]{0:T(1024)} %param.17) | copy-start | bytes 55300
  441.0 7.7 %copy-start.11 = (f32[1,256,512]{2,1,0:T(8,128)S(1)}, f32[1,256,512]{2,1,0:T(8,128)}, u32[]{:S(2)}) copy-start(f32[1,256,512]{2,1,0:T(8,128)} %param.13) | copy-start | bytes 1572868
  441.1 5.3 %collective-permute-start.26 = (bf16[4,16,512]{2,1,0:T(8,128)(2,1)S(1)}, bf16[4,16,512]{2,1,0:T(8,128)(2,1)S(1)}, u32[]{:S(2)}, u32[]{:S(2)}) collective-permute-start(bf16[4,16,512]{2,1,0:T(8,128)(2,1)S(1)} %get-tuple-element.131), channel_id=1, source_target_pairs={{0,6},{2,4},{4,2},{6,0},{8,14},{10,12},{12,10},{14,8},{16,22},{18,... | collective-permute-start | bytes 196616 | tf_op jit(solution)/shard_map/ppermute | solution.py:490
  442.2 4.7 %collective-permute-start.25 = (bf16[4,16,512]{2,1,0:T(8,128)(2,1)S(1)}, bf16[4,16,512]{2,1,0:T(8,128)(2,1)S(1)}, u32[]{:S(2)}, u32[]{:S(2)}) collective-permute-start(bf16[4,16,512]{2,1,0:T(8,128)(2,1)S(1)} %get-tuple-element.132), channel_id=1, source_target_pairs={{0,4},{2,6},{4,0},{6,2},{8,12},{10,14},{12,8},{14,10},{16,20},{18,... | collective-permute-start | bytes 196616 | tf_op jit(solution)/shard_map/ppermute | solution.py:490
  443.6 4.3 collective-permute-start.24
  (15 other events, 39.5 us)
Sparse Core Ops, SparseCore 0:
  11.4 83.3 all-gather.2

commit v3 on v1

v3 whole, which is shorter than its diff:
```python
import functools
import functools
import math

import jax
import jax.numpy as jnp
from jax import lax
from jax.experimental import pallas as pl
from jax.experimental.pallas import tpu as pltpu
from jax.sharding import PartitionSpec as P

D = 512
HEADS = 8
HD = 64
PAIR = 2 * HD
PAIRS = HEADS // 2
FF = 2048
NF = FF // D
ROW = 192
ROWS_IMG = 64
KEYS = ROW + ROWS_IMG
STEP = 10
RATE = 0.03
GAIN_RATE = 0.4
EPS = 1e-05
LOG2E = math.log2(math.e)
F32 = jnp.float32
BF16 = jnp.bfloat16
MIB = 1024 * 1024


def dot(left, right):
    return jnp.dot(left, right, preferred_element_type=F32)


def dot_nt(left, right):
    return lax.dot_general(left, right, (((1,), (1,)), ((), ())), preferred_element_type=F32)


def normalize(values):
    centred = values - jnp.mean(values, -1, keepdims=True)
    scale = lax.rsqrt(jnp.mean(centred * centred, -1, keepdims=True) + EPS)
    return centred * scale, scale


def head_masks(dtype):
    lane = lax.broadcasted_iota(jnp.int32, (1, PAIR), 1)
    first = (lane < HD).astype(F32)
    return first.astype(dtype), (1.0 - first).astype(dtype)


def tile_spec(*tail, buffers=None):
    zeros = (0,) * len(tail)
    return pl.BlockSpec((1,) + tail, lambda step, *_: (step,) + zeros)


def whole_spec(shape):
    zeros = (0,) * len(shape)
    return pl.BlockSpec(shape, lambda step, *_: zeros, pipeline_mode=pl.Buffered(1))


def weight_spec(block):
    return pl.BlockSpec(
        (1, D, D), lambda step, owner, *_: (owner[block], 0, 0), pipeline_mode=pl.Buffered(1)
    )


def out_whole(shape):
    zeros = (0,) * len(shape)
    return pl.BlockSpec(shape, lambda step, *_: zeros)


def norm_kernel(x_ref, xh_ref, mean_ref):
    normal, _ = normalize(x_ref[0].astype(F32))
    xh_ref[0] = normal.astype(BF16)
    for row in range(mean_ref.shape[1]):
        part = normal[row * ROW : (row + 1) * ROW]
        mean_ref[0, row : row + 1, :] = jnp.mean(part, 0, keepdims=True)


def norm_call(tokens):
    images, count, _ = tokens.shape
    rows = count // ROW
    return pl.pallas_call(
        norm_kernel,
        grid=(images,),
        in_specs=[tile_spec(count, D)],
        out_specs=[tile_spec(count, D), tile_spec(rows, D)],
        out_shape=[
            jax.ShapeDtypeStruct((images, count, D), BF16),
            jax.ShapeDtypeStruct((images, rows, D), F32),
        ],
        compiler_params=pltpu.CompilerParams(vmem_limit_bytes=60 * MIB),
        cost_estimate=pl.CostEstimate(
            flops=images * count * D * 10, bytes_accessed=images * count * D * 4, transcendentals=0
        ),
        name="norm_one",
    )(tokens)


def group_sizes(wide):
    inner = min(4, wide)
    return inner, wide // inner


def write_pieces(place, out_refs, read):
    narrow = len(out_refs)
    inner, outer, height, _ = out_refs[0].shape
    depth = D // narrow // (inner * outer)

    def one(distance, carry):
        for step, out_ref in enumerate(out_refs):
            start = (place[1] ^ step) * (D // narrow) + (place[0] ^ distance) * depth
            here = pl.ds(pl.multiple_of(start, depth), depth)
            for block in range(height // depth):
                value = read(block, here).astype(BF16)
                out_ref[distance % inner, distance // inner, block * depth : (block + 1) * depth, :] = value
        return carry

    lax.fori_loop(0, inner * outer, one, 0)


def attend_kernel(
    parts, place, xh_ref, mean_ref, g_ref, s_ref, *refs
):
    part_refs, refs = refs[:parts], refs[parts:]
    q_ref, k_ref, v_ref, e_ref, o_ref, li_ref, sk_ref, sv_ref, bias_ref, w_ref = refs
    rows = xh_ref.shape[1] // ROW
    first_row = place[0] * rows

    @pl.when(pl.program_id(0) == 0)
    def _():
        query = lax.broadcasted_iota(jnp.int32, (ROW, KEYS), 0)
        key = lax.broadcasted_iota(jnp.int32, (ROW, KEYS), 1)
        for row in range(rows):
            own = jnp.where(key <= query, 0.0, -1e30)
            earlier = jnp.where(key - ROW < first_row + row, math.log2(ROW), -1e30)
            bias_ref[row] = jnp.where(key < ROW, own, earlier)
        if parts == 1:
            w_ref[...] = part_refs[0][...]
            return
        wide, height, _ = part_refs[0].shape
        depth = D // parts // wide

        def one(distance, carry):
            for step, part_ref in enumerate(part_refs):
                start = (place[1] ^ step) * (D // parts) + (place[0] ^ distance) * depth
                here = pl.ds(pl.multiple_of(start, depth), depth)
                for block in range(3):
                    w_ref[block, here, :] = part_ref[distance, block * depth : (block + 1) * depth, :]
            return carry

        lax.fori_loop(0, wide, one, 0)

    a1 = (xh_ref[0].astype(F32) * g_ref[...] + s_ref[...]).astype(BF16)
    q_ref[0] = dot(a1, w_ref[0]).astype(BF16)
    k_ref[0] = dot(a1, w_ref[1]).astype(BF16)
    v_ref[0] = dot(a1, w_ref[2]).astype(BF16)
    mean_a = (mean_ref[0].astype(F32) * g_ref[...] + s_ref[...]).astype(BF16)
    sum_k = dot(mean_a, w_ref[1]).astype(BF16)
    sum_v = dot(mean_a, w_ref[2]).astype(BF16)
    sk_ref[0] = sum_k
    sv_ref[0] = sum_v
    masks = head_masks(BF16)
    ones = [jnp.broadcast_to(mask, (KEYS, PAIR)) for mask in masks]
    scale = LOG2E / math.sqrt(HD)

    for row in range(rows):
        here = slice(row * ROW, (row + 1) * ROW)
        for pair in range(PAIRS):
            lanes = slice(pair * PAIR, (pair + 1) * PAIR)
            query = q_ref[0, here, lanes]
            keys = jnp.concatenate([k_ref[0, here, lanes], sum_k[:, lanes]], 0)
            values = jnp.concatenate([v_ref[0, here, lanes], sum_v[:, lanes]], 0)
            total = None
            for half in range(2):
                score = dot_nt(query, keys * masks[half]) * scale + bias_ref[row]
                weight = jnp.exp2(score - jnp.max(score, -1, keepdims=True)).astype(BF16)
                e_ref[0, row, 2 * pair + half] = weight
                part = dot(weight, jnp.concatenate([values * masks[half], ones[half]], 1))
                total = part if total is None else total + part
            inverse = 1.0 / total[:, PAIR:]
            o_ref[0, here, lanes] = (total[:, :PAIR] * inverse).astype(BF16)
            li_ref[0, here, lanes] = inverse.astype(BF16)


def attend_call(place, normal, mean_all, gain, shift, parts):
    images, count, _ = normal.shape
    rows = count // ROW
    tokens_shape = jax.ShapeDtypeStruct((images, count, D), BF16)
    return pl.pallas_call(
        functools.partial(attend_kernel, len(parts)),
        grid_spec=pltpu.PrefetchScalarGridSpec(
            num_scalar_prefetch=1,
            grid=(images,),
            in_specs=[
                tile_spec(count, D), tile_spec(ROWS_IMG, D), whole_spec((1, D)), whole_spec((1, D)),
            ]
            + [whole_spec(part.shape) for part in parts],
            out_specs=[tile_spec(count, D)] * 3
            + [tile_spec(rows, HEADS, ROW, KEYS)]
            + [tile_spec(count, D)] * 2
            + [tile_spec(ROWS_IMG, D)] * 2,
            scratch_shapes=[
                pltpu.VMEM((rows, ROW, KEYS), F32),
                pltpu.VMEM((3, D, D), BF16),
            ],
        ),
        out_shape=[tokens_shape] * 3
        + [jax.ShapeDtypeStruct((images, rows, HEADS, ROW, KEYS), BF16)]
        + [tokens_shape] * 2
        + [jax.ShapeDtypeStruct((images, ROWS_IMG, D), BF16)] * 2,
        compiler_params=pltpu.CompilerParams(vmem_limit_bytes=60 * MIB),
        cost_estimate=pl.CostEstimate(
            flops=images * count * D * D * 10, bytes_accessed=images * count * D * 20, transcendentals=0
        ),
        name="attend",
    )(place, normal, mean_all, gain, shift, *parts)


def ff_kernel(
    pieces, owner, place, x_ref, o_ref, cot_ref, li_ref, g_ref, s_ref, bu_ref,
    wo_ref, u0_ref, u1_ref, u2_ref, u3_ref, d0_ref, d1_ref, d2_ref, d3_ref,
    act_ref, h_ref, dr_ref, do_ref, gg_ref, gs_ref, gbu_ref, gbd_ref, *refs
):
    grads_refs, (acc_ref, xh_ref, da_ref) = refs[:-3], refs[-3:]
    step = pl.program_id(0)
    ups = (u0_ref, u1_ref, u2_ref, u3_ref)
    downs = (d0_ref, d1_ref, d2_ref, d3_ref)

    @pl.when(step == 0)
    def _():
        acc_ref[...] = jnp.zeros_like(acc_ref)
        gg_ref[...] = jnp.zeros_like(gg_ref)
        gs_ref[...] = jnp.zeros_like(gs_ref)
        gbu_ref[...] = jnp.zeros_like(gbu_ref)
        gbd_ref[...] = jnp.zeros_like(gbd_ref)

    hidden = x_ref[0].astype(F32) + dot(o_ref[0], wo_ref[0])
    normal, spread = normalize(hidden)
    xh_ref[...] = normal
    h_ref[0] = hidden.astype(BF16)
    a2 = (normal * g_ref[...] + s_ref[...]).astype(BF16)
    a2_t = a2.T
    cot = cot_ref[0]
    cot_t = cot.T
    c_one = math.sqrt(2.0 / math.pi)
    c_two = c_one * 0.044715
    for block in range(NF):
        w_up = ups[block][0]
        w_down = downs[block][0]
        pre = dot(a2, w_up) + bu_ref[:, block * D : (block + 1) * D]
        d_act = dot_nt(cot, w_down)
        square = pre * pre
        half = 0.5 + 0.5 * jnp.tanh(pre * (c_one + c_two * square))
        act = pre * half
        slope = half + act * (1.0 - half) * (2.0 * c_one + (6.0 * c_two) * square)
        act = act.astype(BF16)
        d_pre = d_act * slope
        gbu_ref[:, block * D : (block + 1) * D] += jnp.sum(d_pre, 0, keepdims=True)
        d_pre = d_pre.astype(BF16)
        act_ref[0, :, block * D : (block + 1) * D] = act
        part = dot_nt(d_pre, w_up)
        if block == 0:
            da_ref[...] = part
        else:
            da_ref[...] += part
        acc_ref[1 + block] += dot(a2_t, d_pre)
        acc_ref[1 + NF + block] += dot(cot_t, act)
    d_a2 = da_ref[...]
    normal = xh_ref[...]
    gs_ref[...] += jnp.sum(d_a2, 0, keepdims=True)
    gg_ref[...] += jnp.sum(d_a2 * normal, 0, keepdims=True)
    d_normal = d_a2 * g_ref[...]
    middle = jnp.mean(d_normal, -1, keepdims=True)
    along = jnp.mean(d_normal * normal, -1, keepdims=True)
    cot = cot.astype(F32)
    gbd_ref[...] += jnp.sum(cot, 0, keepdims=True)
    d_hidden = cot + spread * (d_normal - middle - normal * along)
    branch = d_hidden.astype(BF16)
    dr_ref[0] = branch
    acc_ref[0] += dot(o_ref[0].T, branch)
    do_ref[0] = (dot_nt(branch, wo_ref[0]) * li_ref[0].astype(F32)).astype(BF16)

    @pl.when(step == pl.num_programs(0) - 1)
    def _():
        for block in range(1 + NF, 1 + 2 * NF):
            acc_ref[block] = acc_ref[block].T
        if pieces:
            write_pieces(place, grads_refs, lambda block, here: acc_ref[block, here, :])
        else:
            grads_refs[0][...] = acc_ref[...].astype(BF16)


def grad_shapes(groups, blocks):
    if groups is None:
        return [(blocks, D, D)]
    narrow, inner, outer = groups
    return [(inner, outer, blocks * (D // narrow // inner // outer), D)] * narrow


def ff_call(owner, place, groups, tokens, attended, cotangent, inverse, gain, shift, bias_up, slots):
    images, count, _ = tokens.shape
    tokens_shape = jax.ShapeDtypeStruct((images, count, D), BF16)
    blocks = 1 + 2 * NF
    grads = grad_shapes(groups, blocks)
    return pl.pallas_call(
        functools.partial(ff_kernel, groups is not None),
        grid_spec=pltpu.PrefetchScalarGridSpec(
            num_scalar_prefetch=2,
            grid=(images,),
            in_specs=[tile_spec(count, D)] * 4
            + [whole_spec((1, D)), whole_spec((1, D)), whole_spec((1, FF))]
            + [weight_spec(3 + block) for block in range(blocks)],
            out_specs=[tile_spec(count, FF)]
            + [tile_spec(count, D)] * 3
            + [out_whole((1, D)), out_whole((1, D)), out_whole((1, FF)), out_whole((1, D))]
            + [out_whole(shape) for shape in grads],
            scratch_shapes=[
                pltpu.VMEM((blocks, D, D), F32),
                pltpu.VMEM((count, D), F32),
                pltpu.VMEM((count, D), F32),
            ],
        ),
        out_shape=[jax.ShapeDtypeStruct((images, count, FF), BF16)]
        + [tokens_shape] * 3
        + [
            jax.ShapeDtypeStruct((1, D), F32),
            jax.ShapeDtypeStruct((1, D), F32),
            jax.ShapeDtypeStruct((1, FF), F32),
            jax.ShapeDtypeStruct((1, D), F32),
        ]
        + [jax.ShapeDtypeStruct(shape, BF16) for shape in grads],
        compiler_params=pltpu.CompilerParams(vmem_limit_bytes=60 * MIB),
        cost_estimate=pl.CostEstimate(
            flops=images * count * D * D * 46, bytes_accessed=images * count * D * 22, transcendentals=0
        ),
        name="feed_forward",
    )(owner, place, tokens, attended, cotangent, inverse, gain, shift, bias_up, *([slots] * blocks))


def down_kernel(owner, act_ref, h_ref, b_ref, d0_ref, d1_ref, d2_ref, d3_ref, *refs):
    out_ref = refs[-1]
    total = h_ref[0].astype(F32) + b_ref[...]
    for block, down in enumerate((d0_ref, d1_ref, d2_ref, d3_ref)):
        total += dot(act_ref[0, :, block * D : (block + 1) * D], down[0])
    out_ref[0] = total.astype(BF16)


def image_spec(start, *tail):
    zeros = (0,) * len(tail)
    return pl.BlockSpec((1,) + tail, lambda step, *_: (start + step,) + zeros)


def down_call(start, stop, before, owner, act, hidden, bias, slots):
    images, count, _ = hidden.shape
    earlier = [] if before is None else [before]
    return pl.pallas_call(
        down_kernel,
        grid_spec=pltpu.PrefetchScalarGridSpec(
            num_scalar_prefetch=1,
            grid=(stop - start,),
            in_specs=[image_spec(start, count, FF), image_spec(start, count, D), whole_spec((1, D))]
            + [weight_spec(4 + NF + block) for block in range(NF)]
            + [pl.BlockSpec(memory_space=pl.ANY)] * len(earlier),
            out_specs=image_spec(start, count, D),
        ),
        out_shape=jax.ShapeDtypeStruct((images, count, D), BF16),
        input_output_aliases={4 + NF: 0} if earlier else {},
        compiler_params=pltpu.CompilerParams(vmem_limit_bytes=60 * MIB),
        cost_estimate=pl.CostEstimate(
            flops=(stop - start) * count * D * D * 8,
            bytes_accessed=(stop - start) * count * D * 12,
            transcendentals=0,
        ),
        name="down",
    )(owner, act, hidden, bias, *([slots] * NF), *earlier)


def back_kernel(first, last, start, pieces, owner, place, *refs):
    (q_ref, k_ref, v_ref, o_ref, do_ref, e_ref, xh_ref, sk_ref, sv_ref, mean_ref, g_ref, s_ref) = refs[:12]
    wq_ref, wk_ref, wv_ref = refs[12:15]
    refs = refs[15:]
    if not first:
        old_acc_ref, old_gg_ref, old_gs_ref = refs[:3]
        refs = refs[4:]
    dlow_ref, dm_ref, acc_ref, gg_ref, gs_ref = refs[:5]
    grads_refs = refs[5:-3]
    grad_ref, dsk_ref, dsv_ref = refs[-3:]
    step = pl.program_id(0)
    rows = q_ref.shape[1] // ROW
    scale = 1.0 / math.sqrt(HD)

    @pl.when(step == 0)
    def _():
        acc_ref[...] = jnp.zeros_like(acc_ref) if first else old_acc_ref[...]
        gg_ref[...] = jnp.zeros_like(gg_ref) if first else old_gg_ref[...]
        gs_ref[...] = jnp.zeros_like(gs_ref) if first else old_gs_ref[...]

    sum_k = sk_ref[0]
    sum_v = sv_ref[0]
    masks = head_masks(BF16)
    blank = jnp.zeros((HD, KEYS), BF16)
    minus = jnp.full((HD, KEYS), -1.0, BF16)
    d_sum_k = jnp.zeros((ROWS_IMG, D), F32)
    d_sum_v = jnp.zeros((ROWS_IMG, D), F32)
    for row in range(rows):
        here = slice(row * ROW, (row + 1) * ROW)
        d_out = do_ref[0, here, :]
        d_out_o = d_out * o_ref[0, here, :]
        q_t = (q_ref[0, here, :] * scale).T
        d_out_t = d_out.T
        v_t = jnp.concatenate([v_ref[0, here, :], sum_v], 0).T
        d_keys = []
        d_values = []
        for pair in range(PAIRS):
            lanes = slice(pair * PAIR, (pair + 1) * PAIR)
            keys = jnp.concatenate([k_ref[0, here, lanes], sum_k[:, lanes]], 0)
            left = jnp.concatenate([d_out[:, lanes], d_out_o[:, lanes]], 1)
            d_query = None
            for half in range(2):
                head = 2 * pair + half
                mine = slice(head * HD, (head + 1) * HD)
                own = v_t[mine]
                right = [own, blank, minus, blank] if half == 0 else [blank, own, blank, minus]
                weight = e_ref[0, row, head]
                d_score = weight * dot(left, jnp.concatenate(right, 0)).astype(BF16)
                d_values.append(dot(d_out_t[mine], weight).astype(BF16))
                d_keys.append(dot(q_t[mine], d_score).astype(BF16))
                part = dot(d_score, keys * masks[half])
                d_query = part if d_query is None else d_query + part
            grad_ref[here, lanes] = (d_query * scale).astype(BF16)
        d_key = jnp.concatenate(d_keys, 0).T
        d_value = jnp.concatenate(d_values, 0).T
        grad_ref[here, D : 2 * D] = d_key[:ROW]
        grad_ref[here, 2 * D :] = d_value[:ROW]
        d_sum_k += d_key[ROW:].astype(F32)
        d_sum_v += d_value[ROW:].astype(F32)
    dsk_ref[step] = d_sum_k.astype(BF16)
    dsv_ref[step] = d_sum_v.astype(BF16)
    normal = xh_ref[0].astype(F32)
    a_t = (normal * g_ref[...] + s_ref[...]).astype(BF16).T
    low = jnp.zeros_like(normal)
    for block, w_ref in enumerate((wq_ref, wk_ref, wv_ref)):
        columns = slice(block * D, (block + 1) * D)
        acc_ref[:, columns] += dot(a_t, grad_ref[:, columns])
        low += dot_nt(grad_ref[:, columns], w_ref[0])
    dlow_ref[0] = low.astype(BF16)
    gs_ref[...] += jnp.sum(low, 0, keepdims=True)
    gg_ref[...] += jnp.sum(low * normal, 0, keepdims=True)

    @pl.when(step == pl.num_programs(0) - 1)
    def _():
        mean_x = mean_ref[start : start + dm_ref.shape[0]].reshape(-1, D).astype(F32)
        mean_t = (mean_x * g_ref[...] + s_ref[...]).astype(BF16).T
        all_k = dsk_ref[...].reshape(-1, D)
        all_v = dsv_ref[...].reshape(-1, D)
        acc_ref[:, D : 2 * D] += dot(mean_t, all_k)
        acc_ref[:, 2 * D :] += dot(mean_t, all_v)
        d_mean = dot_nt(all_k, wk_ref[0]) + dot_nt(all_v, wv_ref[0])
        dm_ref[...] = d_mean.astype(BF16).reshape(dm_ref.shape)
        gs_ref[...] += jnp.sum(d_mean, 0, keepdims=True)
        gg_ref[...] += jnp.sum(d_mean * mean_x, 0, keepdims=True)
        if last and pieces:
            write_pieces(place, grads_refs, lambda block, here: acc_ref[here, block * D : (block + 1) * D])
        elif last:
            for block in range(3):
                grads_refs[0][block] = acc_ref[:, block * D : (block + 1) * D].astype(BF16)


def back_call(start, stop, before, owner, place, groups, operands, gain, shift, slots):
    images, count, _ = operands[0].shape
    rows = count // ROW
    first, last = start == 0, stop == images

    at = functools.partial(image_spec, start)
    grads = grad_shapes(groups, 3) if last else []
    in_specs = (
        [at(count, D)] * 5
        + [at(rows, HEADS, ROW, KEYS), at(count, D), at(ROWS_IMG, D), at(ROWS_IMG, D)]
        + [whole_spec((images, ROWS_IMG, D))]
        + [whole_spec((1, D)), whole_spec((1, D))]
        + [weight_spec(block) for block in range(3)]
    )
    inputs = [owner, place, *operands, gain, shift, slots, slots, slots]
    aliases = {}
    if not first:
        d_low, *sums = before
        in_specs += [whole_spec((D, 3 * D)), whole_spec((1, D)), whole_spec((1, D)), pl.BlockSpec(memory_space=pl.ANY)]
        inputs += [*sums, d_low]
        aliases = {len(inputs) - 1: 0}
    return pl.pallas_call(
        functools.partial(back_kernel, first, last, start, groups is not None),
        grid_spec=pltpu.PrefetchScalarGridSpec(
            num_scalar_prefetch=2,
            grid=(stop - start,),
            in_specs=in_specs,
            out_specs=[
                at(count, D), out_whole((stop - start, ROWS_IMG, D)), out_whole((D, 3 * D)),
                out_whole((1, D)), out_whole((1, D)),
            ]
            + [out_whole(shape) for shape in grads],
            scratch_shapes=[
                pltpu.VMEM((count, 3 * D), BF16),
                pltpu.VMEM((stop - start, ROWS_IMG, D), BF16),
                pltpu.VMEM((stop - start, ROWS_IMG, D), BF16),
            ],
        ),
        out_shape=[
            jax.ShapeDtypeStruct((images, count, D), BF16),
            jax.ShapeDtypeStruct((stop - start, ROWS_IMG, D), BF16),
            jax.ShapeDtypeStruct((D, 3 * D), F32),
            jax.ShapeDtypeStruct((1, D), F32),
            jax.ShapeDtypeStruct((1, D), F32),
        ]
        + [jax.ShapeDtypeStruct(shape, BF16) for shape in grads],
        input_output_aliases=aliases,
        compiler_params=pltpu.CompilerParams(vmem_limit_bytes=60 * MIB),
        cost_estimate=pl.CostEstimate(
            flops=(stop - start) * count * D * D * 20,
            bytes_accessed=(stop - start) * count * D * 24,
            transcendentals=0,
        ),
        name="attend_back",
    )(*inputs)


def last_kernel(x_ref, low_ref, dr_ref, dm_ref, g_ref, *refs):
    out_ref = refs[-1]
    for row in range(dm_ref.shape[1]):
        here = slice(row * ROW, (row + 1) * ROW)
        normal, spread = normalize(x_ref[0, here, :].astype(F32))
        total = low_ref[0, here, :].astype(F32) + dm_ref[0, row : row + 1, :] * (1.0 / ROW)
        d_normal = total * g_ref[...]
        middle = jnp.mean(d_normal, -1, keepdims=True)
        along = jnp.mean(d_normal * normal, -1, keepdims=True)
        out_ref[0, here, :] = dr_ref[0, here, :].astype(F32) + spread * (d_normal - middle - normal * along)


def last_call(start, stop, before, tokens, d_low, d_branch, d_mean, gain):
    images, count, _ = tokens.shape
    earlier = [] if before is None else [before]
    return pl.pallas_call(
        last_kernel,
        grid=(stop - start,),
        in_specs=[image_spec(start, count, D)] * 3
        + [image_spec(start, count // ROW, D), whole_spec((1, D))]
        + [pl.BlockSpec(memory_space=pl.ANY)] * len(earlier),
        out_specs=image_spec(start, count, D),
        out_shape=jax.ShapeDtypeStruct((images, count, D), F32),
        input_output_aliases={5: 0} if earlier else {},
        compiler_params=pltpu.CompilerParams(vmem_limit_bytes=60 * MIB),
        cost_estimate=pl.CostEstimate(
            flops=(stop - start) * count * D * 20,
            bytes_accessed=(stop - start) * count * D * 10,
            transcendentals=0,
        ),
        name="norm_one_back",
    )(tokens, d_low, d_branch, d_mean, gain, *earlier)


def adamw_update(weight_now, gradient, first_moment, second_moment, decay_rate, step_rate):
    first_new = 0.9 * first_moment + 0.1 * gradient
    second_new = 0.95 * second_moment + 0.05 * gradient * gradient
    direction = first_new / (1.0 - 0.9**STEP) / (jnp.sqrt(second_new / (1.0 - 0.95**STEP)) + 1e-08)
    return (weight_now - step_rate * (direction + decay_rate * weight_now), first_new, second_new)


def swap(value, axis, bit):
    size = lax.axis_size(axis)
    return lax.ppermute(value, axis, [(index, index ^ bit) for index in range(size)])


def sum_everywhere(value):
    for axis in ("narrow", "wide"):
        bit = 1
        while bit < lax.axis_size(axis):
            value = value + swap(value, axis, bit)
            bit *= 2
    return value


def join(value):
    inner, outer = group_sizes(lax.axis_size("wide"))
    far = jnp.stack([value] + [swap(value, "wide", inner * step) for step in range(1, outer)])
    near = jnp.stack([far] + [swap(far, "wide", step) for step in range(1, inner)], 1)
    return near.reshape((inner * outer,) + value.shape)


def reorder(value, axis, dim=0):
    return jnp.take(value, lax.axis_index(axis) ^ jnp.arange(lax.axis_size(axis)), axis=dim)


def fetch_blocks(low_master, owners, means, whole_pieces):
    wide = lax.axis_size("wide")
    narrow = lax.axis_size("narrow")
    pieces = lax.all_to_all(low_master.reshape(wide, -1, D), "wide", 0, 0, tiled=True)
    mine = jnp.take(pieces, owners, axis=0)
    count, depth, _ = mine.shape
    joined = join(jnp.concatenate([mine.reshape(-1, D), means.reshape(-1, D)], 0))
    mean_all = reorder(joined[:, count * depth :], "wide").reshape((wide,) + means.shape).swapaxes(0, 1)
    mean_all = mean_all.reshape(means.shape[0], -1, D)
    if whole_pieces:
        return [joined] + [swap(joined, "narrow", step) for step in range(1, narrow)], mean_all
    rows = joined[:, : count * depth]
    halves = jnp.stack([rows] + [swap(rows, "narrow", step) for step in range(1, narrow)])
    halves = reorder(reorder(halves, "narrow"), "wide", 1).reshape(narrow, wide, count, depth, D)
    return [halves.transpose(2, 0, 1, 3, 4).reshape(count, D, D)], mean_all


def piece_lists(grads, groups):
    if len(grads) > 1:
        return list(grads)
    (blocks,) = grads
    narrow = lax.axis_size("narrow")
    wide = lax.axis_size("wide")
    parts = blocks.reshape(blocks.shape[0], narrow, wide, -1, D).transpose(1, 2, 0, 3, 4)
    parts = reorder(reorder(parts, "narrow"), "wide", 1)
    return [by_group(part.reshape(wide, -1, D)) for part in parts]


def by_group(pieces):
    inner, outer = group_sizes(lax.axis_size("wide"))
    return pieces.reshape((outer, inner) + pieces.shape[1:]).swapaxes(0, 1)


def sum_narrow(lists):
    total = lists[0].astype(F32)
    for step in range(1, len(lists)):
        total += swap(lists[step], "narrow", step).astype(F32)
    return total.astype(BF16)


def sum_group(pieces, stride):
    total = pieces[0].astype(F32)
    for step in range(1, len(pieces)):
        total += swap(pieces[step], "wide", step * stride).astype(F32)
    return total


def sum_near(pieces):
    return sum_group(pieces, 1).astype(BF16)


def sum_far(pieces):
    inner, _ = group_sizes(lax.axis_size("wide"))
    return sum_group(pieces, inner)


def after(value, *others):
    return lax.optimization_barrier((value, *others))[0]


def per_device(
    tokens, cotangent, owner_list, master, moment_one, moment_two, small_params, small_one, small_two
):
    images, count, _ = tokens.shape
    rows = count // ROW
    wide = lax.axis_size("wide")
    small = small_params.reshape(1, -1)
    gain_one = small[:, 0:D]
    shift_one = small[:, D : 2 * D]
    gain_two = small[:, 2 * D : 3 * D]
    shift_two = small[:, 3 * D : 4 * D]
    bias_up = small[:, 4 * D : 4 * D + FF]
    bias_down = small[:, 4 * D + FF :]
    low_master = master.astype(BF16)
    slots = lax.all_gather(low_master.reshape(-1, D), ("wide", "narrow"), axis=0, tiled=True)
    slots = slots.reshape(-1, D, D)
    narrow = lax.axis_size("narrow")
    inner, outer = group_sizes(wide)
    depth = D // narrow // wide
    groups = (narrow, inner, outer) if depth % 16 == 0 and narrow > 1 else None
    me = lax.axis_index("wide")
    place = jnp.stack([me, lax.axis_index("narrow")]).astype(jnp.int32)
    normal, means = norm_call(tokens)
    parts, mean_all = fetch_blocks(low_master, owner_list[:3], means.astype(BF16), groups is not None)
    queries, keys, values, weights, attended, inverse, sum_k, sum_v = attend_call(
        place, normal, mean_all, gain_one, shift_one, parts
    )
    act, hidden, d_branch, d_out, gain_two_grad, shift_two_grad, bias_up_grad, bias_down_grad, *grads_late = ff_call(
        owner_list, place, groups, tokens, attended, cotangent, inverse, gain_two, shift_two, bias_up, slots
    )
    quarter = images // 4
    half = images // 2

    late = piece_lists(grads_late, groups)
    block_out = down_call(0, quarter, None, owner_list, act, hidden, bias_down, slots)
    late = after(sum_narrow(late), block_out)
    operands = (after(queries, late), keys, values, attended, d_out, weights, normal, sum_k, sum_v, mean_all)
    back = functools.partial(
        back_call, owner=owner_list, place=place, groups=groups, operands=operands, gain=gain_one,
        shift=shift_one, slots=slots,
    )
    d_low, mean_first, *sums = back(0, half, None)
    late, d_low, *sums = lax.optimization_barrier((sum_near(late), d_low, *sums))
    late_shares = sum_far(late)
    d_low, mean_second, _, gain_one_grad, shift_one_grad, *grads_early = back(half, images, [d_low] + sums)

    d_mean = jnp.concatenate([mean_first, mean_second], 0).reshape(images, wide, rows, D).swapaxes(0, 1)
    d_mean = by_group(reorder(d_mean.reshape(wide, -1, D), "wide"))
    early = sum_narrow(piece_lists(grads_early, groups))
    block_out = down_call(
        quarter, images - quarter, block_out, owner_list, after(act, early), hidden, bias_down, slots
    )
    early = after(sum_near(jnp.concatenate([early, d_mean], 2)), block_out)
    block_out = down_call(
        images - quarter, images, block_out, owner_list, after(act, early), hidden, bias_down, slots
    )
    shares = after(sum_far(early), block_out)
    own_mean = shares[3 * depth :].reshape(images, rows, D)
    shares = jnp.concatenate([shares[: 3 * depth], late_shares], 0).reshape(-1, depth, D).astype(BF16)

    slotted = jnp.zeros((wide, depth, D), BF16).at[owner_list ^ me].set(shares)
    slotted = slotted.reshape(outer, inner, depth, D)
    moved = jnp.stack([slotted[0]] + [swap(slotted[step], "wide", step * inner) for step in range(1, outer)], 1)
    grad_tokens = last_call(0, half, None, tokens, d_low, d_branch, own_mean, gain_one)
    moved, grad_tokens = lax.optimization_barrier((moved, grad_tokens))
    moved = jnp.stack([moved[0]] + [swap(moved[step], "wide", step) for step in range(1, inner)], 1)
    grad_tokens = last_call(half, images, grad_tokens, tokens, d_low, d_branch, own_mean, gain_one)
    moved, grad_tokens = lax.optimization_barrier((moved, grad_tokens))
    own_grad = reorder(moved.reshape(wide, depth, D), "wide").reshape(1, -1, D).astype(F32)
    small_grad = sum_everywhere(
        jnp.concatenate(
            [gain_one_grad, shift_one_grad, gain_two_grad, shift_two_grad, bias_up_grad, bias_down_grad], 1
        )
    ).reshape(-1)
    owns_slot = jnp.any(owner_list == me)
    slot_weight, slot_first, slot_second = adamw_update(
        master, own_grad, moment_one, moment_two, 0.1, RATE
    )
    new_master = jnp.where(owns_slot, slot_weight, master)
    new_one = jnp.where(owns_slot, slot_first, moment_one)
    new_two = jnp.where(owns_slot, slot_second, moment_two)
    small_new, small_one_new, small_two_new = adamw_update(
        small_params, small_grad, small_one, small_two, 0.0, GAIN_RATE
    )
    return (block_out, grad_tokens, new_master, new_one, new_two, small_new, small_one_new, small_two_new)


def solution(mesh):
    split = P("narrow", "wide", None)
    slot = P("wide", "narrow", None)
    return jax.shard_map(
        per_device,
        mesh=mesh,
        in_specs=(split, split, P(), slot, slot, slot, P(), P(), P()),
        out_specs=(split, split, slot, slot, slot, P(), P(), P()),
        check_vma=False,
    )
```

time: 560 us -> 410 us (0.73)
  waiting for transfers between devices: 98.6 us -> 35.2 us
  blocking collectives: 60.6 us -> 0 us
  Pallas kernels: 300 us -> 276 us
  local copies, waits for them, and re-layouts: 32.1 us -> 10.8 us
  starting transfers between devices: 39.8 us -> 50.4 us
    all_to_all x6 -> x1, waiting for transfers between devices: 71.1 us -> 0.01 us  [fetch_blocks(): lax.all_to_all(low_master.reshape(wide, -1, D), 'wide', 0, 0, tiled=True)]
    all_gather x1 -> x0, blocking collectives: 47.9 us -> none  [per_device(): lax.all_gather(means.astype(BF16).reshape(-1, D), 'wide', axis=0, tiled=T...]
    ppermute x5 -> x32, starting transfers between devices: 7.24 us -> 42 us  [swap(): lax.ppermute(value, axis, [(index, index ^ bit) for index in range(size)])]
    ppermute x5 -> x32, waiting for transfers between devices: 8.34 us -> 35.1 us  [swap(): lax.ppermute(value, axis, [(index, index ^ bit) for index in range(size)])]
    all_to_all x6 -> x1, starting transfers between devices: 32.6 us -> 8.32 us  [fetch_blocks(): lax.all_to_all(low_master.reshape(wide, -1, D), 'wide', 0, 0, tiled=True)]
    pallas_call x4 -> x9, Pallas kernels: 290 us -> 267 us  [the longest x1 106 us: ff_call(): pl.pallas_call(functools.partial(ff_kernel, groups is not None), grid_spe...]
    all_gather x1, waiting for transfers between devices: 19.1 us -> 0.02 us  [per_device(): lax.all_gather(low_master.reshape(-1, D), ('wide', 'narrow'), axis=0, til...]
    all_to_all x1 -> x0, blocking collectives: 12.7 us -> none  [share_sums(): lax.all_to_all(grads.reshape(blocks, narrow, D // narrow, D), 'narrow', 1...]
  transfers between devices with their start and end apart: 12 -> 34, of which waited for: 8 -> 7; matrix products, arithmetic and copies ran while one was open for 5% -> 4% of each run, Pallas kernels for 4% -> 32%
where the time goes in v3:
time: 410 us; the launch traced here: 404 us
  Pallas kernels  276 us (67%)
  starting transfers between devices  50.4 us (12%)
  waiting for transfers between devices  35.2 us (9%)
  other arithmetic  17.4 us (4%)
  between operations  14.9 us (4%)
  local copies, waits for them, and re-layouts  10.8 us (3%)
    pallas_call x1, Pallas kernels, ff_call(): pl.pallas_call(functools.partial(ff_kernel, groups is not None), grid_spe...  106 us
    pallas_call x2, Pallas kernels, back_call(): pl.pallas_call(functools.partial(back_kernel, first, last, start, groups...  80.1 us
    ppermute x32, starting transfers between devices, swap(): lax.ppermute(value, axis, [(index, index ^ bit) for index in range(size)])  42 us
    ppermute x32, waiting for transfers between devices, swap(): lax.ppermute(value, axis, [(index, index ^ bit) for index in range(size)])  35.1 us
    pallas_call x1, Pallas kernels, attend_call(): pl.pallas_call(functools.partial(attend_kernel, len(parts)), grid_spec=pl...  34.4 us
    pallas_call x3, Pallas kernels, down_call(): pl.pallas_call(down_kernel, grid_spec=pltpu.PrefetchScalarGridSpec(num_sc...  28.3 us
    pallas_call x2, Pallas kernels, last_call(): pl.pallas_call(last_kernel, grid=(stop - start,), in_specs=[image_spec(st...  17.9 us
    pallas_call x1, Pallas kernels, norm_call(): pl.pallas_call(norm_kernel, grid=(images,), in_specs=[tile_spec(count, D)...  9.09 us
  transfers between devices with their start and end apart: 34, of which 7 were waited for; matrix products, arithmetic and copies ran while one was open for 4% of the time, Pallas kernels for 32%

profile of v3, /device:TPU:0, one launch (start us, length us, event | category | flops | bytes accessed | tf_op | source)
XLA Modules:
  0.0 404.5 jit_solution(8900477424234649007)
XLA Ops:
  7.2 1.8 convert_element_type.109
  9.0 8.3 %all-to-all-start = ((bf16[16,16,512]{2,1,0:T(8,128)(2,1)}), bf16[16,16,512]{2,1,0:T(8,128)(2,1)S(1)}, u32[]{:S(2)}, u32[]{:S(2)}) async-start(bf16[16,16,512]{2,1,0:T(8,128)(2,1)} %bitcast.144), calls=%async_computation | async-start | bytes 524288 | tf_op jit(solution)/shard_map/all_to_all | solution.py:597
  18.2 9.1 %norm_one.1 = (bf16[8,768,512]{2,1,0:T(8,128)(2,1)}, f32[8,4,512]{2,1,0:T(4,128)}) custom-call(bf16[8,768,512]{2,1,0:T(8,128)(2,1)} %x_ref.7), custom_call_target="tpu_custom_call" | custom-call | flops 31457280 | bytes 12582912 | tf_op jit(solution)/shard_map/norm_one/pallas_call | solution.py:84
  28.8 2.0 collective-permute-start
  30.8 2.4 collective-permute-start.1
  33.3 2.9 collective-permute-done
  36.2 4.6 %collective-permute-done.1 = bf16[80,512]{1,0:T(8,128)(2,1)S(1)} collective-permute-done((bf16[80,512]{1,0:T(8,128)(2,1)S(1)}, bf16[80,512]{1,0:T(8,128)(2,1)S(1)}, u32[]{:S(2)}, u32[]{:S(2)}) %collective-permute-start.1) | collective-permute-done | bytes 81952 | tf_op jit(solution)/shard_map/ppermute | solution.py:571
  40.9 1.3 collective-permute-start.3
  42.2 1.1 collective-permute-start.4
  43.3 1.1 collective-permute-start.5
  44.4 13.5 %collective-permute-done.3 = bf16[4,80,512]{2,1,0:T(8,128)(2,1)S(1)} collective-permute-done((bf16[4,80,512]{2,1,0:T(8,128)(2,1)S(1)}, bf16[4,80,512]{2,1,0:T(8,128)(2,1)S(1)}, u32[]{:S(2)}, u32[]{:S(2)}) %collective-permute-start.3) | collective-permute-done | bytes 327712 | tf_op jit(solution)/shard_map/ppermute | solution.py:571
  57.9 6.2 %collective-permute-done.5 = bf16[4,80,512]{2,1,0:T(8,128)(2,1)S(1)} collective-permute-done((bf16[4,80,512]{2,1,0:T(8,128)(2,1)S(1)}, bf16[4,80,512]{2,1,0:T(8,128)(2,1)S(1)}, u32[]{:S(2)}, u32[]{:S(2)}) %collective-permute-start.5) | collective-permute-done | bytes 327712 | tf_op jit(solution)/shard_map/ppermute | solution.py:571
  68.2 0.9 reshape.205.mean_ref.refs_9_
  69.1 34.4 %attend.1 = (bf16[8,768,512]{2,1,0:T(8,128)(2,1)}, bf16[8,768,512]{2,1,0:T(8,128)(2,1)}, bf16[8,768,512]{2,1,0:T(8,128)(2,1)}, bf16[8,4,8,192,256]{4,3,2,1,0:T(8...) custom-call(s32[2]{0:T(128)} %pad_add_fusion.place, ...), custom_call_target="tpu_custom_call" | custom-call | flops 16106127360 | bytes 62914560 | tf_op jit(solution)/shard_map/attend/pallas_call | solution.py:191
  103.6 106.1 %feed_forward.1 = (bf16[8,768,2048]{2,1,0:T(8,128)(2,1)}, bf16[8,768,512]{2,1,0:T(8,128)(2,1)}, bf16[8,768,512]{2,1,0:T(8,128)(2,1)}, bf16[8,768,512]{2,1,0:T(8,...) custom-call(s32[12]{0:T(128)} %owner.11, ...), custom_call_target="tpu_custom_call" | custom-call | flops 74088185856 | bytes 69206016 | tf_op jit(solution)/shard_map/feed_forward/pallas_call | solution.py:307
  210.7 8.1 %down.3.refs_0_ = bf16[8,768,512]{2,1,0:T(8,128)(2,1)} custom-call(s32[12]{0:T(128)} %owner.11, bf16[8,768,2048]{2,1,0:T(8,128)(2,1)} %get-tuple-element.86.act_ref, bf16[8,768,512]{2,1,0:T(8,128)(2,1)} %get-tuple-element.63.h_ref, f32[1,512]{1,0:T(1,128)} %get-tuple-element.133.b_ref, bf16[16,512,512]{2,1,0:T(8,128)(2,1)} %bitcast.121, ...), custom_call_target="tpu_custom_call" | custom-call | flops 3221225472 | bytes 9437184 | tf_op jit(solution)/shard_map/down/pallas_call | solution.py:358
  218.8 1.4 copy-done.1
  220.2 3.1 add_convert_fusion
  223.4 2.4 collective-permute-start.10
  227.0 38.8 %attend_back.2 = (bf16[8,768,512]{2,1,0:T(8,128)(2,1)}, bf16[4,64,512]{2,1,0:T(8,128)(2,1)}, f32[512,1536]{1,0:T(8,128)}, f32[1,512]{1,0:T(1,128)}, f32[1,512]{1,0:T(1,128)}) custom-call(s32[12]{0:T(128)} %owner.11, s32[2]{0:T(128)} %pad_add_fusion.place, bf16[8,768,512]{2,1,0:T(8,128)(2,1)} %get-tuple-element.65.refs_0_, ...), custom_call_target="tpu_custom_call" | custom-call | flops 16106127360 | bytes 37748736 | tf_op jit(solution)/shard_map/attend_back/pallas_call | solution.py:492
  265.9 1.7 fusion.2
  267.7 41.2 %attend_back.3 = (bf16[8,768,512]{2,1,0:T(8,128)(2,1)}, bf16[4,64,512]{2,1,0:T(8,128)(2,1)}, f32[512,1536]{1,0:T(8,128)}, f32[1,512]{1,0:T(1,128)}, f32[1,512]{1...) custom-call(s32[12]{0:T(128)} %owner.11, ...), custom_call_target="tpu_custom_call", output_to_operand_aliasing={{0}: (20, {})} | custom-call | flops 16106127360 | bytes 37748736 | tf_op jit(solution)/shard_map/attend_back/pallas_call | solution.py:492
  311.8 1.8 collective-permute-start.28
  313.6 2.0 collective-permute-done.28
  315.6 1.8 collective-permute-start.29
  317.4 1.0 pad_maximum_fusion.1
  319.7 1.6 collective-permute-start.18
  321.3 1.3 collective-permute-start.19
  322.5 1.6 collective-permute-start.20
  325.0 4.8 %collective-permute-done.30 = f32[1,4608]{1,0:T(1,128)S(1)} collective-permute-done((f32[1,4608]{1,0:T(1,128)S(1)}, f32[1,4608]{1,0:T(1,128)S(1)}, u32[]{:S(2)}, u32[]{:S(2)}) %collective-permute-start.30) | collective-permute-done | bytes 18464 | tf_op jit(solution)/shard_map/ppermute | solution.py:571
  329.9 3.5 collective-permute-start.31
  333.4 1.0 collective-permute-done.19
  334.5 1.4 add_convert_fusion.1
  336.0 1.5 collective-permute-start.12
  338.0 1.5 collective-permute-start.14
  339.5 12.2 %down.4.refs_0_ = bf16[8,768,512]{2,1,0:T(8,128)(2,1)} custom-call(s32[12]{0:T(128)} %owner.11, bf16[8,768,2048]{2,1,0:T(8,128)(2,1)} %get-tuple-element.86.act_ref, bf16[8,768,512]{2,1,0:T(8,128)(2,1)} %get-tuple-element.63.h_ref, f32[1,512]{1,0:T(1,128)} %get-tuple-element.133.b_ref, ...), custom_call_target="tpu_custom_call", output_to_operand_aliasing={{}: (8, {})} | custom-call | flops 6442450944 | bytes 18874368 | tf_op jit(solution)/shard_map/down/pallas_call | solution.py:358
  351.9 2.6 collective-permute-start.15
  354.5 1.7 collective-permute-start.16
  356.2 1.4 collective-permute-start.17
  357.6 8.1 %down.5 = bf16[8,768,512]{2,1,0:T(8,128)(2,1)} custom-call(s32[12]{0:T(128)} %owner.11, bf16[8,768,2048]{2,1,0:T(8,128)(2,1)} %get-tuple-element.86.act_ref, bf16[8,768,512]{2,1,0:T(8,128)(2,1)} %get-tuple-element.63.h_ref, f32[1,512]{1,0:T(1,128)} %get-tuple-element.133.b_ref, bf16[16,512,512]{2,1,0:T(8,128)(2,1)} %bitcast.135, ...), custom_call_target="tpu_custom_call", output_to_operand_aliasing={{}: (8, {})} | custom-call | flops 3221225472 | bytes 9437184 | tf_op jit(solution)/shard_map/down/pallas_call | solution.py:358
  365.8 1.0 scatter_fusion
  367.4 2.4 collective-permute-start.22
  369.8 1.4 collective-permute-start.23
  372.0 8.9 %norm_one_back.2.refs_0_ = f32[8,768,512]{2,1,0:T(8,128)} custom-call(bf16[8,768,512]{2,1,0:T(8,128)(2,1)} %x_ref.7, bf16[8,768,512]{2,1,0:T(8,128)(2,1)} %get-tuple-element.89.low_ref, bf16[8,768,512]{2,1,0:T(8,128)(2,1)} %get-tuple-element.90.dr_ref, f32[8,4,512]{2,1,0:T(4,128)} %reshape.212.dm_ref, f32[1,512]{1,0:T(1,128)} %get-tuple-element.137.g_ref.refs_10_), custom_call_target="tpu_custom_call" | custom-call | flops 31457280 | bytes 15728640 | tf_op jit(solution)/shard_map/norm_one_back/pallas_call | solution.py:543
  381.7 1.7 collective-permute-start.25
  383.4 1.2 collective-permute-start.26
  385.2 8.9 %norm_one_back.3 = f32[8,768,512]{2,1,0:T(8,128)} custom-call(bf16[8,768,512]{2,1,0:T(8,128)(2,1)} %x_ref.7, bf16[8,768,512]{2,1,0:T(8,128)(2,1)} %get-tuple-element.89.low_ref, bf16[8,768,512]{2,1,0:T(8,128)(2,1)} %get-tuple-element.90.dr_ref, f32[8,4,512]{2,1,0:T(4,128)} %reshape.212.dm_ref, ...), custom_call_target="tpu_custom_call", output_to_operand_aliasing={{}: (5, {})} | custom-call | flops 31457280 | bytes 15728640 | tf_op jit(solution)/shard_map/norm_one_back/pallas_call | solution.py:543
  394.9 2.5 fusion.8
  (144 shorter events, 18.3 us)
Async XLA Ops:
  7.2 96.4 %all-gather.3.cloned.1.call-start = ((), (), s32[]{:S(2)}) async-start(), calls=%async_computation.1 | async-start | bytes 8650752 | tf_op jit(solution)/shard_map/all_gather | solution.py:668
  9.0 19.2 %all-to-all-start = ((bf16[16,16,512]{2,1,0:T(8,128)(2,1)}), bf16[16,16,512]{2,1,0:T(8,128)(2,1)S(1)}, u32[]{:S(2)}, u32[]{:S(2)}) async-start(bf16[16,16,512]{2,1,0:T(8,128)(2,1)} %bitcast.144), calls=%async_computation | async-start | bytes 524288 | tf_op jit(solution)/shard_map/all_to_all | solution.py:597
  27.3 37.1 %copy-start.7 = (f32[4608]{0:T(1024)S(1)}, f32[4608]{0:T(1024)}, u32[]{:S(2)}) copy-start(f32[4608]{0:T(1024)} %param.17) | copy-start | bytes 55300
  28.8 7.3 %collective-permute-start = (bf16[80,512]{1,0:T(8,128)(2,1)S(1)}, bf16[80,512]{1,0:T(8,128)(2,1)S(1)}, u32[]{:S(2)}, u32[]{:S(2)}) collective-permute-start(bf16[80,512]{1,0:T(8,128)(2,1)S(1)} %get-tuple-element.132), channel_id=1, source_target_pairs={{0,8},{2,10},{4,12},{6,14},{8,0},{10,2},{12,4},{14,6},{16,24},{18,... | collective-permute-start | bytes 245768 | tf_op jit(solution)/shard_map/ppermute | solution.py:571
  30.8 10.0 %collective-permute-start.1 = (bf16[80,512]{1,0:T(8,128)(2,1)S(1)}, bf16[80,512]{1,0:T(8,128)(2,1)S(1)}, u32[]{:S(2)}, u32[]{:S(2)}) collective-permute-start(bf16[80,512]{1,0:T(8,128)(2,1)S(1)} %get-tuple-element.132), channel_id=1, source_target_pairs={{0,16},{2,18},{4,20},{6,22},{8,24},{10,26},{12,28},{14,30},{16,0},... | collective-permute-start | bytes 245768 | tf_op jit(solution)/shard_map/ppermute | solution.py:571
  33.2 7.6 %collective-permute-start.2 = (bf16[80,512]{1,0:T(8,128)(2,1)S(1)}, bf16[80,512]{1,0:T(8,128)(2,1)S(1)}, u32[]{:S(2)}, u32[]{:S(2)}) collective-permute-start(bf16[80,512]{1,0:T(8,128)(2,1)S(1)} %get-tuple-element.132), channel_id=1, source_target_pairs={{0,24},{2,26},{4,28},{6,30},{8,16},{10,18},{12,20},{14,22},{16,8},... | collective-permute-start | bytes 245768 | tf_op jit(solution)/shard_map/ppermute | solution.py:571
  40.9 17.0 %collective-permute-start.3 = (bf16[4,80,512]{2,1,0:T(8,128)(2,1)S(1)}, bf16[4,80,512]{2,1,0:T(8,128)(2,1)S(1)}, u32[]{:S(2)}, u32[]{:S(2)}) collective-permute-start(bf16[4,80,512]{2,1,0:T(8,128)(2,1)S(1)} %get-tuple-element.122), channel_id=1, source_target_pairs={{0,2},{2,0},{4,6},{6,4},{8,10},{10,8},{12,14},{14,12},{16,18},{18,... | collective-permute-start | bytes 983048 | tf_op jit(solution)/shard_map/ppermute | solution.py:571
  42.2 15.7 %collective-permute-start.4 = (bf16[4,80,512]{2,1,0:T(8,128)(2,1)S(1)}, bf16[4,80,512]{2,1,0:T(8,128)(2,1)S(1)}, u32[]{:S(2)}, u32[]{:S(2)}) collective-permute-start(bf16[4,80,512]{2,1,0:T(8,128)(2,1)S(1)} %get-tuple-element.122), channel_id=1, source_target_pairs={{0,4},{2,6},{4,0},{6,2},{8,12},{10,14},{12,8},{14,10},{16,20},{18,... | collective-permute-start | bytes 983048 | tf_op jit(solution)/shard_map/ppermute | solution.py:571
  43.3 20.8 %collective-permute-start.5 = (bf16[4,80,512]{2,1,0:T(8,128)(2,1)S(1)}, bf16[4,80,512]{2,1,0:T(8,128)(2,1)S(1)}, u32[]{:S(2)}, u32[]{:S(2)}) collective-permute-start(bf16[4,80,512]{2,1,0:T(8,128)(2,1)S(1)} %get-tuple-element.122), channel_id=1, source_target_pairs={{0,6},{2,4},{4,2},{6,0},{8,14},{10,12},{12,10},{14,8},{16,22},{18,... | collective-permute-start | bytes 983048 | tf_op jit(solution)/shard_map/ppermute | solution.py:571
  64.3 4.8 %collective-permute-start.6 = (bf16[16,80,512]{2,1,0:T(8,128)(2,1)S(1)}, bf16[16,80,512]{2,1,0:T(8,128)(2,1)}, u32[]{:S(2)}, u32[]{:S(2)}) collective-permute-start(bf16[16,80,512]{2,1,0:T(8,128)(2,1)S(1)} %bitcast.141), channel_id=1, source_target_pairs={{0,1},{1,0},{2,3},{3,2},{4,5},{5,4},{6,7},{7,6},{8,9},{9,8},{10,11... | collective-permute-start | bytes 3932168 | tf_op jit(solution)/shard_map/ppermute | solution.py:571
  103.6 106.5 %copy-start.11 = (s32[12]{0:T(128)S(1)}, s32[12]{0:T(128)}, u32[]{:S(2)}) copy-start(s32[12]{0:T(128)} %owner.11) | copy-start | bytes 148
  209.8 9.0 %collective-permute-start.7 = (bf16[4,4,144,512]{3,2,1,0:T(8,128)(2,1)}, bf16[4,4,144,512]{3,2,1,0:T(8,128)(2,1)S(1)}, u32[]{:S(2)}, u32[]{:S(2)}) collective-permute-start(bf16[4,4,144,512]{3,2,1,0:T(8,128)(2,1)} %get-tuple-element.62), channel_id=1, source_target_pairs={{0,1},{1,0},{2,3},{3,2},{4,5},{5,4},{6,7},{7,6},{8,9},{9,8},{10,11... | collective-permute-start | bytes 7077896 | tf_op jit(solution)/shard_map/ppermute | solution.py:571
  223.4 42.4 %collective-permute-start.10 = (bf16[4,144,512]{2,1,0:T(8,128)(2,1)S(1)}, bf16[4,144,512]{2,1,0:T(8,128)(2,1)}, u32[]{:S(2)}, u32[]{:S(2)}) collective-permute-start(bf16[4,144,512]{2,1,0:T(8,128)(2,1)S(1)} %get-tuple-element.107), channel_id=1, source_target_pairs={{0,6},{2,4},{4,2},{6,0},{8,14},{10,12},{12,10},{14,8},{16,22},{18,... | collective-permute-start | bytes 1769480 | tf_op jit(solution)/shard_map/ppermute | solution.py:571
  225.8 40.0 %collective-permute-start.8 = (bf16[4,144,512]{2,1,0:T(8,128)(2,1)S(1)}, bf16[4,144,512]{2,1,0:T(8,128)(2,1)}, u32[]{:S(2)}, u32[]{:S(2)}) collective-permute-start(bf16[4,144,512]{2,1,0:T(8,128)(2,1)S(1)} %get-tuple-element.106), channel_id=1, source_target_pairs={{0,2},{2,0},{4,6},{6,4},{8,10},{10,8},{12,14},{14,12},{16,18},{18,... | collective-permute-start | bytes 1769480 | tf_op jit(solution)/shard_map/ppermute | solution.py:571
  226.7 39.1 %collective-permute-start.9 = (bf16[4,144,512]{2,1,0:T(8,128)(2,1)S(1)}, bf16[4,144,512]{2,1,0:T(8,128)(2,1)}, u32[]{:S(2)}, u32[]{:S(2)}) collective-permute-start(bf16[4,144,512]{2,1,0:T(8,128)(2,1)S(1)} %get-tuple-element.108), channel_id=1, source_target_pairs={{0,4},{2,6},{4,0},{6,2},{8,12},{10,14},{12,8},{14,10},{16,20},{18,... | collective-permute-start | bytes 1769480 | tf_op jit(solution)/shard_map/ppermute | solution.py:571
  267.6 42.6 %copy-start.19 = (f32[1,512]{1,0:T(1,128)S(1)}, f32[1,512]{1,0:T(1,128)}, u32[]{:S(2)}) copy-start(f32[1,512]{1,0:T(1,128)} %get-tuple-element.97) | copy-start | bytes 6148
  267.6 42.6 %copy-start.18 = (f32[1,512]{1,0:T(1,128)S(1)}, f32[1,512]{1,0:T(1,128)}, u32[]{:S(2)}) copy-start(f32[1,512]{1,0:T(1,128)} %get-tuple-element.98) | copy-start | bytes 6148
  267.6 42.6 %copy-start.13 = (f32[1,2048]{1,0:T(1,128)S(1)}, f32[1,2048]{1,0:T(1,128)}, u32[]{:S(2)}) copy-start(f32[1,2048]{1,0:T(1,128)} %get-tuple-element.99) | copy-start | bytes 24580
  267.6 42.6 %copy-start.17 = (f32[1,512]{1,0:T(1,128)S(1)}, f32[1,512]{1,0:T(1,128)}, u32[]{:S(2)}) copy-start(f32[1,512]{1,0:T(1,128)} %get-tuple-element.100) | copy-start | bytes 6148
  267.6 42.7 %copy-start.12 = (s32[12]{0:T(128)S(1)}, s32[12]{0:T(128)}, u32[]{:S(2)}) copy-start(s32[12]{0:T(128)} %owner.11) | copy-start | bytes 148
  267.6 43.4 %copy-start.16 = (pred[16]{0:T(512)(128)(4,1)S(1)}, pred[16]{0:T(512)(128)(4,1)}, u32[]{:S(2)}) copy-start(pred[16]{0:T(512)(128)(4,1)} %copy-done.15) | copy-start | bytes 52
  267.6 49.8 %copy-start.6 = (bf16[4,64,512]{2,1,0:T(8,128)(2,1)S(1)}, bf16[4,64,512]{2,1,0:T(8,128)(2,1)}, u32[]{:S(2)}) copy-start(bf16[4,64,512]{2,1,0:T(8,128)(2,1)} %get-tuple-element.82) | copy-start | bytes 786436
  310.3 1.5 collective-permute-start.27
  311.2 23.2 %collective-permute-start.11 = (bf16[4,4,48,512]{3,2,1,0:T(8,128)(2,1)}, bf16[4,4,48,512]{3,2,1,0:T(8,128)(2,1)}, u32[]{:S(2)}, u32[]{:S(2)}) collective-permute-start(bf16[4,4,48,512]{3,2,1,0:T(8,128)(2,1)} %get-tuple-element.81), channel_id=1, source_target_pairs={{0,1},{1,0},{2,3},{3,2},{4,5},{5,4},{6,7},{7,6},{8,9},{9,8},{10,11... | collective-permute-start | bytes 2359304 | tf_op jit(solution)/shard_map/ppermute | solution.py:571
  311.8 3.8 collective-permute-start.28
  315.6 8.5 %collective-permute-start.29 = (f32[1,4608]{1,0:T(1,128)S(1)}, f32[1,4608]{1,0:T(1,128)S(1)}, u32[]{:S(2)}, u32[]{:S(2)}) collective-permute-start(f32[1,4608]{1,0:T(1,128)S(1)} %add.136), channel_id=1, source_target_pairs={{0,4},{2,6},{4,0},{6,2},{8,12},{10,14},{12,8},{14,10},{16,20},{18,... | collective-permute-start | bytes 55304 | tf_op jit(solution)/shard_map/ppermute | solution.py:571
  318.7 15.8 %copy-start.3 = (bf16[4,4,48,512]{3,2,1,0:T(8,128)(2,1)S(1)}, bf16[4,4,48,512]{3,2,1,0:T(8,128)(2,1)}, u32[]{:S(2)}) copy-start(bf16[4,4,48,512]{3,2,1,0:T(8,128)(2,1)} %get-tuple-element.80) | copy-start | bytes 2359300
  319.7 13.7 %collective-permute-start.18 = (bf16[144,512]{1,0:T(8,128)(2,1)S(1)}, bf16[144,512]{1,0:T(8,128)(2,1)S(1)}, u32[]{:S(2)}, u32[]{:S(2)}) collective-permute-start(bf16[144,512]{1,0:T(8,128)(2,1)S(1)} %get-tuple-element.115), channel_id=1, source_target_pairs={{0,8},{2,10},{4,12},{6,14},{8,0},{10,2},{12,4},{14,6},{16,24},{18,... | collective-permute-start | bytes 442376 | tf_op jit(solution)/shard_map/ppermute | solution.py:571
  321.3 13.1 %collective-permute-start.19 = (bf16[144,512]{1,0:T(8,128)(2,1)S(1)}, bf16[144,512]{1,0:T(8,128)(2,1)S(1)}, u32[]{:S(2)}, u32[]{:S(2)}) collective-permute-start(bf16[144,512]{1,0:T(8,128)(2,1)S(1)} %get-tuple-element.117), channel_id=1, source_target_pairs={{0,16},{2,18},{4,20},{6,22},{8,24},{10,26},{12,28},{14,30},{16,0},... | collective-permute-start | bytes 442376 | tf_op jit(solution)/shard_map/ppermute | solution.py:571
  322.5 11.8 %collective-permute-start.20 = (bf16[144,512]{1,0:T(8,128)(2,1)S(1)}, bf16[144,512]{1,0:T(8,128)(2,1)S(1)}, u32[]{:S(2)}, u32[]{:S(2)}) collective-permute-start(bf16[144,512]{1,0:T(8,128)(2,1)S(1)} %get-tuple-element.116), channel_id=1, source_target_pairs={{0,24},{2,26},{4,28},{6,30},{8,16},{10,18},{12,20},{14,22},{16,8},... | collective-permute-start | bytes 442376 | tf_op jit(solution)/shard_map/ppermute | solution.py:571
  324.2 5.7 %collective-permute-start.30 = (f32[1,4608]{1,0:T(1,128)S(1)}, f32[1,4608]{1,0:T(1,128)S(1)}, u32[]{:S(2)}, u32[]{:S(2)}) collective-permute-start(f32[1,4608]{1,0:T(1,128)S(1)} %add.137), channel_id=1, source_target_pairs={{0,8},{2,10},{4,12},{6,14},{8,0},{10,2},{12,4},{14,6},{16,24},{18,... | collective-permute-start | bytes 55304 | tf_op jit(solution)/shard_map/ppermute | solution.py:571
  329.9 41.4 %collective-permute-start.31 = (f32[1,4608]{1,0:T(1,128)S(1)}, f32[1,4608]{1,0:T(1,128)S(1)}, u32[]{:S(2)}, u32[]{:S(2)}) collective-permute-start(f32[1,4608]{1,0:T(1,128)S(1)} %add.138), channel_id=1, source_target_pairs={{0,16},{2,18},{4,20},{6,22},{8,24},{10,26},{12,28},{14,30},{16,0},... | collective-permute-start | bytes 55304 | tf_op jit(solution)/shard_map/ppermute | solution.py:571
  336.0 15.7 %collective-permute-start.12 = (bf16[4,80,512]{2,1,0:T(8,128)(2,1)S(1)}, bf16[4,80,512]{2,1,0:T(8,128)(2,1)S(1)}, u32[]{:S(2)}, u32[]{:S(2)}) collective-permute-start(bf16[4,80,512]{2,1,0:T(8,128)(2,1)S(1)} %get-tuple-element.109), channel_id=1, source_target_pairs={{0,2},{2,0},{4,6},{6,4},{8,10},{10,8},{12,14},{14,12},{16,18},{18,... | collective-permute-start | bytes 983048 | tf_op jit(solution)/shard_map/ppermute | solution.py:571
  337.4 14.2 %collective-permute-start.13 = (bf16[4,80,512]{2,1,0:T(8,128)(2,1)S(1)}, bf16[4,80,512]{2,1,0:T(8,128)(2,1)S(1)}, u32[]{:S(2)}, u32[]{:S(2)}) collective-permute-start(bf16[4,80,512]{2,1,0:T(8,128)(2,1)S(1)} %get-tuple-element.111), channel_id=1, source_target_pairs={{0,4},{2,6},{4,0},{6,2},{8,12},{10,14},{12,8},{14,10},{16,20},{18,... | collective-permute-start | bytes 983048 | tf_op jit(solution)/shard_map/ppermute | solution.py:571
  338.0 13.7 %collective-permute-start.14 = (bf16[4,80,512]{2,1,0:T(8,128)(2,1)S(1)}, bf16[4,80,512]{2,1,0:T(8,128)(2,1)S(1)}, u32[]{:S(2)}, u32[]{:S(2)}) collective-permute-start(bf16[4,80,512]{2,1,0:T(8,128)(2,1)S(1)} %get-tuple-element.110), channel_id=1, source_target_pairs={{0,6},{2,4},{4,2},{6,0},{8,14},{10,12},{12,10},{14,8},{16,22},{18,... | collective-permute-start | bytes 983048 | tf_op jit(solution)/shard_map/ppermute | solution.py:571
  351.9 13.7 %collective-permute-start.15 = (bf16[80,512]{1,0:T(8,128)(2,1)S(1)}, bf16[80,512]{1,0:T(8,128)(2,1)S(1)}, u32[]{:S(2)}, u32[]{:S(2)}) collective-permute-start(bf16[80,512]{1,0:T(8,128)(2,1)S(1)} %get-tuple-element.118), channel_id=1, source_target_pairs={{0,8},{2,10},{4,12},{6,14},{8,0},{10,2},{12,4},{14,6},{16,24},{18,... | collective-permute-start | bytes 245768 | tf_op jit(solution)/shard_map/ppermute | solution.py:571
  354.5 11.2 %collective-permute-start.16 = (bf16[80,512]{1,0:T(8,128)(2,1)S(1)}, bf16[80,512]{1,0:T(8,128)(2,1)S(1)}, u32[]{:S(2)}, u32[]{:S(2)}) collective-permute-start(bf16[80,512]{1,0:T(8,128)(2,1)S(1)} %get-tuple-element.120), channel_id=1, source_target_pairs={{0,16},{2,18},{4,20},{6,22},{8,24},{10,26},{12,28},{14,30},{16,0},... | collective-permute-start | bytes 245768 | tf_op jit(solution)/shard_map/ppermute | solution.py:571
  356.2 9.5 %collective-permute-start.17 = (bf16[80,512]{1,0:T(8,128)(2,1)S(1)}, bf16[80,512]{1,0:T(8,128)(2,1)S(1)}, u32[]{:S(2)}, u32[]{:S(2)}) collective-permute-start(bf16[80,512]{1,0:T(8,128)(2,1)S(1)} %get-tuple-element.119), channel_id=1, source_target_pairs={{0,24},{2,26},{4,28},{6,30},{8,16},{10,18},{12,20},{14,22},{16,8},... | collective-permute-start | bytes 245768 | tf_op jit(solution)/shard_map/ppermute | solution.py:571
  366.8 14.1 %collective-permute-start.21 = (bf16[4,16,512]{2,1,0:T(8,128)(2,1)S(1)}, bf16[4,16,512]{2,1,0:T(8,128)(2,1)S(1)}, u32[]{:S(2)}, u32[]{:S(2)}) collective-permute-start(bf16[4,16,512]{2,1,0:T(8,128)(2,1)S(1)} %get-tuple-element.130), channel_id=1, source_target_pairs={{0,8},{2,10},{4,12},{6,14},{8,0},{10,2},{12,4},{14,6},{16,24},{18,... | collective-permute-start | bytes 196616 | tf_op jit(solution)/shard_map/ppermute | solution.py:571
  367.4 13.5 %collective-permute-start.22 = (bf16[4,16,512]{2,1,0:T(8,128)(2,1)S(1)}, bf16[4,16,512]{2,1,0:T(8,128)(2,1)S(1)}, u32[]{:S(2)}, u32[]{:S(2)}) collective-permute-start(bf16[4,16,512]{2,1,0:T(8,128)(2,1)S(1)} %get-tuple-element.129), channel_id=1, source_target_pairs={{0,16},{2,18},{4,20},{6,22},{8,24},{10,26},{12,28},{14,30},{16,0},... | collective-permute-start | bytes 196616 | tf_op jit(solution)/shard_map/ppermute | solution.py:571
  369.8 11.1 %collective-permute-start.23 = (bf16[4,16,512]{2,1,0:T(8,128)(2,1)S(1)}, bf16[4,16,512]{2,1,0:T(8,128)(2,1)S(1)}, u32[]{:S(2)}, u32[]{:S(2)}) collective-permute-start(bf16[4,16,512]{2,1,0:T(8,128)(2,1)S(1)} %get-tuple-element.128), channel_id=1, source_target_pairs={{0,24},{2,26},{4,28},{6,30},{8,16},{10,18},{12,20},{14,22},{16,8},... | collective-permute-start | bytes 196616 | tf_op jit(solution)/shard_map/ppermute | solution.py:571
  371.9 12.6 %copy-start.8 = (f32[4608]{0:T(1024)S(1)}, f32[4608]{0:T(1024)}, u32[]{:S(2)}) copy-start(f32[4608]{0:T(1024)} %param.17) | copy-start | bytes 55300
  371.9 12.6 %copy-start.9 = (f32[4608]{0:T(1024)S(1)}, f32[4608]{0:T(1024)}, u32[]{:S(2)}) copy-start(f32[4608]{0:T(1024)} %param.18) | copy-start | bytes 55300
  372.0 12.6 %copy-start.10 = (f32[4608]{0:T(1024)S(1)}, f32[4608]{0:T(1024)}, u32[]{:S(2)}) copy-start(f32[4608]{0:T(1024)} %param.19) | copy-start | bytes 55300
  381.0 13.2 %collective-permute-start.24 = (bf16[4,16,512]{2,1,0:T(8,128)(2,1)S(1)}, bf16[4,16,512]{2,1,0:T(8,128)(2,1)S(1)}, u32[]{:S(2)}, u32[]{:S(2)}) collective-permute-start(bf16[4,16,512]{2,1,0:T(8,128)(2,1)S(1)} %get-tuple-element.126), channel_id=1, source_target_pairs={{0,2},{2,0},{4,6},{6,4},{8,10},{10,8},{12,14},{14,12},{16,18},{18,... | collective-permute-start | bytes 196616 | tf_op jit(solution)/shard_map/ppermute | solution.py:571
  381.7 12.4 %collective-permute-start.25 = (bf16[4,16,512]{2,1,0:T(8,128)(2,1)S(1)}, bf16[4,16,512]{2,1,0:T(8,128)(2,1)S(1)}, u32[]{:S(2)}, u32[]{:S(2)}) collective-permute-start(bf16[4,16,512]{2,1,0:T(8,128)(2,1)S(1)} %get-tuple-element.125), channel_id=1, source_target_pairs={{0,4},{2,6},{4,0},{6,2},{8,12},{10,14},{12,8},{14,10},{16,20},{18,... | collective-permute-start | bytes 196616 | tf_op jit(solution)/shard_map/ppermute | solution.py:571
  383.4 10.8 %collective-permute-start.26 = (bf16[4,16,512]{2,1,0:T(8,128)(2,1)S(1)}, bf16[4,16,512]{2,1,0:T(8,128)(2,1)S(1)}, u32[]{:S(2)}, u32[]{:S(2)}) collective-permute-start(bf16[4,16,512]{2,1,0:T(8,128)(2,1)S(1)} %get-tuple-element.124), channel_id=1, source_target_pairs={{0,6},{2,4},{4,2},{6,0},{8,14},{10,12},{12,10},{14,8},{16,22},{18,... | collective-permute-start | bytes 196616 | tf_op jit(solution)/shard_map/ppermute | solution.py:571
  385.2 9.7 %copy-start.5 = (f32[1,256,512]{2,1,0:T(8,128)S(1)}, f32[1,256,512]{2,1,0:T(8,128)}, u32[]{:S(2)}) copy-start(f32[1,256,512]{2,1,0:T(8,128)} %param.15) | copy-start | bytes 1572868
  (7 other events, 39.0 us)
Sparse Core Ops, SparseCore 0:
  10.9 88.4 all-gather.2

commit v4 on v3

--- a/solution.py
+++ b/solution.py
@@ -70,8 +70,8 @@
     return pl.BlockSpec(shape, lambda step, *_: zeros)
 
 
-def norm_kernel(x_ref, xh_ref, mean_ref):
-    normal, _ = normalize(x_ref[0].astype(F32))
+def norm_kernel(x_ref, xh_ref, scale_ref, mean_ref):
+    normal, scale_ref[0] = normalize(x_ref[0].astype(F32))
     xh_ref[0] = normal.astype(BF16)
     for row in range(mean_ref.shape[1]):
         part = normal[row * ROW : (row + 1) * ROW]
@@ -85,9 +85,10 @@
         norm_kernel,
         grid=(images,),
         in_specs=[tile_spec(count, D)],
-        out_specs=[tile_spec(count, D), tile_spec(rows, D)],
+        out_specs=[tile_spec(count, D), tile_spec(count, 1), tile_spec(rows, D)],
         out_shape=[
             jax.ShapeDtypeStruct((images, count, D), BF16),
+            jax.ShapeDtypeStruct((images, count, 1), F32),
             jax.ShapeDtypeStruct((images, rows, D), F32),
         ],
         compiler_params=pltpu.CompilerParams(vmem_limit_bytes=60 * MIB),
@@ -121,8 +122,9 @@
 
 
 def attend_kernel(
-    parts, place, xh_ref, mean_ref, g_ref, s_ref, *refs
+    parts, place, xh_ref, mean_ref, params_ref, *refs
 ):
+    g_ref, s_ref = params_ref.at[:, 0:D], params_ref.at[:, D : 2 * D]
     part_refs, refs = refs[:parts], refs[parts:]
     q_ref, k_ref, v_ref, e_ref, o_ref, li_ref, sk_ref, sv_ref, bias_ref, w_ref = refs
     rows = xh_ref.shape[1] // ROW
@@ -132,9 +134,11 @@
     def _():
         query = lax.broadcasted_iota(jnp.int32, (ROW, KEYS), 0)
         key = lax.broadcasted_iota(jnp.int32, (ROW, KEYS), 1)
+        summary = jnp.maximum(key - ROW, 0)
+        image_row = (place[0] ^ lax.div(summary, rows)) * rows + lax.rem(summary, rows)
         for row in range(rows):
             own = jnp.where(key <= query, 0.0, -1e30)
-            earlier = jnp.where(key - ROW < first_row + row, math.log2(ROW), -1e30)
+            earlier = jnp.where(image_row < first_row + row, math.log2(ROW), -1e30)
             bias_ref[row] = jnp.where(key < ROW, own, earlier)
         if parts == 1:
             w_ref[...] = part_refs[0][...]
@@ -184,7 +188,7 @@
             li_ref[0, here, lanes] = inverse.astype(BF16)
 
 
-def attend_call(place, normal, mean_all, gain, shift, parts):
+def attend_call(place, normal, mean_all, params, parts):
     images, count, _ = normal.shape
     rows = count // ROW
     tokens_shape = jax.ShapeDtypeStruct((images, count, D), BF16)
@@ -194,7 +198,7 @@
             num_scalar_prefetch=1,
             grid=(images,),
             in_specs=[
-                tile_spec(count, D), tile_spec(ROWS_IMG, D), whole_spec((1, D)), whole_spec((1, D)),
+                tile_spec(count, D), tile_spec(ROWS_IMG, D), whole_spec(params.shape),
             ]
             + [whole_spec(part.shape) for part in parts],
             out_specs=[tile_spec(count, D)] * 3
@@ -215,15 +219,19 @@
             flops=images * count * D * D * 10, bytes_accessed=images * count * D * 20, transcendentals=0
         ),
         name="attend",
-    )(place, normal, mean_all, gain, shift, *parts)
+    )(place, normal, mean_all, params, *parts)
 
 
 def ff_kernel(
-    pieces, owner, place, x_ref, o_ref, cot_ref, li_ref, g_ref, s_ref, bu_ref,
+    pieces, finished, owner, place, x_ref, o_ref, cot_ref, li_ref, params_ref,
     wo_ref, u0_ref, u1_ref, u2_ref, u3_ref, d0_ref, d1_ref, d2_ref, d3_ref,
-    act_ref, h_ref, dr_ref, do_ref, gg_ref, gs_ref, gbu_ref, gbd_ref, *refs
+    out_ref, act_ref, h_ref, dr_ref, do_ref, small_ref, *refs
 ):
-    grads_refs, (acc_ref, xh_ref, da_ref) = refs[:-3], refs[-3:]
+    grads_refs, (acc_ref, xh_ref, dp_ref) = refs[:-3], refs[-3:]
+    gg_ref, gs_ref = small_ref.at[:, 0:D], small_ref.at[:, D : 2 * D]
+    gbu_ref, gbd_ref = small_ref.at[:, 2 * D : 2 * D + FF], small_ref.at[:, 2 * D + FF :]
+    g_ref, s_ref = params_ref.at[:, 2 * D : 3 * D], params_ref.at[:, 3 * D : 4 * D]
+    bu_ref, bd_ref = params_ref.at[:, 4 * D : 4 * D + FF], params_ref.at[:, 4 * D + FF :]
     step = pl.program_id(0)
     ups = (u0_ref, u1_ref, u2_ref, u3_ref)
     downs = (d0_ref, d1_ref, d2_ref, d3_ref)
@@ -231,10 +239,7 @@
     @pl.when(step == 0)
     def _():
         acc_ref[...] = jnp.zeros_like(acc_ref)
-        gg_ref[...] = jnp.zeros_like(gg_ref)
-        gs_ref[...] = jnp.zeros_like(gs_ref)
-        gbu_ref[...] = jnp.zeros_like(gbu_ref)
-        gbd_ref[...] = jnp.zeros_like(gbd_ref)
+        small_ref[...] = jnp.zeros_like(small_ref)
 
     hidden = x_ref[0].astype(F32) + dot(o_ref[0], wo_ref[0])
     normal, spread = normalize(hidden)
@@ -246,28 +251,41 @@
     cot_t = cot.T
     c_one = math.sqrt(2.0 / math.pi)
     c_two = c_one * 0.044715
-    for block in range(NF):
-        w_up = ups[block][0]
-        w_down = downs[block][0]
-        pre = dot(a2, w_up) + bu_ref[:, block * D : (block + 1) * D]
-        d_act = dot_nt(cot, w_down)
+    width = D // 2
+    ones = jnp.ones((16, a2_t.shape[1]), BF16)
+    a2_ones = jnp.concatenate([a2_t, ones], 0)
+
+    def first_products(start):
+        block, inside = start // D, slice(start % D, start % D + width)
+        pre = dot(a2, ups[block][0, :, inside]) + bu_ref[:, start : start + width]
+        return pre, dot_nt(cot, downs[block][0, inside, :])
+
+    following = first_products(0)
+    for start in range(0, FF, width):
+        block, inside, columns = start // D, slice(start % D, start % D + width), slice(start, start + width)
+        pre, d_act = following
+        if start + width < FF:
+            following = first_products(start + width)
         square = pre * pre
         half = 0.5 + 0.5 * jnp.tanh(pre * (c_one + c_two * square))
         act = pre * half
         slope = half + act * (1.0 - half) * (2.0 * c_one + (6.0 * c_two) * square)
         act = act.astype(BF16)
-        d_pre = d_act * slope
-        gbu_ref[:, block * D : (block + 1) * D] += jnp.sum(d_pre, 0, keepdims=True)
-        d_pre = d_pre.astype(BF16)
-        act_ref[0, :, block * D : (block + 1) * D] = act
-        part = dot_nt(d_pre, w_up)
-        if block == 0:
-            da_ref[...] = part
-        else:
-            da_ref[...] += part
-        acc_ref[1 + block] += dot(a2_t, d_pre)
-        acc_ref[1 + NF + block] += dot(cot_t, act)
-    d_a2 = da_ref[...]
+        d_pre = (d_act * slope).astype(BF16)
+        act_ref[0, :, columns] = act
+        dp_ref[:, columns] = d_pre
+        part = dot(a2_ones, d_pre)
+        acc_ref[1 + block, :, inside] += part[:D]
+        gbu_ref[:, columns] += part[D : D + 1]
+        acc_ref[1 + NF + block, :, inside] += dot(cot_t, act)
+
+    @pl.when(step < finished)
+    def _():
+        output(act_ref, h_ref, bd_ref, downs, out_ref)
+
+    d_a2 = dot_nt(dp_ref[:, 0:D], ups[0][0])
+    for block in range(1, NF):
+        d_a2 += dot_nt(dp_ref[:, block * D : (block + 1) * D], ups[block][0])
     normal = xh_ref[...]
     gs_ref[...] += jnp.sum(d_a2, 0, keepdims=True)
     gg_ref[...] += jnp.sum(d_a2 * normal, 0, keepdims=True)
@@ -299,52 +317,58 @@
     return [(inner, outer, blocks * (D // narrow // inner // outer), D)] * narrow
 
 
-def ff_call(owner, place, groups, tokens, attended, cotangent, inverse, gain, shift, bias_up, slots):
+def ff_call(owner, place, groups, finished, tokens, attended, cotangent, inverse, params, slots):
     images, count, _ = tokens.shape
     tokens_shape = jax.ShapeDtypeStruct((images, count, D), BF16)
     blocks = 1 + 2 * NF
     grads = grad_shapes(groups, blocks)
     return pl.pallas_call(
-        functools.partial(ff_kernel, groups is not None),
+        functools.partial(ff_kernel, groups is not None, finished),
         grid_spec=pltpu.PrefetchScalarGridSpec(
             num_scalar_prefetch=2,
             grid=(images,),
             in_specs=[tile_spec(count, D)] * 4
-            + [whole_spec((1, D)), whole_spec((1, D)), whole_spec((1, FF))]
+            + [whole_spec(params.shape)]
             + [weight_spec(3 + block) for block in range(blocks)],
-            out_specs=[tile_spec(count, FF)]
-            + [tile_spec(count, D)] * 3
-            + [out_whole((1, D)), out_whole((1, D)), out_whole((1, FF)), out_whole((1, D))]
+            out_specs=[
+                pl.BlockSpec((1, count, D), lambda step, *_: (jnp.minimum(step, finished - 1), 0, 0)),
+                pl.BlockSpec((1, count, FF), lambda step, *_: (jnp.maximum(step - finished, 0), 0, 0)),
+                pl.BlockSpec((1, count, D), lambda step, *_: (jnp.maximum(step - finished, 0), 0, 0)),
+            ]
+            + [tile_spec(count, D)] * 2
+            + [out_whole((1, 3 * D + FF))]
             + [out_whole(shape) for shape in grads],
             scratch_shapes=[
                 pltpu.VMEM((blocks, D, D), F32),
                 pltpu.VMEM((count, D), F32),
-                pltpu.VMEM((count, D), F32),
+                pltpu.VMEM((count, FF), BF16),
             ],
         ),
-        out_shape=[jax.ShapeDtypeStruct((images, count, FF), BF16)]
-        + [tokens_shape] * 3
-        + [
-            jax.ShapeDtypeStruct((1, D), F32),
-            jax.ShapeDtypeStruct((1, D), F32),
-            jax.ShapeDtypeStruct((1, FF), F32),
-            jax.ShapeDtypeStruct((1, D), F32),
+        out_shape=[
+            tokens_shape,
+            jax.ShapeDtypeStruct((images - finished, count, FF), BF16),
+            jax.ShapeDtypeStruct((images - finished, count, D), BF16),
         ]
+        + [tokens_shape] * 2
+        + [jax.ShapeDtypeStruct((1, 3 * D + FF), F32)]
         + [jax.ShapeDtypeStruct(shape, BF16) for shape in grads],
         compiler_params=pltpu.CompilerParams(vmem_limit_bytes=60 * MIB),
         cost_estimate=pl.CostEstimate(
             flops=images * count * D * D * 46, bytes_accessed=images * count * D * 22, transcendentals=0
         ),
         name="feed_forward",
-    )(owner, place, tokens, attended, cotangent, inverse, gain, shift, bias_up, *([slots] * blocks))
-
-
-def down_kernel(owner, act_ref, h_ref, b_ref, d0_ref, d1_ref, d2_ref, d3_ref, *refs):
-    out_ref = refs[-1]
+    )(owner, place, tokens, attended, cotangent, inverse, params, *([slots] * blocks))
+
+
+def output(act_ref, h_ref, b_ref, downs, out_ref):
     total = h_ref[0].astype(F32) + b_ref[...]
-    for block, down in enumerate((d0_ref, d1_ref, d2_ref, d3_ref)):
+    for block, down in enumerate(downs):
         total += dot(act_ref[0, :, block * D : (block + 1) * D], down[0])
     out_ref[0] = total.astype(BF16)
+
+
+def down_kernel(owner, act_ref, h_ref, params_ref, d0_ref, d1_ref, d2_ref, d3_ref, before_ref, out_ref):
+    output(act_ref, h_ref, params_ref.at[:, 4 * D + FF :], (d0_ref, d1_ref, d2_ref, d3_ref), out_ref)
 
 
 def image_spec(start, *tail):
@@ -352,50 +376,44 @@
     return pl.BlockSpec((1,) + tail, lambda step, *_: (start + step,) + zeros)
 
 
-def down_call(start, stop, before, owner, act, hidden, bias, slots):
-    images, count, _ = hidden.shape
-    earlier = [] if before is None else [before]
+def down_call(before, owner, act, hidden, params, slots):
+    images, count, _ = before.shape
+    left = hidden.shape[0]
     return pl.pallas_call(
         down_kernel,
         grid_spec=pltpu.PrefetchScalarGridSpec(
             num_scalar_prefetch=1,
-            grid=(stop - start,),
-            in_specs=[image_spec(start, count, FF), image_spec(start, count, D), whole_spec((1, D))]
+            grid=(left,),
+            in_specs=[tile_spec(count, FF), tile_spec(count, D), whole_spec(params.shape)]
             + [weight_spec(4 + NF + block) for block in range(NF)]
-            + [pl.BlockSpec(memory_space=pl.ANY)] * len(earlier),
-            out_specs=image_spec(start, count, D),
+            + [pl.BlockSpec(memory_space=pl.ANY)],
+            out_specs=image_spec(images - left, count, D),
         ),
         out_shape=jax.ShapeDtypeStruct((images, count, D), BF16),
-        input_output_aliases={4 + NF: 0} if earlier else {},
+        input_output_aliases={4 + NF: 0},
         compiler_params=pltpu.CompilerParams(vmem_limit_bytes=60 * MIB),
         cost_estimate=pl.CostEstimate(
-            flops=(stop - start) * count * D * D * 8,
-            bytes_accessed=(stop - start) * count * D * 12,
-            transcendentals=0,
+            flops=left * count * D * D * 8, bytes_accessed=left * count * D * 12, transcendentals=0
         ),
         name="down",
-    )(owner, act, hidden, bias, *([slots] * NF), *earlier)
-
-
-def back_kernel(first, last, start, pieces, owner, place, *refs):
-    (q_ref, k_ref, v_ref, o_ref, do_ref, e_ref, xh_ref, sk_ref, sv_ref, mean_ref, g_ref, s_ref) = refs[:12]
-    wq_ref, wk_ref, wv_ref = refs[12:15]
-    refs = refs[15:]
-    if not first:
-        old_acc_ref, old_gg_ref, old_gs_ref = refs[:3]
-        refs = refs[4:]
-    dlow_ref, dm_ref, acc_ref, gg_ref, gs_ref = refs[:5]
-    grads_refs = refs[5:-3]
-    grad_ref, dsk_ref, dsv_ref = refs[-3:]
+    )(owner, act, hidden, params, *([slots] * NF), before)
+
+
+def back_kernel(pieces, owner, place, *refs):
+    (q_ref, k_ref, v_ref, o_ref, do_ref, e_ref, xh_ref, sk_ref, sv_ref, mean_ref, params_ref) = refs[:11]
+    wq_ref, wk_ref, wv_ref = refs[11:14]
+    g_ref, s_ref = params_ref.at[:, 0:D], params_ref.at[:, D : 2 * D]
+    dlow_ref, dm_ref, small_ref, *grads_refs = refs[14:-4]
+    gg_ref, gs_ref = small_ref.at[:, 0:D], small_ref.at[:, D : 2 * D]
+    acc_ref, grad_ref, dsk_ref, dsv_ref = refs[-4:]
     step = pl.program_id(0)
     rows = q_ref.shape[1] // ROW
     scale = 1.0 / math.sqrt(HD)
 
     @pl.when(step == 0)
     def _():
-        acc_ref[...] = jnp.zeros_like(acc_ref) if first else old_acc_ref[...]
-        gg_ref[...] = jnp.zeros_like(gg_ref) if first else old_gg_ref[...]
-        gs_ref[...] = jnp.zeros_like(gs_ref) if first else old_gs_ref[...]
+        acc_ref[...] = jnp.zeros_like(acc_ref)
+        small_ref[...] = jnp.zeros_like(small_ref)
 
     sum_k = sk_ref[0]
     sum_v = sv_ref[0]
@@ -451,7 +469,7 @@
 
     @pl.when(step == pl.num_programs(0) - 1)
     def _():
-        mean_x = mean_ref[start : start + dm_ref.shape[0]].reshape(-1, D).astype(F32)
+        mean_x = mean_ref[...].reshape(-1, D).astype(F32)
         mean_t = (mean_x * g_ref[...] + s_ref[...]).astype(BF16).T
         all_k = dsk_ref[...].reshape(-1, D)
         all_v = dsv_ref[...].reshape(-1, D)
@@ -461,75 +479,55 @@
         dm_ref[...] = d_mean.astype(BF16).reshape(dm_ref.shape)
         gs_ref[...] += jnp.sum(d_mean, 0, keepdims=True)
         gg_ref[...] += jnp.sum(d_mean * mean_x, 0, keepdims=True)
-        if last and pieces:
+        if pieces:
             write_pieces(place, grads_refs, lambda block, here: acc_ref[here, block * D : (block + 1) * D])
-        elif last:
+        else:
             for block in range(3):
                 grads_refs[0][block] = acc_ref[:, block * D : (block + 1) * D].astype(BF16)
 
 
-def back_call(start, stop, before, owner, place, groups, operands, gain, shift, slots):
+def back_call(owner, place, groups, operands, params, slots):
     images, count, _ = operands[0].shape
     rows = count // ROW
-    first, last = start == 0, stop == images
-
-    at = functools.partial(image_spec, start)
-    grads = grad_shapes(groups, 3) if last else []
-    in_specs = (
-        [at(count, D)] * 5
-        + [at(rows, HEADS, ROW, KEYS), at(count, D), at(ROWS_IMG, D), at(ROWS_IMG, D)]
-        + [whole_spec((images, ROWS_IMG, D))]
-        + [whole_spec((1, D)), whole_spec((1, D))]
-        + [weight_spec(block) for block in range(3)]
-    )
-    inputs = [owner, place, *operands, gain, shift, slots, slots, slots]
-    aliases = {}
-    if not first:
-        d_low, *sums = before
-        in_specs += [whole_spec((D, 3 * D)), whole_spec((1, D)), whole_spec((1, D)), pl.BlockSpec(memory_space=pl.ANY)]
-        inputs += [*sums, d_low]
-        aliases = {len(inputs) - 1: 0}
+    grads = grad_shapes(groups, 3)
     return pl.pallas_call(
-        functools.partial(back_kernel, first, last, start, groups is not None),
+        functools.partial(back_kernel, groups is not None),
         grid_spec=pltpu.PrefetchScalarGridSpec(
             num_scalar_prefetch=2,
-            grid=(stop - start,),
-            in_specs=in_specs,
-            out_specs=[
-                at(count, D), out_whole((stop - start, ROWS_IMG, D)), out_whole((D, 3 * D)),
-                out_whole((1, D)), out_whole((1, D)),
-            ]
+            grid=(images,),
+            in_specs=[tile_spec(count, D)] * 5
+            + [tile_spec(rows, HEADS, ROW, KEYS), tile_spec(count, D)]
+            + [tile_spec(ROWS_IMG, D)] * 2
+            + [whole_spec((images, ROWS_IMG, D)), whole_spec(params.shape)]
+            + [weight_spec(block) for block in range(3)],
+            out_specs=[tile_spec(count, D), out_whole((images, ROWS_IMG, D)), out_whole((1, 2 * D))]
             + [out_whole(shape) for shape in grads],
             scratch_shapes=[
+                pltpu.VMEM((D, 3 * D), F32),
                 pltpu.VMEM((count, 3 * D), BF16),
-                pltpu.VMEM((stop - start, ROWS_IMG, D), BF16),
-                pltpu.VMEM((stop - start, ROWS_IMG, D), BF16),
+                pltpu.VMEM((images, ROWS_IMG, D), BF16),
+                pltpu.VMEM((images, ROWS_IMG, D), BF16),
             ],
         ),
         out_shape=[
             jax.ShapeDtypeStruct((images, count, D), BF16),
-            jax.ShapeDtypeStruct((stop - start, ROWS_IMG, D), BF16),
-            jax.ShapeDtypeStruct((D, 3 * D), F32),
-            jax.ShapeDtypeStruct((1, D), F32),
-            jax.ShapeDtypeStruct((1, D), F32),
+            jax.ShapeDtypeStruct((images, ROWS_IMG, D), BF16),
+            jax.ShapeDtypeStruct((1, 2 * D), F32),
         ]
         + [jax.ShapeDtypeStruct(shape, BF16) for shape in grads],
-        input_output_aliases=aliases,
         compiler_params=pltpu.CompilerParams(vmem_limit_bytes=60 * MIB),
         cost_estimate=pl.CostEstimate(
-            flops=(stop - start) * count * D * D * 20,
-            bytes_accessed=(stop - start) * count * D * 24,
-            transcendentals=0,
+            flops=images * count * D * D * 20, bytes_accessed=images * count * D * 24, transcendentals=0
         ),
         name="attend_back",
-    )(*inputs)
-
-
-def last_kernel(x_ref, low_ref, dr_ref, dm_ref, g_ref, *refs):
-    out_ref = refs[-1]
+    )(owner, place, *operands, params, slots, slots, slots)
+
+
+def last_kernel(xh_ref, scale_ref, low_ref, dr_ref, dm_ref, params_ref, out_ref):
+    g_ref = params_ref.at[:, 0:D]
     for row in range(dm_ref.shape[1]):
         here = slice(row * ROW, (row + 1) * ROW)
-        normal, spread = normalize(x_ref[0, here, :].astype(F32))
+        normal, spread = xh_ref[0, here, :].astype(F32), scale_ref[0, here, :]
         total = low_ref[0, here, :].astype(F32) + dm_ref[0, row : row + 1, :] * (1.0 / ROW)
         d_normal = total * g_ref[...]
         middle = jnp.mean(d_normal, -1, keepdims=True)
@@ -537,26 +535,21 @@
         out_ref[0, here, :] = dr_ref[0, here, :].astype(F32) + spread * (d_normal - middle - normal * along)
 
 
-def last_call(start, stop, before, tokens, d_low, d_branch, d_mean, gain):
-    images, count, _ = tokens.shape
-    earlier = [] if before is None else [before]
+def last_call(normal, scale, d_low, d_branch, d_mean, params):
+    images, count, _ = normal.shape
     return pl.pallas_call(
         last_kernel,
-        grid=(stop - start,),
-        in_specs=[image_spec(start, count, D)] * 3
-        + [image_spec(start, count // ROW, D), whole_spec((1, D))]
-        + [pl.BlockSpec(memory_space=pl.ANY)] * len(earlier),
-        out_specs=image_spec(start, count, D),
+        grid=(images,),
+        in_specs=[tile_spec(count, D), tile_spec(count, 1), tile_spec(count, D), tile_spec(count, D)]
+        + [tile_spec(count // ROW, D), whole_spec(params.shape)],
+        out_specs=tile_spec(count, D),
         out_shape=jax.ShapeDtypeStruct((images, count, D), F32),
-        input_output_aliases={5: 0} if earlier else {},
         compiler_params=pltpu.CompilerParams(vmem_limit_bytes=60 * MIB),
         cost_estimate=pl.CostEstimate(
-            flops=(stop - start) * count * D * 20,
-            bytes_accessed=(stop - start) * count * D * 10,
-            transcendentals=0,
+            flops=images * count * D * 20, bytes_accessed=images * count * D * 11, transcendentals=0
         ),
         name="norm_one_back",
-    )(tokens, d_low, d_branch, d_mean, gain, *earlier)
+    )(normal, scale, d_low, d_branch, d_mean, params)
 
 
 def adamw_update(weight_now, gradient, first_moment, second_moment, decay_rate, step_rate):
@@ -571,13 +564,15 @@
     return lax.ppermute(value, axis, [(index, index ^ bit) for index in range(size)])
 
 
-def sum_everywhere(value):
-    for axis in ("narrow", "wide"):
-        bit = 1
-        while bit < lax.axis_size(axis):
-            value = value + swap(value, axis, bit)
-            bit *= 2
-    return value
+def sum_steps():
+    inner, outer = group_sizes(lax.axis_size("wide"))
+
+    def bits(axis, size, stride):
+        return [[(axis, stride << bit)] for bit in range(size.bit_length() - 1)]
+
+    near = bits("wide", inner, 1)
+    far = [[("wide", inner * distance) for distance in range(1, outer)]]
+    return bits("narrow", lax.axis_size("narrow"), 1) + near[:1] + far + near[1:]
 
 
 def join(value):
@@ -598,7 +593,7 @@
     mine = jnp.take(pieces, owners, axis=0)
     count, depth, _ = mine.shape
     joined = join(jnp.concatenate([mine.reshape(-1, D), means.reshape(-1, D)], 0))
-    mean_all = reorder(joined[:, count * depth :], "wide").reshape((wide,) + means.shape).swapaxes(0, 1)
+    mean_all = joined[:, count * depth :].reshape((wide,) + means.shape).swapaxes(0, 1)
     mean_all = mean_all.reshape(means.shape[0], -1, D)
     if whole_pieces:
         return [joined] + [swap(joined, "narrow", step) for step in range(1, narrow)], mean_all
@@ -658,12 +653,6 @@
     rows = count // ROW
     wide = lax.axis_size("wide")
     small = small_params.reshape(1, -1)
-    gain_one = small[:, 0:D]
-    shift_one = small[:, D : 2 * D]
-    gain_two = small[:, 2 * D : 3 * D]
-    shift_two = small[:, 3 * D : 4 * D]
-    bias_up = small[:, 4 * D : 4 * D + FF]
-    bias_down = small[:, 4 * D + FF :]
     low_master = master.astype(BF16)
     slots = lax.all_gather(low_master.reshape(-1, D), ("wide", "narrow"), axis=0, tiled=True)
     slots = slots.reshape(-1, D, D)
@@ -672,59 +661,56 @@
     depth = D // narrow // wide
     groups = (narrow, inner, outer) if depth % 16 == 0 and narrow > 1 else None
     me = lax.axis_index("wide")
+    names = owner_list[None, :] == jnp.arange(wide, dtype=jnp.int32)[:, None]
+    owned = jnp.any(names, 1)
+    block_of = jnp.argmax(names, 1)
     place = jnp.stack([me, lax.axis_index("narrow")]).astype(jnp.int32)
-    normal, means = norm_call(tokens)
+    normal, scale, means = norm_call(tokens)
     parts, mean_all = fetch_blocks(low_master, owner_list[:3], means.astype(BF16), groups is not None)
     queries, keys, values, weights, attended, inverse, sum_k, sum_v = attend_call(
-        place, normal, mean_all, gain_one, shift_one, parts
+        place, normal, mean_all, small, parts
     )
-    act, hidden, d_branch, d_out, gain_two_grad, shift_two_grad, bias_up_grad, bias_down_grad, *grads_late = ff_call(
-        owner_list, place, groups, tokens, attended, cotangent, inverse, gain_two, shift_two, bias_up, slots
+    half = images // 2
+    block_out, act, hidden, d_branch, d_out, late_small, *grads_late = ff_call(
+        owner_list, place, groups, images - half, tokens, attended, cotangent, inverse, small, slots
     )
-    quarter = images // 4
-    half = images // 2
-
-    late = piece_lists(grads_late, groups)
-    block_out = down_call(0, quarter, None, owner_list, act, hidden, bias_down, slots)
-    late = after(sum_narrow(late), block_out)
-    operands = (after(queries, late), keys, values, attended, d_out, weights, normal, sum_k, sum_v, mean_all)
-    back = functools.partial(
-        back_call, owner=owner_list, place=place, groups=groups, operands=operands, gain=gain_one,
-        shift=shift_one, slots=slots,
+
+    tie = lax.optimization_barrier
+    late, queries = tie((sum_narrow(piece_lists(grads_late, groups)), queries))
+    operands = (queries, keys, values, attended, d_out, weights, normal, sum_k, sum_v, mean_all)
+    d_low, d_mean, early_small, *grads_early = back_call(
+        owner_list, place, groups, operands, small, slots
     )
-    d_low, mean_first, *sums = back(0, half, None)
-    late, d_low, *sums = lax.optimization_barrier((sum_near(late), d_low, *sums))
-    late_shares = sum_far(late)
-    d_low, mean_second, _, gain_one_grad, shift_one_grad, *grads_early = back(half, images, [d_low] + sums)
-
-    d_mean = jnp.concatenate([mean_first, mean_second], 0).reshape(images, wide, rows, D).swapaxes(0, 1)
-    d_mean = by_group(reorder(d_mean.reshape(wide, -1, D), "wide"))
-    early = sum_narrow(piece_lists(grads_early, groups))
-    block_out = down_call(
-        quarter, images - quarter, block_out, owner_list, after(act, early), hidden, bias_down, slots
-    )
-    early = after(sum_near(jnp.concatenate([early, d_mean], 2)), block_out)
-    block_out = down_call(
-        images - quarter, images, block_out, owner_list, after(act, early), hidden, bias_down, slots
-    )
-    shares = after(sum_far(early), block_out)
+    late, early_small, *grads_early = tie((sum_near(late), early_small, *grads_early))
+    small_sums = jnp.concatenate([early_small, late_small], 1)
+    steps = sum_steps()
+
+    def small_step():
+        total = small_sums
+        for axis, distance in steps.pop(0) if steps else ():
+            total += swap(small_sums, axis, distance)
+        return total
+
+    d_mean = d_mean.reshape(images, wide, rows, D).swapaxes(0, 1).reshape(wide, -1, D)
+    d_mean = by_group(d_mean)
+    early, small_sums, act, late = tie((sum_narrow(piece_lists(grads_early, groups)), small_step(), act, late))
+    late = sum_far(late)
+    block_out = down_call(block_out, owner_list, act, hidden, small, slots)
+    early = sum_near(jnp.concatenate([early, d_mean], 2))
+    early, late, small_sums, block_out = tie((early, late, small_step(), block_out))
+    shares, small_sums = tie((sum_far(early), small_step()))
     own_mean = shares[3 * depth :].reshape(images, rows, D)
-    shares = jnp.concatenate([shares[: 3 * depth], late_shares], 0).reshape(-1, depth, D).astype(BF16)
-
-    slotted = jnp.zeros((wide, depth, D), BF16).at[owner_list ^ me].set(shares)
-    slotted = slotted.reshape(outer, inner, depth, D)
-    moved = jnp.stack([slotted[0]] + [swap(slotted[step], "wide", step * inner) for step in range(1, outer)], 1)
-    grad_tokens = last_call(0, half, None, tokens, d_low, d_branch, own_mean, gain_one)
-    moved, grad_tokens = lax.optimization_barrier((moved, grad_tokens))
-    moved = jnp.stack([moved[0]] + [swap(moved[step], "wide", step) for step in range(1, inner)], 1)
-    grad_tokens = last_call(half, images, grad_tokens, tokens, d_low, d_branch, own_mean, gain_one)
-    moved, grad_tokens = lax.optimization_barrier((moved, grad_tokens))
-    own_grad = reorder(moved.reshape(wide, depth, D), "wide").reshape(1, -1, D).astype(F32)
-    small_grad = sum_everywhere(
-        jnp.concatenate(
-            [gain_one_grad, shift_one_grad, gain_two_grad, shift_two_grad, bias_up_grad, bias_down_grad], 1
-        )
-    ).reshape(-1)
+    shares = jnp.concatenate([shares[: 3 * depth], late], 0).reshape(-1, depth, D).astype(BF16)
+
+    moved = jnp.where(owned[:, None, None], jnp.take(shares, block_of, axis=0), jnp.zeros((), BF16))
+    moved = lax.all_to_all(moved, "wide", 0, 0, tiled=True)
+    small_sums = small_step()
+    grad_tokens = last_call(normal, scale, d_low, d_branch, own_mean, small)
+    moved, small_sums, grad_tokens = tie((moved, small_sums, grad_tokens))
+    own_grad = moved.reshape(1, -1, D).astype(F32)
+    while steps:
+        small_sums = small_step()
+    small_grad = small_sums.reshape(-1)
     owns_slot = jnp.any(owner_list == me)
     slot_weight, slot_first, slot_second = adamw_update(
         master, own_grad, moment_one, moment_two, 0.1, RATE

time: 410 us -> 373 us (0.910); the launches traced: 404 us -> 372 us
  Pallas kernels: 276 us -> 254 us
  starting transfers between devices: 50.4 us -> 43.9 us
  local copies, waits for them, and re-layouts: 10.8 us -> 5.45 us
    pallas_call x3 -> x1, Pallas kernels: 28.3 us -> 12.4 us  [down_call(): pl.pallas_call(down_kernel, grid_spec=pltpu.PrefetchScalarGridSpec(num_sc...]
    ppermute x32 -> x27, starting transfers between devices: 42 us -> 31.2 us  [swap(): lax.ppermute(value, axis, [(index, index ^ bit) for index in range(size)])]
    pallas_call x5 -> x3, Pallas kernels: 204 us -> 196 us  [the longest x1 110 us: ff_call(): pl.pallas_call(functools.partial(ff_kernel, groups is not None, finished)...]
    all_to_all x0 -> x1, starting transfers between devices: none -> 4.29 us  [per_device(): moved = lax.all_to_all(moved, 'wide', 0, 0, tiled=True)]
    ppermute x32 -> x27, waiting for transfers between devices: 35.1 us -> 37.2 us  [swap(): lax.ppermute(value, axis, [(index, index ^ bit) for index in range(size)])]
  transfers between devices with their start and end apart: 34 -> 30, of which waited for: 7 -> 12; matrix products, arithmetic and copies ran while one was open for 4% -> 3% of each run, Pallas kernels for 32% -> 39%
where the time goes in v4:
time: 373 us; the launch traced here: 372 us
  Pallas kernels  254 us (68%)
  starting transfers between devices  43.9 us (12%)
  waiting for transfers between devices  37.3 us (10%)
  other arithmetic  17 us (5%)
  between operations  14.6 us (4%)
  local copies, waits for them, and re-layouts  5.45 us (1%)
    pallas_call x1, Pallas kernels, ff_call(): pl.pallas_call(functools.partial(ff_kernel, groups is not None, finished)...  110 us
    pallas_call x1, Pallas kernels, back_call(): pl.pallas_call(functools.partial(back_kernel, groups is not None), grid_s...  69.4 us
    ppermute x27, waiting for transfers between devices, swap(): lax.ppermute(value, axis, [(index, index ^ bit) for index in range(size)])  37.2 us
    pallas_call x1, Pallas kernels, attend_call(): pl.pallas_call(functools.partial(attend_kernel, len(parts)), grid_spec=pl...  35.4 us
    ppermute x27, starting transfers between devices, swap(): lax.ppermute(value, axis, [(index, index ^ bit) for index in range(size)])  31.2 us
    pallas_call x1, Pallas kernels, last_call(): pl.pallas_call(last_kernel, grid=(images,), in_specs=[tile_spec(count, D)...  16.6 us
    pallas_call x1, Pallas kernels, down_call(): pl.pallas_call(down_kernel, grid_spec=pltpu.PrefetchScalarGridSpec(num_sc...  12.4 us
    pallas_call x1, Pallas kernels, norm_call(): pl.pallas_call(norm_kernel, grid=(images,), in_specs=[tile_spec(count, D)...  10.2 us
  transfers between devices with their start and end apart: 30, of which 12 were waited for; matrix products, arithmetic and copies ran while one was open for 3% of the time, Pallas kernels for 39%

profile of v4, /device:TPU:0, one launch (start us, length us, event | category | flops | bytes accessed | tf_op | source)
XLA Modules:
  0.0 372.3 jit_solution(1684735794717544017)
XLA Ops:
  7.2 1.8 convert_element_type.112
  9.0 8.3 %all-to-all-start = ((bf16[16,16,512]{2,1,0:T(8,128)(2,1)}), bf16[16,16,512]{2,1,0:T(8,128)(2,1)S(1)}, u32[]{:S(2)}, u32[]{:S(2)}) async-start(bf16[16,16,512]{2,1,0:T(8,128)(2,1)} %bitcast.98), calls=%async_computation | async-start | bytes 524288 | tf_op jit(solution)/shard_map/all_to_all | solution.py:592
  17.3 0.7 compare_and_fusion.1
  18.2 10.2 %norm_one.1 = (bf16[8,768,512]{2,1,0:T(8,128)(2,1)}, f32[8,768,1]{2,1,0:T(8,128)}, f32[8,4,512]{2,1,0:T(4,128)}) custom-call(bf16[8,768,512]{2,1,0:T(8,128)(2,1)} %x_ref.3), custom_call_target="tpu_custom_call" | custom-call | flops 31457280 | bytes 12582912 | tf_op jit(solution)/shard_map/norm_one/pallas_call | solution.py:84
  28.3 0.9 convert_element_type.113
  29.9 2.0 collective-permute-start
  31.9 2.3 collective-permute-start.1
  34.4 2.4 collective-permute-done
  36.8 4.8 %collective-permute-done.1 = bf16[80,512]{1,0:T(8,128)(2,1)S(1)} collective-permute-done((bf16[80,512]{1,0:T(8,128)(2,1)S(1)}, bf16[80,512]{1,0:T(8,128)(2,1)S(1)}, u32[]{:S(2)}, u32[]{:S(2)}) %collective-permute-start.1) | collective-permute-done | bytes 81952 | tf_op jit(solution)/shard_map/ppermute | solution.py:564
  41.6 1.5 collective-permute-start.3
  43.1 1.1 collective-permute-start.4
  44.2 1.0 collective-permute-start.5
  45.1 13.2 %collective-permute-done.3 = bf16[4,80,512]{2,1,0:T(8,128)(2,1)S(1)} collective-permute-done((bf16[4,80,512]{2,1,0:T(8,128)(2,1)S(1)}, bf16[4,80,512]{2,1,0:T(8,128)(2,1)S(1)}, u32[]{:S(2)}, u32[]{:S(2)}) %collective-permute-start.3) | collective-permute-done | bytes 327712 | tf_op jit(solution)/shard_map/ppermute | solution.py:564
  58.3 6.6 %collective-permute-done.5 = bf16[4,80,512]{2,1,0:T(8,128)(2,1)S(1)} collective-permute-done((bf16[4,80,512]{2,1,0:T(8,128)(2,1)S(1)}, bf16[4,80,512]{2,1,0:T(8,128)(2,1)S(1)}, u32[]{:S(2)}, u32[]{:S(2)}) %collective-permute-start.5) | collective-permute-done | bytes 327712 | tf_op jit(solution)/shard_map/ppermute | solution.py:564
  65.2 0.8 reshape.110.params_ref.refs_10_
  66.0 0.7 pad_add_fusion.place
  67.0 0.9 reshape.109.mean_ref.refs_9_
  68.4 35.4 %attend.1 = (bf16[8,768,512]{2,1,0:T(8,128)(2,1)}, bf16[8,768,512]{2,1,0:T(8,128)(2,1)}, bf16[8,768,512]{2,1,0:T(8,128)(2,1)}, bf16[8,4,8,192,256]{4,3,2,1,0:T(8...) custom-call(s32[2]{0:T(128)} %pad_add_fusion.place, ...), custom_call_target="tpu_custom_call" | custom-call | flops 16106127360 | bytes 62914560 | tf_op jit(solution)/shard_map/attend/pallas_call | solution.py:195
  103.8 110.1 %feed_forward.1 = (bf16[8,768,512]{2,1,0:T(8,128)(2,1)}, bf16[4,768,2048]{2,1,0:T(8,128)(2,1)}, bf16[4,768,512]{2,1,0:T(8,128)(2,1)}, bf16[8,768,512]{2,1,0:T(8,...) custom-call(s32[12]{0:T(128)} %owner.5, ...), custom_call_target="tpu_custom_call" | custom-call | flops 74088185856 | bytes 69206016 | tf_op jit(solution)/shard_map/feed_forward/pallas_call | solution.py:325
  215.2 3.5 collective-permute-done.7
  218.7 2.4 add_convert_fusion
  221.3 1.1 collective-permute-start.8
  222.4 2.4 collective-permute-start.9
  224.8 69.4 %attend_back.1 = (bf16[8,768,512]{2,1,0:T(8,128)(2,1)}, bf16[8,64,512]{2,1,0:T(8,128)(2,1)}, f32[1,1024]{1,0:T(1,128)}, bf16[4,4,48,512]{3,2,1,0:T(8,128)(2,1)}, bf16[4,4,48,512]{3,2,1,0:T(8,128)(2,1)}) custom-call(s32[12]{0:T(128)} %owner.5, s32[2]{0:T(128)} %pad_add_fusion.place, bf16[8,768,512]{2,1,0:T(8,128)(2,1)} %get-tuple-element.60.refs_0_, ...), custom_call_target="tpu_custom_call" | custom-call | flops 32212254720 | bytes 75497472 | tf_op jit(solution)/shard_map/attend_back/pallas_call | solution.py:493
  294.3 1.8 fusion.2
  297.0 1.6 collective-permute-done.12
  298.9 0.7 slice_bitcast_fusion.5
  299.6 1.8 collective-permute-start.16
  302.4 0.8 collective-permute-start.17
  303.1 1.6 collective-permute-start.18
  304.8 1.9 collective-permute-start.13
  306.9 1.5 collective-permute-start.15
  308.4 12.4 %down.1 = bf16[8,768,512]{2,1,0:T(8,128)(2,1)} custom-call(s32[12]{0:T(128)} %owner.5, bf16[4,768,2048]{2,1,0:T(8,128)(2,1)} %get-tuple-element.80.act_ref, bf16[4,768,512]{2,1,0:T(8,128)(2,1)} %get-tuple-element.81.h_ref, f32[1,4608]{1,0:T(1,128)} %reshape.110.params_ref.refs_10_, bf16[16,512,512]{2,1,0:T(8,128)(2,1)} %bitcast.89, ...), custom_call_target="tpu_custom_call", output_to_operand_aliasing={{}: (8, {})} | custom-call | flops 6442450944 | bytes 18874368 | tf_op jit(solution)/shard_map/down/pallas_call | solution.py:382
  320.9 1.1 fusion.18
  322.2 1.1 fusion.5
  323.3 1.1 collective-permute-start.23
  324.4 1.7 collective-permute-start.24
  326.0 1.7 collective-permute-start.25
  328.0 2.6 collective-permute-start.21
  330.5 1.7 collective-permute-start.22
  332.3 1.7 collective-permute-done.20
  334.0 0.9 collective-permute-done.21
  334.9 1.9 collective-permute-done.22
  337.4 0.8 select_select_fusion
  338.2 4.3 %all-to-all-start.1 = ((bf16[16,16,512]{2,1,0:T(8,128)(2,1)}), bf16[16,16,512]{2,1,0:T(8,128)(2,1)S(1)}, u32[]{:S(2)}, u32[]{:S(2)}) async-start(bf16[16,16,512]{2,1,0:T(8,128)(2,1)} %select_select_fusion), calls=%async_computation.1 | async-start | bytes 524288 | tf_op jit(solution)/shard_map/all_to_all | solution.py:706
  342.5 1.9 collective-permute-start.26
  345.8 16.6 %norm_one_back.1 = f32[8,768,512]{2,1,0:T(8,128)} custom-call(bf16[8,768,512]{2,1,0:T(8,128)(2,1)} %get-tuple-element.52.xh_ref.refs_6_, f32[8,768,1]{2,1,0:T(8,128)} %get-tuple-element.90.scale_ref, bf16[8,768,512]{2,1,0:T(8,128)(2,1)} %get-tuple-element.91.low_ref, bf16[8,768,512]{2,1,0:T(8,128)(2,1)} %get-tuple-element.92.dr_ref, ...), custom_call_target="tpu_custom_call" | custom-call | flops 62914560 | bytes 34603008 | tf_op jit(solution)/shard_map/norm_one_back/pallas_call | solution.py:540
  363.1 2.3 fusion.8
  (110 shorter events, 8.9 us)
Async XLA Ops:
  7.2 96.6 %all-gather.3.cloned.1.call-start = ((), (), s32[]{:S(2)}) async-start(), calls=%async_computation.2 | async-start | bytes 8650752 | tf_op jit(solution)/shard_map/all_gather | solution.py:657
  9.0 20.2 %all-to-all-start = ((bf16[16,16,512]{2,1,0:T(8,128)(2,1)}), bf16[16,16,512]{2,1,0:T(8,128)(2,1)S(1)}, u32[]{:S(2)}, u32[]{:S(2)}) async-start(bf16[16,16,512]{2,1,0:T(8,128)(2,1)} %bitcast.98), calls=%async_computation | async-start | bytes 524288 | tf_op jit(solution)/shard_map/all_to_all | solution.py:592
  28.3 36.9 %copy-start.6 = (f32[4608]{0:T(1024)S(1)}, f32[4608]{0:T(1024)}, u32[]{:S(2)}) copy-start(f32[4608]{0:T(1024)} %param.15) | copy-start | bytes 55300
  29.9 6.8 %collective-permute-start = (bf16[80,512]{1,0:T(8,128)(2,1)S(1)}, bf16[80,512]{1,0:T(8,128)(2,1)S(1)}, u32[]{:S(2)}, u32[]{:S(2)}) collective-permute-start(bf16[80,512]{1,0:T(8,128)(2,1)S(1)} %get-tuple-element.119), channel_id=1, source_target_pairs={{0,8},{2,10},{4,12},{6,14},{8,0},{10,2},{12,4},{14,6},{16,24},{18,... | collective-permute-start | bytes 245768 | tf_op jit(solution)/shard_map/ppermute | solution.py:564
  31.9 9.6 %collective-permute-start.1 = (bf16[80,512]{1,0:T(8,128)(2,1)S(1)}, bf16[80,512]{1,0:T(8,128)(2,1)S(1)}, u32[]{:S(2)}, u32[]{:S(2)}) collective-permute-start(bf16[80,512]{1,0:T(8,128)(2,1)S(1)} %get-tuple-element.119), channel_id=1, source_target_pairs={{0,16},{2,18},{4,20},{6,22},{8,24},{10,26},{12,28},{14,30},{16,0},... | collective-permute-start | bytes 245768 | tf_op jit(solution)/shard_map/ppermute | solution.py:564
  34.2 7.3 %collective-permute-start.2 = (bf16[80,512]{1,0:T(8,128)(2,1)S(1)}, bf16[80,512]{1,0:T(8,128)(2,1)S(1)}, u32[]{:S(2)}, u32[]{:S(2)}) collective-permute-start(bf16[80,512]{1,0:T(8,128)(2,1)S(1)} %get-tuple-element.119), channel_id=1, source_target_pairs={{0,24},{2,26},{4,28},{6,30},{8,16},{10,18},{12,20},{14,22},{16,8},... | collective-permute-start | bytes 245768 | tf_op jit(solution)/shard_map/ppermute | solution.py:564
  41.6 16.7 %collective-permute-start.3 = (bf16[4,80,512]{2,1,0:T(8,128)(2,1)S(1)}, bf16[4,80,512]{2,1,0:T(8,128)(2,1)S(1)}, u32[]{:S(2)}, u32[]{:S(2)}) collective-permute-start(bf16[4,80,512]{2,1,0:T(8,128)(2,1)S(1)} %get-tuple-element.117), channel_id=1, source_target_pairs={{0,2},{2,0},{4,6},{6,4},{8,10},{10,8},{12,14},{14,12},{16,18},{18,... | collective-permute-start | bytes 983048 | tf_op jit(solution)/shard_map/ppermute | solution.py:564
  43.1 15.3 %collective-permute-start.4 = (bf16[4,80,512]{2,1,0:T(8,128)(2,1)S(1)}, bf16[4,80,512]{2,1,0:T(8,128)(2,1)S(1)}, u32[]{:S(2)}, u32[]{:S(2)}) collective-permute-start(bf16[4,80,512]{2,1,0:T(8,128)(2,1)S(1)} %get-tuple-element.117), channel_id=1, source_target_pairs={{0,4},{2,6},{4,0},{6,2},{8,12},{10,14},{12,8},{14,10},{16,20},{18,... | collective-permute-start | bytes 983048 | tf_op jit(solution)/shard_map/ppermute | solution.py:564
  44.2 20.8 %collective-permute-start.5 = (bf16[4,80,512]{2,1,0:T(8,128)(2,1)S(1)}, bf16[4,80,512]{2,1,0:T(8,128)(2,1)S(1)}, u32[]{:S(2)}, u32[]{:S(2)}) collective-permute-start(bf16[4,80,512]{2,1,0:T(8,128)(2,1)S(1)} %get-tuple-element.117), channel_id=1, source_target_pairs={{0,6},{2,4},{4,2},{6,0},{8,14},{10,12},{12,10},{14,8},{16,22},{18,... | collective-permute-start | bytes 983048 | tf_op jit(solution)/shard_map/ppermute | solution.py:564
  65.1 3.2 copy-start
  65.1 3.2 collective-permute-start.6
  103.8 110.2 %copy-start.13 = (s32[12]{0:T(128)S(1)}, s32[12]{0:T(128)}, u32[]{:S(2)}) copy-start(s32[12]{0:T(128)} %owner.5) | copy-start | bytes 148
  213.9 4.8 %collective-permute-start.7 = (bf16[4,4,144,512]{3,2,1,0:T(8,128)(2,1)}, bf16[4,4,144,512]{3,2,1,0:T(8,128)(2,1)S(1)}, u32[]{:S(2)}, u32[]{:S(2)}) collective-permute-start(bf16[4,4,144,512]{3,2,1,0:T(8,128)(2,1)} %get-tuple-element.57), channel_id=1, source_target_pairs={{0,1},{1,0},{2,3},{3,2},{4,5},{5,4},{6,7},{7,6},{8,9},{9,8},{10,11... | collective-permute-start | bytes 7077896 | tf_op jit(solution)/shard_map/ppermute | solution.py:564
  214.6 4.1 %copy-start.17 = (s32[16]{0:T(128)}, s32[16]{0:T(128)S(1)}, u32[]{:S(2)}) copy-start(s32[16]{0:T(128)S(1)} %get-tuple-element.84) | copy-start | bytes 196
  221.3 73.0 %collective-permute-start.10 = (bf16[4,144,512]{2,1,0:T(8,128)(2,1)S(1)}, bf16[4,144,512]{2,1,0:T(8,128)(2,1)}, u32[]{:S(2)}, u32[]{:S(2)}) collective-permute-start(bf16[4,144,512]{2,1,0:T(8,128)(2,1)S(1)} %get-tuple-element.102), channel_id=1, source_target_pairs={{0,6},{2,4},{4,2},{6,0},{8,14},{10,12},{12,10},{14,8},{16,22},{18,... | collective-permute-start | bytes 1769480 | tf_op jit(solution)/shard_map/ppermute | solution.py:564
  221.3 73.0 %collective-permute-start.8 = (bf16[4,144,512]{2,1,0:T(8,128)(2,1)S(1)}, bf16[4,144,512]{2,1,0:T(8,128)(2,1)}, u32[]{:S(2)}, u32[]{:S(2)}) collective-permute-start(bf16[4,144,512]{2,1,0:T(8,128)(2,1)S(1)} %get-tuple-element.101), channel_id=1, source_target_pairs={{0,2},{2,0},{4,6},{6,4},{8,10},{10,8},{12,14},{14,12},{16,18},{18,... | collective-permute-start | bytes 1769480 | tf_op jit(solution)/shard_map/ppermute | solution.py:564
  222.4 71.9 %collective-permute-start.9 = (bf16[4,144,512]{2,1,0:T(8,128)(2,1)S(1)}, bf16[4,144,512]{2,1,0:T(8,128)(2,1)}, u32[]{:S(2)}, u32[]{:S(2)}) collective-permute-start(bf16[4,144,512]{2,1,0:T(8,128)(2,1)S(1)} %get-tuple-element.103), channel_id=1, source_target_pairs={{0,4},{2,6},{4,0},{6,2},{8,12},{10,14},{12,8},{14,10},{16,20},{18,... | collective-permute-start | bytes 1769480 | tf_op jit(solution)/shard_map/ppermute | solution.py:564
  294.2 2.0 copy-start.18
  294.3 2.0 copy-start.11
  294.3 2.1 copy-start.10
  294.3 2.6 copy-start.14
  294.3 4.3 %copy-start.2 = (bf16[4,4,48,512]{3,2,1,0:T(8,128)(2,1)S(1)}, bf16[4,4,48,512]{3,2,1,0:T(8,128)(2,1)}, u32[]{:S(2)}) copy-start(bf16[4,4,48,512]{3,2,1,0:T(8,128)(2,1)} %get-tuple-element.70) | copy-start | bytes 2359300
  296.2 5.2 %copy-start.12 = (s32[16]{0:T(128)S(1)}, s32[16]{0:T(128)}, u32[]{:S(2)}) copy-start(s32[16]{0:T(128)} %compare_select_fusion) | copy-start | bytes 196
  296.2 5.2 %copy-start.3 = (bf16[8,64,512]{2,1,0:T(8,128)(2,1)S(1)}, bf16[8,64,512]{2,1,0:T(8,128)(2,1)}, u32[]{:S(2)}) copy-start(bf16[8,64,512]{2,1,0:T(8,128)(2,1)} %get-tuple-element.77) | copy-start | bytes 1572868
  296.2 2.4 collective-permute-start.11
  296.3 2.2 collective-permute-start.12
  299.6 7.3 %collective-permute-start.16 = (bf16[144,512]{1,0:T(8,128)(2,1)}, bf16[144,512]{1,0:T(8,128)(2,1)}, u32[]{:S(2)}, u32[]{:S(2)}) collective-permute-start(bf16[144,512]{1,0:T(8,128)(2,1)} %get-tuple-element.110), channel_id=1, source_target_pairs={{0,8},{2,10},{4,12},{6,14},{8,0},{10,2},{12,4},{14,6},{16,24},{18,... | collective-permute-start | bytes 442376 | tf_op jit(solution)/shard_map/ppermute | solution.py:564
  301.9 4.9 %collective-permute-start.19 = (f32[1,4608]{1,0:T(1,128)S(1)}, f32[1,4608]{1,0:T(1,128)S(1)}, u32[]{:S(2)}, u32[]{:S(2)}) collective-permute-start(f32[1,4608]{1,0:T(1,128)S(1)} %add.104), channel_id=1, source_target_pairs={{0,2},{2,0},{4,6},{6,4},{8,10},{10,8},{12,14},{14,12},{16,18},{18,... | collective-permute-start | bytes 55304 | tf_op jit(solution)/shard_map/ppermute | solution.py:564
  302.4 18.5 %collective-permute-start.17 = (bf16[144,512]{1,0:T(8,128)(2,1)S(1)}, bf16[144,512]{1,0:T(8,128)(2,1)}, u32[]{:S(2)}, u32[]{:S(2)}) collective-permute-start(bf16[144,512]{1,0:T(8,128)(2,1)S(1)} %get-tuple-element.112), channel_id=1, source_target_pairs={{0,16},{2,18},{4,20},{6,22},{8,24},{10,26},{12,28},{14,30},{16,0},... | collective-permute-start | bytes 442376 | tf_op jit(solution)/shard_map/ppermute | solution.py:564
  303.1 17.7 %collective-permute-start.18 = (bf16[144,512]{1,0:T(8,128)(2,1)S(1)}, bf16[144,512]{1,0:T(8,128)(2,1)}, u32[]{:S(2)}, u32[]{:S(2)}) collective-permute-start(bf16[144,512]{1,0:T(8,128)(2,1)S(1)} %get-tuple-element.111), channel_id=1, source_target_pairs={{0,24},{2,26},{4,28},{6,30},{8,16},{10,18},{12,20},{14,22},{16,8},... | collective-permute-start | bytes 442376 | tf_op jit(solution)/shard_map/ppermute | solution.py:564
  304.8 17.2 %collective-permute-start.13 = (bf16[4,80,512]{2,1,0:T(8,128)(2,1)S(1)}, bf16[4,80,512]{2,1,0:T(8,128)(2,1)S(1)}, u32[]{:S(2)}, u32[]{:S(2)}) collective-permute-start(bf16[4,80,512]{2,1,0:T(8,128)(2,1)S(1)} %get-tuple-element.104), channel_id=1, source_target_pairs={{0,2},{2,0},{4,6},{6,4},{8,10},{10,8},{12,14},{14,12},{16,18},{18,... | collective-permute-start | bytes 983048 | tf_op jit(solution)/shard_map/ppermute | solution.py:564
  306.8 15.4 %collective-permute-start.14 = (bf16[4,80,512]{2,1,0:T(8,128)(2,1)S(1)}, bf16[4,80,512]{2,1,0:T(8,128)(2,1)S(1)}, u32[]{:S(2)}, u32[]{:S(2)}) collective-permute-start(bf16[4,80,512]{2,1,0:T(8,128)(2,1)S(1)} %get-tuple-element.106), channel_id=1, source_target_pairs={{0,4},{2,6},{4,0},{6,2},{8,12},{10,14},{12,8},{14,10},{16,20},{18,... | collective-permute-start | bytes 983048 | tf_op jit(solution)/shard_map/ppermute | solution.py:564
  306.9 15.3 %collective-permute-start.15 = (bf16[4,80,512]{2,1,0:T(8,128)(2,1)S(1)}, bf16[4,80,512]{2,1,0:T(8,128)(2,1)}, u32[]{:S(2)}, u32[]{:S(2)}) collective-permute-start(bf16[4,80,512]{2,1,0:T(8,128)(2,1)S(1)} %get-tuple-element.105), channel_id=1, source_target_pairs={{0,6},{2,4},{4,2},{6,0},{8,14},{10,12},{12,10},{14,8},{16,22},{18,... | collective-permute-start | bytes 983048 | tf_op jit(solution)/shard_map/ppermute | solution.py:564
  322.0 22.4 %copy-start.15 = (s32[12]{0:T(128)S(1)}, s32[12]{0:T(128)}, u32[]{:S(2)}) copy-start(s32[12]{0:T(128)} %owner.5) | copy-start | bytes 148
  323.3 7.2 %collective-permute-start.23 = (f32[1,4608]{1,0:T(1,128)S(1)}, f32[1,4608]{1,0:T(1,128)S(1)}, u32[]{:S(2)}, u32[]{:S(2)}) collective-permute-start(f32[1,4608]{1,0:T(1,128)S(1)} %add.111), channel_id=1, source_target_pairs={{0,8},{2,10},{4,12},{6,14},{8,0},{10,2},{12,4},{14,6},{16,24},{18,... | collective-permute-start | bytes 55304 | tf_op jit(solution)/shard_map/ppermute | solution.py:564
  324.4 7.9 %collective-permute-start.24 = (f32[1,4608]{1,0:T(1,128)S(1)}, f32[1,4608]{1,0:T(1,128)S(1)}, u32[]{:S(2)}, u32[]{:S(2)}) collective-permute-start(f32[1,4608]{1,0:T(1,128)S(1)} %add.111), channel_id=1, source_target_pairs={{0,16},{2,18},{4,20},{6,22},{8,24},{10,26},{12,28},{14,30},{16,0},... | collective-permute-start | bytes 55304 | tf_op jit(solution)/shard_map/ppermute | solution.py:564
  326.0 6.2 %collective-permute-start.25 = (f32[1,4608]{1,0:T(1,128)S(1)}, f32[1,4608]{1,0:T(1,128)S(1)}, u32[]{:S(2)}, u32[]{:S(2)}) collective-permute-start(f32[1,4608]{1,0:T(1,128)S(1)} %add.111), channel_id=1, source_target_pairs={{0,24},{2,26},{4,28},{6,30},{8,16},{10,18},{12,20},{14,22},{16,8},... | collective-permute-start | bytes 55304 | tf_op jit(solution)/shard_map/ppermute | solution.py:564
  327.8 6.2 %collective-permute-start.20 = (bf16[80,512]{1,0:T(8,128)(2,1)S(1)}, bf16[80,512]{1,0:T(8,128)(2,1)S(1)}, u32[]{:S(2)}, u32[]{:S(2)}) collective-permute-start(bf16[80,512]{1,0:T(8,128)(2,1)S(1)} %get-tuple-element.113), channel_id=1, source_target_pairs={{0,8},{2,10},{4,12},{6,14},{8,0},{10,2},{12,4},{14,6},{16,24},{18,... | collective-permute-start | bytes 245768 | tf_op jit(solution)/shard_map/ppermute | solution.py:564
  328.0 6.9 %collective-permute-start.21 = (bf16[80,512]{1,0:T(8,128)(2,1)S(1)}, bf16[80,512]{1,0:T(8,128)(2,1)S(1)}, u32[]{:S(2)}, u32[]{:S(2)}) collective-permute-start(bf16[80,512]{1,0:T(8,128)(2,1)S(1)} %get-tuple-element.115), channel_id=1, source_target_pairs={{0,16},{2,18},{4,20},{6,22},{8,24},{10,26},{12,28},{14,30},{16,0},... | collective-permute-start | bytes 245768 | tf_op jit(solution)/shard_map/ppermute | solution.py:564
  330.5 6.2 %collective-permute-start.22 = (bf16[80,512]{1,0:T(8,128)(2,1)S(1)}, bf16[80,512]{1,0:T(8,128)(2,1)S(1)}, u32[]{:S(2)}, u32[]{:S(2)}) collective-permute-start(bf16[80,512]{1,0:T(8,128)(2,1)S(1)} %get-tuple-element.114), channel_id=1, source_target_pairs={{0,24},{2,26},{4,28},{6,30},{8,16},{10,18},{12,20},{14,22},{16,8},... | collective-permute-start | bytes 245768 | tf_op jit(solution)/shard_map/ppermute | solution.py:564
  338.2 24.1 %all-to-all-start.1 = ((bf16[16,16,512]{2,1,0:T(8,128)(2,1)}), bf16[16,16,512]{2,1,0:T(8,128)(2,1)S(1)}, u32[]{:S(2)}, u32[]{:S(2)}) async-start(bf16[16,16,512]{2,1,0:T(8,128)(2,1)} %select_select_fusion), calls=%async_computation.1 | async-start | bytes 524288 | tf_op jit(solution)/shard_map/all_to_all | solution.py:706
  342.5 19.8 %collective-permute-start.26 = (f32[1,4608]{1,0:T(1,128)S(1)}, f32[1,4608]{1,0:T(1,128)S(1)}, u32[]{:S(2)}, u32[]{:S(2)}) collective-permute-start(f32[1,4608]{1,0:T(1,128)S(1)} %add_add_fusion), channel_id=1, source_target_pairs={{0,4},{2,6},{4,0},{6,2},{8,12},{10,14},{12,8},{14,10},{16,20},{18,... | collective-permute-start | bytes 55304 | tf_op jit(solution)/shard_map/ppermute | solution.py:564
  345.7 16.7 %copy-start.7 = (f32[4608]{0:T(1024)S(1)}, f32[4608]{0:T(1024)}, u32[]{:S(2)}) copy-start(f32[4608]{0:T(1024)} %param.15) | copy-start | bytes 55300
  345.7 16.7 %copy-start.8 = (f32[4608]{0:T(1024)S(1)}, f32[4608]{0:T(1024)}, u32[]{:S(2)}) copy-start(f32[4608]{0:T(1024)} %param.16) | copy-start | bytes 55300
  345.7 16.7 %copy-start.9 = (f32[4608]{0:T(1024)S(1)}, f32[4608]{0:T(1024)}, u32[]{:S(2)}) copy-start(f32[4608]{0:T(1024)} %param.17) | copy-start | bytes 55300
  345.7 17.3 %copy-start.1 = (f32[1,256,512]{2,1,0:T(8,128)S(1)}, f32[1,256,512]{2,1,0:T(8,128)}, u32[]{:S(2)}) copy-start(f32[1,256,512]{2,1,0:T(8,128)} %param.12) | copy-start | bytes 1572868
  345.7 17.3 %copy-start.4 = (f32[1,256,512]{2,1,0:T(8,128)S(1)}, f32[1,256,512]{2,1,0:T(8,128)}, u32[]{:S(2)}) copy-start(f32[1,256,512]{2,1,0:T(8,128)} %param.14) | copy-start | bytes 1572868
  345.7 17.3 %copy-start.5 = (f32[1,256,512]{2,1,0:T(8,128)S(1)}, f32[1,256,512]{2,1,0:T(8,128)}, u32[]{:S(2)}) copy-start(f32[1,256,512]{2,1,0:T(8,128)} %param.13) | copy-start | bytes 1572868
  (1 other events, 2.0 us)
Sparse Core Ops, SparseCore 0:
  11.4 88.1 all-gather.2

commit v5 on v4

--- a/solution.py
+++ b/solution.py
@@ -1,5 +1,6 @@
 import functools
 import functools
+import itertools
 import math
 
 import jax
@@ -54,6 +55,11 @@
     return pl.BlockSpec((1,) + tail, lambda step, *_: (step,) + zeros)
 
 
+def two_spec(*tail):
+    zeros = (0,) * len(tail)
+    return pl.BlockSpec((2,) + tail, lambda step, *_: (step,) + zeros)
+
+
 def whole_spec(shape):
     zeros = (0,) * len(shape)
     return pl.BlockSpec(shape, lambda step, *_: zeros, pipeline_mode=pl.Buffered(1))
@@ -68,6 +74,10 @@
 def out_whole(shape):
     zeros = (0,) * len(shape)
     return pl.BlockSpec(shape, lambda step, *_: zeros)
+
+
+def with_ones(rows):
+    return jnp.concatenate([rows, jnp.ones((16, rows.shape[1]), rows.dtype)], 0)
 
 
 def norm_kernel(x_ref, xh_ref, scale_ref, mean_ref):
@@ -75,7 +85,7 @@
     xh_ref[0] = normal.astype(BF16)
     for row in range(mean_ref.shape[1]):
         part = normal[row * ROW : (row + 1) * ROW]
-        mean_ref[0, row : row + 1, :] = jnp.mean(part, 0, keepdims=True)
+        mean_ref[0, row : row + 1, :] = jnp.mean(part, 0, keepdims=True).astype(BF16)
 
 
 def norm_call(tokens):
@@ -89,7 +99,7 @@
         out_shape=[
             jax.ShapeDtypeStruct((images, count, D), BF16),
             jax.ShapeDtypeStruct((images, count, 1), F32),
-            jax.ShapeDtypeStruct((images, rows, D), F32),
+            jax.ShapeDtypeStruct((images, rows, D), BF16),
         ],
         compiler_params=pltpu.CompilerParams(vmem_limit_bytes=60 * MIB),
         cost_estimate=pl.CostEstimate(
@@ -223,11 +233,11 @@
 
 
 def ff_kernel(
-    pieces, finished, owner, place, x_ref, o_ref, cot_ref, li_ref, params_ref,
+    pieces, owner, place, x_ref, o_ref, cot_ref, li_ref, params_ref,
     wo_ref, u0_ref, u1_ref, u2_ref, u3_ref, d0_ref, d1_ref, d2_ref, d3_ref,
-    out_ref, act_ref, h_ref, dr_ref, do_ref, small_ref, *refs
+    out_ref, dr_ref, do_ref, small_ref, *refs
 ):
-    grads_refs, (acc_ref, xh_ref, dp_ref) = refs[:-3], refs[-3:]
+    grads_refs, (acc_ref, h_ref, xh_ref, act_ref, dp_ref) = refs[:-5], refs[-5:]
     gg_ref, gs_ref = small_ref.at[:, 0:D], small_ref.at[:, D : 2 * D]
     gbu_ref, gbd_ref = small_ref.at[:, 2 * D : 2 * D + FF], small_ref.at[:, 2 * D + FF :]
     g_ref, s_ref = params_ref.at[:, 2 * D : 3 * D], params_ref.at[:, 3 * D : 4 * D]
@@ -244,7 +254,7 @@
     hidden = x_ref[0].astype(F32) + dot(o_ref[0], wo_ref[0])
     normal, spread = normalize(hidden)
     xh_ref[...] = normal
-    h_ref[0] = hidden.astype(BF16)
+    h_ref[...] = hidden + bd_ref[...]
     a2 = (normal * g_ref[...] + s_ref[...]).astype(BF16)
     a2_t = a2.T
     cot = cot_ref[0]
@@ -252,8 +262,7 @@
     c_one = math.sqrt(2.0 / math.pi)
     c_two = c_one * 0.044715
     width = D // 2
-    ones = jnp.ones((16, a2_t.shape[1]), BF16)
-    a2_ones = jnp.concatenate([a2_t, ones], 0)
+    a2_ones = with_ones(a2_t)
 
     def first_products(start):
         block, inside = start // D, slice(start % D, start % D + width)
@@ -272,17 +281,12 @@
         slope = half + act * (1.0 - half) * (2.0 * c_one + (6.0 * c_two) * square)
         act = act.astype(BF16)
         d_pre = (d_act * slope).astype(BF16)
-        act_ref[0, :, columns] = act
+        act_ref[:, columns] = act
         dp_ref[:, columns] = d_pre
         part = dot(a2_ones, d_pre)
         acc_ref[1 + block, :, inside] += part[:D]
         gbu_ref[:, columns] += part[D : D + 1]
         acc_ref[1 + NF + block, :, inside] += dot(cot_t, act)
-
-    @pl.when(step < finished)
-    def _():
-        output(act_ref, h_ref, bd_ref, downs, out_ref)
-
     d_a2 = dot_nt(dp_ref[:, 0:D], ups[0][0])
     for block in range(1, NF):
         d_a2 += dot_nt(dp_ref[:, block * D : (block + 1) * D], ups[block][0])
@@ -297,6 +301,10 @@
     d_hidden = cot + spread * (d_normal - middle - normal * along)
     branch = d_hidden.astype(BF16)
     dr_ref[0] = branch
+    total = h_ref[...]
+    for block, down in enumerate(downs):
+        total += dot(act_ref[:, block * D : (block + 1) * D], down[0])
+    out_ref[0] = total.astype(BF16)
     acc_ref[0] += dot(o_ref[0].T, branch)
     do_ref[0] = (dot_nt(branch, wo_ref[0]) * li_ref[0].astype(F32)).astype(BF16)
 
@@ -317,95 +325,46 @@
     return [(inner, outer, blocks * (D // narrow // inner // outer), D)] * narrow
 
 
-def ff_call(owner, place, groups, finished, tokens, attended, cotangent, inverse, params, slots):
+def ff_call(owner, place, groups, tokens, attended, cotangent, inverse, params, slots):
     images, count, _ = tokens.shape
     tokens_shape = jax.ShapeDtypeStruct((images, count, D), BF16)
     blocks = 1 + 2 * NF
     grads = grad_shapes(groups, blocks)
     return pl.pallas_call(
-        functools.partial(ff_kernel, groups is not None, finished),
+        functools.partial(ff_kernel, groups is not None),
         grid_spec=pltpu.PrefetchScalarGridSpec(
             num_scalar_prefetch=2,
             grid=(images,),
             in_specs=[tile_spec(count, D)] * 4
             + [whole_spec(params.shape)]
             + [weight_spec(3 + block) for block in range(blocks)],
-            out_specs=[
-                pl.BlockSpec((1, count, D), lambda step, *_: (jnp.minimum(step, finished - 1), 0, 0)),
-                pl.BlockSpec((1, count, FF), lambda step, *_: (jnp.maximum(step - finished, 0), 0, 0)),
-                pl.BlockSpec((1, count, D), lambda step, *_: (jnp.maximum(step - finished, 0), 0, 0)),
-            ]
-            + [tile_spec(count, D)] * 2
+            out_specs=[tile_spec(count, D)] * 3
             + [out_whole((1, 3 * D + FF))]
             + [out_whole(shape) for shape in grads],
             scratch_shapes=[
                 pltpu.VMEM((blocks, D, D), F32),
                 pltpu.VMEM((count, D), F32),
+                pltpu.VMEM((count, D), F32),
+                pltpu.VMEM((count, FF), BF16),
                 pltpu.VMEM((count, FF), BF16),
             ],
         ),
-        out_shape=[
-            tokens_shape,
-            jax.ShapeDtypeStruct((images - finished, count, FF), BF16),
-            jax.ShapeDtypeStruct((images - finished, count, D), BF16),
-        ]
-        + [tokens_shape] * 2
+        out_shape=[tokens_shape] * 3
         + [jax.ShapeDtypeStruct((1, 3 * D + FF), F32)]
         + [jax.ShapeDtypeStruct(shape, BF16) for shape in grads],
         compiler_params=pltpu.CompilerParams(vmem_limit_bytes=60 * MIB),
         cost_estimate=pl.CostEstimate(
-            flops=images * count * D * D * 46, bytes_accessed=images * count * D * 22, transcendentals=0
+            flops=images * count * D * D * 54, bytes_accessed=images * count * D * 14, transcendentals=0
         ),
         name="feed_forward",
     )(owner, place, tokens, attended, cotangent, inverse, params, *([slots] * blocks))
 
 
-def output(act_ref, h_ref, b_ref, downs, out_ref):
-    total = h_ref[0].astype(F32) + b_ref[...]
-    for block, down in enumerate(downs):
-        total += dot(act_ref[0, :, block * D : (block + 1) * D], down[0])
-    out_ref[0] = total.astype(BF16)
-
-
-def down_kernel(owner, act_ref, h_ref, params_ref, d0_ref, d1_ref, d2_ref, d3_ref, before_ref, out_ref):
-    output(act_ref, h_ref, params_ref.at[:, 4 * D + FF :], (d0_ref, d1_ref, d2_ref, d3_ref), out_ref)
-
-
-def image_spec(start, *tail):
-    zeros = (0,) * len(tail)
-    return pl.BlockSpec((1,) + tail, lambda step, *_: (start + step,) + zeros)
-
-
-def down_call(before, owner, act, hidden, params, slots):
-    images, count, _ = before.shape
-    left = hidden.shape[0]
-    return pl.pallas_call(
-        down_kernel,
-        grid_spec=pltpu.PrefetchScalarGridSpec(
-            num_scalar_prefetch=1,
-            grid=(left,),
-            in_specs=[tile_spec(count, FF), tile_spec(count, D), whole_spec(params.shape)]
-            + [weight_spec(4 + NF + block) for block in range(NF)]
-            + [pl.BlockSpec(memory_space=pl.ANY)],
-            out_specs=image_spec(images - left, count, D),
-        ),
-        out_shape=jax.ShapeDtypeStruct((images, count, D), BF16),
-        input_output_aliases={4 + NF: 0},
-        compiler_params=pltpu.CompilerParams(vmem_limit_bytes=60 * MIB),
-        cost_estimate=pl.CostEstimate(
-            flops=left * count * D * D * 8, bytes_accessed=left * count * D * 12, transcendentals=0
-        ),
-        name="down",
-    )(owner, act, hidden, params, *([slots] * NF), before)
-
-
 def back_kernel(pieces, owner, place, *refs):
     (q_ref, k_ref, v_ref, o_ref, do_ref, e_ref, xh_ref, sk_ref, sv_ref, mean_ref, params_ref) = refs[:11]
-    wq_ref, wk_ref, wv_ref = refs[11:14]
-    g_ref, s_ref = params_ref.at[:, 0:D], params_ref.at[:, D : 2 * D]
-    dlow_ref, dm_ref, small_ref, *grads_refs = refs[14:-4]
-    gg_ref, gs_ref = small_ref.at[:, 0:D], small_ref.at[:, D : 2 * D]
-    acc_ref, grad_ref, dsk_ref, dsv_ref = refs[-4:]
+    weights = refs[11:14]
+    grad_ref, dm_ref, small_ref, *grads_refs = refs[14:-3]
+    acc_ref, dsk_ref, dsv_ref = refs[-3:]
     step = pl.program_id(0)
     rows = q_ref.shape[1] // ROW
     scale = 1.0 / math.sqrt(HD)
@@ -413,7 +372,6 @@
     @pl.when(step == 0)
     def _():
         acc_ref[...] = jnp.zeros_like(acc_ref)
-        small_ref[...] = jnp.zeros_like(small_ref)
 
     sum_k = sk_ref[0]
     sum_v = sv_ref[0]
@@ -447,43 +405,47 @@
                 d_keys.append(dot(q_t[mine], d_score).astype(BF16))
                 part = dot(d_score, keys * masks[half])
                 d_query = part if d_query is None else d_query + part
-            grad_ref[here, lanes] = (d_query * scale).astype(BF16)
+            grad_ref[0, here, lanes] = (d_query * scale).astype(BF16)
         d_key = jnp.concatenate(d_keys, 0).T
         d_value = jnp.concatenate(d_values, 0).T
-        grad_ref[here, D : 2 * D] = d_key[:ROW]
-        grad_ref[here, 2 * D :] = d_value[:ROW]
+        grad_ref[0, here, D : 2 * D] = d_key[:ROW]
+        grad_ref[0, here, 2 * D :] = d_value[:ROW]
         d_sum_k += d_key[ROW:].astype(F32)
         d_sum_v += d_value[ROW:].astype(F32)
     dsk_ref[step] = d_sum_k.astype(BF16)
     dsv_ref[step] = d_sum_v.astype(BF16)
-    normal = xh_ref[0].astype(F32)
-    a_t = (normal * g_ref[...] + s_ref[...]).astype(BF16).T
-    low = jnp.zeros_like(normal)
-    for block, w_ref in enumerate((wq_ref, wk_ref, wv_ref)):
-        columns = slice(block * D, (block + 1) * D)
-        acc_ref[:, columns] += dot(a_t, grad_ref[:, columns])
-        low += dot_nt(grad_ref[:, columns], w_ref[0])
-    dlow_ref[0] = low.astype(BF16)
-    gs_ref[...] += jnp.sum(low, 0, keepdims=True)
-    gg_ref[...] += jnp.sum(low * normal, 0, keepdims=True)
+    acc_ref[...] += dot(with_ones(xh_ref[0].T), grad_ref[0])
 
     @pl.when(step == pl.num_programs(0) - 1)
     def _():
-        mean_x = mean_ref[...].reshape(-1, D).astype(F32)
-        mean_t = (mean_x * g_ref[...] + s_ref[...]).astype(BF16).T
+        mean_t = with_ones(mean_ref[...].reshape(-1, D).T)
         all_k = dsk_ref[...].reshape(-1, D)
         all_v = dsv_ref[...].reshape(-1, D)
         acc_ref[:, D : 2 * D] += dot(mean_t, all_k)
         acc_ref[:, 2 * D :] += dot(mean_t, all_v)
-        d_mean = dot_nt(all_k, wk_ref[0]) + dot_nt(all_v, wv_ref[0])
+        d_mean = dot_nt(all_k, weights[1][0]) + dot_nt(all_v, weights[2][0])
         dm_ref[...] = d_mean.astype(BF16).reshape(dm_ref.shape)
-        gs_ref[...] += jnp.sum(d_mean, 0, keepdims=True)
-        gg_ref[...] += jnp.sum(d_mean * mean_x, 0, keepdims=True)
+        gain_grad = jnp.zeros((D, 1), F32)
+        shift_grad = jnp.zeros((1, D), F32)
+        gain = jnp.broadcast_to(params_ref[:, 0:D], (8, D)).T[:, 0:1]
+        shift = jnp.broadcast_to(params_ref[:, D : 2 * D], (8, D)).T[:, 0:1]
+        for block, w_ref in enumerate(weights):
+            columns = slice(block * D, (block + 1) * D)
+            product = acc_ref[0:D, columns]
+            sums = acc_ref[D : D + 1, columns]
+            gain_grad += jnp.sum(product * w_ref[0].astype(F32), -1, keepdims=True)
+            high = sums.astype(BF16)
+            parts = jnp.concatenate([high, (sums - high.astype(F32)).astype(BF16)], 0)
+            parts = jnp.concatenate([parts, jnp.zeros((14, D), BF16)], 0)
+            shift_grad += jnp.sum(dot_nt(parts, w_ref[0]), 0, keepdims=True)
+            acc_ref[0:D, columns] = product * gain + shift * sums
+        small_ref[:, 0:D] = jnp.broadcast_to(gain_grad, (D, 128)).T[0:1]
+        small_ref[:, D:] = shift_grad
         if pieces:
             write_pieces(place, grads_refs, lambda block, here: acc_ref[here, block * D : (block + 1) * D])
         else:
             for block in range(3):
-                grads_refs[0][block] = acc_ref[:, block * D : (block + 1) * D].astype(BF16)
+                grads_refs[0][block] = acc_ref[0:D, block * D : (block + 1) * D].astype(BF16)
 
 
 def back_call(owner, place, groups, operands, params, slots):
@@ -500,17 +462,16 @@
             + [tile_spec(ROWS_IMG, D)] * 2
             + [whole_spec((images, ROWS_IMG, D)), whole_spec(params.shape)]
             + [weight_spec(block) for block in range(3)],
-            out_specs=[tile_spec(count, D), out_whole((images, ROWS_IMG, D)), out_whole((1, 2 * D))]
+            out_specs=[tile_spec(count, 3 * D), out_whole((images, ROWS_IMG, D)), out_whole((1, 2 * D))]
             + [out_whole(shape) for shape in grads],
             scratch_shapes=[
-                pltpu.VMEM((D, 3 * D), F32),
-                pltpu.VMEM((count, 3 * D), BF16),
+                pltpu.VMEM((D + 16, 3 * D), F32),
                 pltpu.VMEM((images, ROWS_IMG, D), BF16),
                 pltpu.VMEM((images, ROWS_IMG, D), BF16),
             ],
         ),
         out_shape=[
-            jax.ShapeDtypeStruct((images, count, D), BF16),
+            jax.ShapeDtypeStruct((images, count, 3 * D), BF16),
             jax.ShapeDtypeStruct((images, ROWS_IMG, D), BF16),
             jax.ShapeDtypeStruct((1, 2 * D), F32),
         ]
@@ -523,26 +484,50 @@
     )(owner, place, *operands, params, slots, slots, slots)
 
 
+def low_kernel(owner, grad_ref, wq_ref, wk_ref, wv_ref, low_ref):
+    joined = jnp.concatenate([wq_ref[0], wk_ref[0], wv_ref[0]], 1)
+    low_ref[...] = dot_nt(grad_ref[...].reshape(-1, 3 * D), joined).astype(BF16).reshape(low_ref.shape)
+
+
+def low_call(owner, grads, slots):
+    images, count, _ = grads.shape
+    return pl.pallas_call(
+        low_kernel,
+        grid_spec=pltpu.PrefetchScalarGridSpec(
+            num_scalar_prefetch=1,
+            grid=(images // 2,),
+            in_specs=[two_spec(count, 3 * D)] + [weight_spec(block) for block in range(3)],
+            out_specs=two_spec(count, D),
+        ),
+        out_shape=jax.ShapeDtypeStruct((images, count, D), BF16),
+        compiler_params=pltpu.CompilerParams(vmem_limit_bytes=60 * MIB),
+        cost_estimate=pl.CostEstimate(
+            flops=images * count * D * D * 6, bytes_accessed=images * count * D * 8, transcendentals=0
+        ),
+        name="project_back",
+    )(owner, grads, slots, slots, slots)
+
+
 def last_kernel(xh_ref, scale_ref, low_ref, dr_ref, dm_ref, params_ref, out_ref):
     g_ref = params_ref.at[:, 0:D]
-    for row in range(dm_ref.shape[1]):
+    for image, row in itertools.product(range(2), range(dm_ref.shape[1])):
         here = slice(row * ROW, (row + 1) * ROW)
-        normal, spread = xh_ref[0, here, :].astype(F32), scale_ref[0, here, :]
-        total = low_ref[0, here, :].astype(F32) + dm_ref[0, row : row + 1, :] * (1.0 / ROW)
+        normal, spread = xh_ref[image, here, :].astype(F32), scale_ref[image, here, :]
+        total = low_ref[image, here, :].astype(F32) + dm_ref[image, row : row + 1, :] * (1.0 / ROW)
         d_normal = total * g_ref[...]
         middle = jnp.mean(d_normal, -1, keepdims=True)
         along = jnp.mean(d_normal * normal, -1, keepdims=True)
-        out_ref[0, here, :] = dr_ref[0, here, :].astype(F32) + spread * (d_normal - middle - normal * along)
+        out_ref[image, here, :] = dr_ref[image, here, :].astype(F32) + spread * (d_normal - middle - normal * along)
 
 
 def last_call(normal, scale, d_low, d_branch, d_mean, params):
     images, count, _ = normal.shape
     return pl.pallas_call(
         last_kernel,
-        grid=(images,),
-        in_specs=[tile_spec(count, D), tile_spec(count, 1), tile_spec(count, D), tile_spec(count, D)]
-        + [tile_spec(count // ROW, D), whole_spec(params.shape)],
-        out_specs=tile_spec(count, D),
+        grid=(images // 2,),
+        in_specs=[two_spec(count, D), two_spec(count, 1), two_spec(count, D), two_spec(count, D)]
+        + [two_spec(count // ROW, D), whole_spec(params.shape)],
+        out_specs=two_spec(count, D),
         out_shape=jax.ShapeDtypeStruct((images, count, D), F32),
         compiler_params=pltpu.CompilerParams(vmem_limit_bytes=60 * MIB),
         cost_estimate=pl.CostEstimate(
@@ -564,15 +549,15 @@
     return lax.ppermute(value, axis, [(index, index ^ bit) for index in range(size)])
 
 
-def sum_steps():
-    inner, outer = group_sizes(lax.axis_size("wide"))
-
-    def bits(axis, size, stride):
-        return [[(axis, stride << bit)] for bit in range(size.bit_length() - 1)]
-
-    near = bits("wide", inner, 1)
-    far = [[("wide", inner * distance) for distance in range(1, outer)]]
-    return bits("narrow", lax.axis_size("narrow"), 1) + near[:1] + far + near[1:]
+def to_rows(values):
+    high = lax.reduce_precision(values, 8, 7)
+    rows = jnp.concatenate([high, values - high], 1).reshape(-1, D).astype(BF16)
+    return jnp.pad(rows, ((0, -rows.shape[0] % 16), (0, 0)))
+
+
+def from_rows(rows, size):
+    count = size // D
+    return (rows[:count] + rows[count : 2 * count]).reshape(1, size)
 
 
 def join(value):
@@ -665,53 +650,53 @@
     owned = jnp.any(names, 1)
     block_of = jnp.argmax(names, 1)
     place = jnp.stack([me, lax.axis_index("narrow")]).astype(jnp.int32)
+    place, small, owned, block_of, tokens = lax.optimization_barrier((place, small, owned, block_of, tokens))
     normal, scale, means = norm_call(tokens)
-    parts, mean_all = fetch_blocks(low_master, owner_list[:3], means.astype(BF16), groups is not None)
+    parts, mean_all = fetch_blocks(low_master, owner_list[:3], means, groups is not None)
     queries, keys, values, weights, attended, inverse, sum_k, sum_v = attend_call(
         place, normal, mean_all, small, parts
     )
-    half = images // 2
-    block_out, act, hidden, d_branch, d_out, late_small, *grads_late = ff_call(
-        owner_list, place, groups, images - half, tokens, attended, cotangent, inverse, small, slots
+    block_out, d_branch, d_out, late_small, *grads_late = ff_call(
+        owner_list, place, groups, tokens, attended, cotangent, inverse, small, slots
     )
 
     tie = lax.optimization_barrier
     late, queries = tie((sum_narrow(piece_lists(grads_late, groups)), queries))
     operands = (queries, keys, values, attended, d_out, weights, normal, sum_k, sum_v, mean_all)
-    d_low, d_mean, early_small, *grads_early = back_call(
+    d_joined, d_mean, early_small, *grads_early = back_call(
         owner_list, place, groups, operands, small, slots
     )
     late, early_small, *grads_early = tie((sum_near(late), early_small, *grads_early))
     small_sums = jnp.concatenate([early_small, late_small], 1)
-    steps = sum_steps()
-
-    def small_step():
-        total = small_sums
-        for axis, distance in steps.pop(0) if steps else ():
-            total += swap(small_sums, axis, distance)
-        return total
-
-    d_mean = d_mean.reshape(images, wide, rows, D).swapaxes(0, 1).reshape(wide, -1, D)
-    d_mean = by_group(d_mean)
-    early, small_sums, act, late = tie((sum_narrow(piece_lists(grads_early, groups)), small_step(), act, late))
+    size = small_sums.shape[1]
+    bit = 1
+    while bit < narrow:
+        small_sums = small_sums + swap(small_sums, "narrow", bit)
+        bit *= 2
+    d_mean = by_group(d_mean.reshape(images, wide, rows, D).swapaxes(0, 1).reshape(wide, -1, D))
+    early = sum_narrow(piece_lists(grads_early, groups))
+    early, small_sums, d_joined, late = tie((early, small_sums, d_joined, late))
     late = sum_far(late)
-    block_out = down_call(block_out, owner_list, act, hidden, small, slots)
-    early = sum_near(jnp.concatenate([early, d_mean], 2))
-    early, late, small_sums, block_out = tie((early, late, small_step(), block_out))
-    shares, small_sums = tie((sum_far(early), small_step()))
-    own_mean = shares[3 * depth :].reshape(images, rows, D)
-    shares = jnp.concatenate([shares[: 3 * depth], late], 0).reshape(-1, depth, D).astype(BF16)
+    d_low = low_call(owner_list, d_joined, slots)
+
+    cuts = (3 * depth, 3 * depth + images * rows)
+    small_rows = to_rows(small_sums)
+    near = jnp.concatenate([early, d_mean], 2).reshape(inner, outer * cuts[1], D)
+    near = sum_group([jnp.concatenate([near[step], small_rows], 0) for step in range(inner)], 1)
+    near, late, d_low = tie((near, late, d_low))
+    small_rows = to_rows(from_rows(near[outer * cuts[1] :], size))
+    far = near[: outer * cuts[1]].astype(BF16).reshape(outer, cuts[1], D)
+    far = sum_group([jnp.concatenate([far[step], small_rows], 0) for step in range(outer)], inner)
+    own_mean = far[cuts[0] : cuts[1]].reshape(images, rows, D)
+    small_grad = from_rows(far[cuts[1] :], size).reshape(-1)
+    shares = jnp.concatenate([far[: cuts[0]], late], 0).reshape(-1, depth, D).astype(BF16)
 
     moved = jnp.where(owned[:, None, None], jnp.take(shares, block_of, axis=0), jnp.zeros((), BF16))
     moved = lax.all_to_all(moved, "wide", 0, 0, tiled=True)
-    small_sums = small_step()
     grad_tokens = last_call(normal, scale, d_low, d_branch, own_mean, small)
-    moved, small_sums, grad_tokens = tie((moved, small_sums, grad_tokens))
+    moved, grad_tokens = tie((moved, grad_tokens))
     own_grad = moved.reshape(1, -1, D).astype(F32)
-    while steps:
-        small_sums = small_step()
-    small_grad = small_sums.reshape(-1)
-    owns_slot = jnp.any(owner_list == me)
+    owns_slot = owned[me]
     slot_weight, slot_first, slot_second = adamw_update(
         master, own_grad, moment_one, moment_two, 0.1, RATE
     )

time: 373 us -> 373 us (level); the launches traced: 372 us -> 367 us
  Pallas kernels: 254 us -> 247 us
    pallas_call x1, Pallas kernels: 69.4 us -> 60.8 us  [back_call(): pl.pallas_call(functools.partial(back_kernel, groups is not None), grid_s...]
    ppermute x27 -> x22, starting transfers between devices: 31.2 us -> 30.6 us  [swap(): lax.ppermute(value, axis, [(index, index ^ bit) for index in range(size)])]
    ppermute x27 -> x22, waiting for transfers between devices: 37.2 us -> 36.9 us  [swap(): lax.ppermute(value, axis, [(index, index ^ bit) for index in range(size)])]
  transfers between devices with their start and end apart: 30 -> 25, of which waited for: 12 -> 12; matrix products, arithmetic and copies ran while one was open for 3% -> 3% of each run, Pallas kernels for 39% -> 37%
where the time goes in v5:
time: 373 us; the launch traced here: 367 us
  Pallas kernels  247 us (66%)
  starting transfers between devices  43.9 us (12%)
  waiting for transfers between devices  37 us (10%)
  other arithmetic  16.6 us (4%)
  between operations  15 us (4%)
  local copies, waits for them, and re-layouts  7.88 us (2%)
    pallas_call x1, Pallas kernels, ff_call(): pl.pallas_call(functools.partial(ff_kernel, groups is not None), grid_spe...  110 us
    pallas_call x1, Pallas kernels, back_call(): pl.pallas_call(functools.partial(back_kernel, groups is not None), grid_s...  60.8 us
    ppermute x22, waiting for transfers between devices, swap(): lax.ppermute(value, axis, [(index, index ^ bit) for index in range(size)])  36.9 us
    pallas_call x1, Pallas kernels, attend_call(): pl.pallas_call(functools.partial(attend_kernel, len(parts)), grid_spec=pl...  34.3 us
    ppermute x22, starting transfers between devices, swap(): lax.ppermute(value, axis, [(index, index ^ bit) for index in range(size)])  30.6 us
    pallas_call x1, Pallas kernels, low_call(): pl.pallas_call(low_kernel, grid_spec=pltpu.PrefetchScalarGridSpec(num_sca...  15.9 us
    pallas_call x1, Pallas kernels, last_call(): pl.pallas_call(last_kernel, grid=(images // 2,), in_specs=[two_spec(count...  15.2 us
    pallas_call x1, Pallas kernels, norm_call(): pl.pallas_call(norm_kernel, grid=(images,), in_specs=[tile_spec(count, D)...  10.1 us
  transfers between devices with their start and end apart: 25, of which 12 were waited for; matrix products, arithmetic and copies ran while one was open for 3% of the time, Pallas kernels for 37%

profile of v5, /device:TPU:0, one launch (start us, length us, event | category | flops | bytes accessed | tf_op | source)
XLA Modules:
  0.0 366.9 jit_solution(11777284252928723388)
XLA Ops:
  7.2 1.8 convert_element_type.112
  9.0 8.3 %all-to-all-start = ((bf16[16,16,512]{2,1,0:T(8,128)(2,1)}), bf16[16,16,512]{2,1,0:T(8,128)(2,1)S(1)}, u32[]{:S(2)}, u32[]{:S(2)}) async-start(bf16[16,16,512]{2,1,0:T(8,128)(2,1)} %bitcast.84), calls=%async_computation | async-start | bytes 524288 | tf_op jit(solution)/shard_map/all_to_all | solution.py:577
  17.4 1.4 iota_reduce_fusion
  18.7 0.6 pad_add_fusion.place
  19.3 1.3 reshape.151.params_ref.refs_10_
  20.7 1.3 fusion.25
  22.0 10.1 %norm_one.1 = (bf16[8,768,512]{2,1,0:T(8,128)(2,1)}, f32[8,768,1]{2,1,0:T(8,128)}, bf16[8,4,512]{2,1,0:T(4,128)(2,1)}) custom-call(bf16[8,768,512]{2,1,0:T(8,128)(2,1)} %x_ref.1), custom_call_target="tpu_custom_call" | custom-call | flops 31457280 | bytes 12582912 | tf_op jit(solution)/shard_map/norm_one/pallas_call | solution.py:94
  32.1 0.8 reshape.153
  33.8 3.8 %collective-permute-start.2 = (bf16[80,512]{1,0:T(8,128)(2,1)S(1)}, bf16[80,512]{1,0:T(8,128)(2,1)S(1)}, u32[]{:S(2)}, u32[]{:S(2)}) collective-permute-start(bf16[80,512]{1,0:T(8,128)(2,1)S(1)} %get-tuple-element.119), channel_id=1, source_target_pairs={{0,24},{2,26},{4,28},{6,30},{8,16},{10,18},{12,20},{14,22},{16,8},... | collective-permute-start | bytes 245768 | tf_op jit(solution)/shard_map/ppermute | solution.py:549
  37.6 0.6 collective-permute-start
  38.2 2.8 collective-permute-done.2
  41.0 5.9 %collective-permute-done.1 = bf16[80,512]{1,0:T(8,128)(2,1)S(1)} collective-permute-done((bf16[80,512]{1,0:T(8,128)(2,1)S(1)}, bf16[80,512]{1,0:T(8,128)(2,1)S(1)}, u32[]{:S(2)}, u32[]{:S(2)}) %collective-permute-start.1) | collective-permute-done | bytes 81952 | tf_op jit(solution)/shard_map/ppermute | solution.py:549
  47.0 2.4 collective-permute-start.5
  49.4 0.6 collective-permute-start.4
  50.5 8.1 %collective-permute-done.5 = bf16[4,80,512]{2,1,0:T(8,128)(2,1)S(1)} collective-permute-done((bf16[4,80,512]{2,1,0:T(8,128)(2,1)S(1)}, bf16[4,80,512]{2,1,0:T(8,128)(2,1)S(1)}, u32[]{:S(2)}, u32[]{:S(2)}) %collective-permute-start.5) | collective-permute-done | bytes 327712 | tf_op jit(solution)/shard_map/ppermute | solution.py:549
  58.6 4.5 %collective-permute-done.4 = bf16[4,80,512]{2,1,0:T(8,128)(2,1)S(1)} collective-permute-done((bf16[4,80,512]{2,1,0:T(8,128)(2,1)S(1)}, bf16[4,80,512]{2,1,0:T(8,128)(2,1)S(1)}, u32[]{:S(2)}, u32[]{:S(2)}) %collective-permute-start.4) | collective-permute-done | bytes 327712 | tf_op jit(solution)/shard_map/ppermute | solution.py:549
  63.1 0.6 collective-permute-done.3
  64.3 0.9 reshape.156.mean_ref.refs_9_
  65.2 3.7 %collective-permute-done.6.refs_1_ = bf16[16,80,512]{2,1,0:T(8,128)(2,1)} collective-permute-done((bf16[16,80,512]{2,1,0:T(8,128)(2,1)S(1)}, bf16[16,80,512]{2,1,0:T(8,128)(2,1)}, u32[]{:S(2)}, u32[]{:S(2)}) %collective-permute-start.6) | collective-permute-done | bytes 1310752 | tf_op jit(solution)/shard_map/ppermute | solution.py:549
  68.9 34.3 %attend.1 = (bf16[8,768,512]{2,1,0:T(8,128)(2,1)}, bf16[8,768,512]{2,1,0:T(8,128)(2,1)}, bf16[8,768,512]{2,1,0:T(8,128)(2,1)}, bf16[8,4,8,192,256]{4,3,2,1,0:T(8...) custom-call(s32[2]{0:T(128)} %pad_add_fusion.place, ...), custom_call_target="tpu_custom_call" | custom-call | flops 16106127360 | bytes 62914560 | tf_op jit(solution)/shard_map/attend/pallas_call | solution.py:205
  103.3 110.2 %feed_forward.1 = (bf16[8,768,512]{2,1,0:T(8,128)(2,1)}, bf16[8,768,512]{2,1,0:T(8,128)(2,1)}, bf16[8,768,512]{2,1,0:T(8,128)(2,1)}, f32[1,3584]{1,0:T(1,128)}, ...) custom-call(s32[12]{0:T(128)} %owner.5, s32[2]{0:T(128)} %pad_add_fusion.place, ...), custom_call_target="tpu_custom_call" | custom-call | flops 86973087744 | bytes 44040192 | tf_op jit(solution)/shard_map/feed_forward/pallas_call | solution.py:333
  213.8 4.6 %collective-permute-done.7 = bf16[4,4,144,512]{3,2,1,0:T(8,128)(2,1)S(1)} collective-permute-done((bf16[4,4,144,512]{3,2,1,0:T(8,128)(2,1)}, bf16[4,4,144,512]{3,2,1,0:T(8,128)(2,1)S(1)}, u32[]{:S(2)}, u32[]{:S(2)}) %collective-permute-start.7) | collective-permute-done | bytes 2359328 | tf_op jit(solution)/shard_map/ppermute | solution.py:549
  218.4 2.4 add_convert_fusion
  221.0 1.5 collective-permute-start.9
  222.5 1.9 collective-permute-start.8
  224.4 60.8 %attend_back.1 = (bf16[8,768,1536]{2,1,0:T(8,128)(2,1)}, bf16[8,64,512]{2,1,0:T(8,128)(2,1)}, f32[1,1024]{1,0:T(1,128)}, bf16[4,4,48,512]{3,2,1,0:T(8,128)(2,1)}, bf16[4,4,48,512]{3,2,1,0:T(8,128)(2,1)}) custom-call(s32[12]{0:T(128)} %owner.5, s32[2]{0:T(128)} %pad_add_fusion.place, bf16[8,768,512]{2,1,0:T(8,128)(2,1)} %get-tuple-element.66.refs_0_, ...), custom_call_target="tpu_custom_call" | custom-call | flops 32212254720 | bytes 75497472 | tf_op jit(solution)/shard_map/attend_back/pallas_call | solution.py:455
  285.3 1.7 fusion.2
  287.7 1.2 reshape.159
  289.8 1.4 add_convert_fusion.1
  291.2 3.4 collective-permute-start.18
  294.9 1.0 collective-permute-start.15
  295.9 0.7 collective-permute-start.14
  296.5 1.9 collective-permute-start.13
  298.5 0.7 collective-permute-done.18
  299.2 6.7 %collective-permute-start.16 = (bf16[144,512]{1,0:T(8,128)(2,1)S(1)}, bf16[144,512]{1,0:T(8,128)(2,1)S(1)}, u32[]{:S(2)}, u32[]{:S(2)}) collective-permute-start(bf16[144,512]{1,0:T(8,128)(2,1)S(1)} %get-tuple-element.109), channel_id=1, source_target_pairs={{0,8},{2,10},{4,12},{6,14},{8,0},{10,2},{12,4},{14,6},{16,24},{18,... | collective-permute-start | bytes 442376 | tf_op jit(solution)/shard_map/ppermute | solution.py:549
  305.9 15.9 %project_back.1.low_ref = bf16[8,768,512]{2,1,0:T(8,128)(2,1)} custom-call(s32[12]{0:T(128)} %owner.5, bf16[8,768,1536]{2,1,0:T(8,128)(2,1)} %get-tuple-element.86.grad_ref, bf16[16,512,512]{2,1,0:T(8,128)(2,1)} %bitcast.78, bf16[16,512,512]{2,1,0:T(8,128)(2,1)} %bitcast.79, bf16[16,512,512]{2,1,0:T(8,128)(2,1)} %bitcast.80), custom_call_target="tpu_custom_call" | custom-call | flops 9663676416 | bytes 25165824 | tf_op jit(solution)/shard_map/project_back/pallas_call | solution.py:494
  321.8 1.0 fusion.16
  323.4 2.4 collective-permute-start.21
  325.8 2.0 collective-permute-start.19
  327.8 3.1 collective-permute-done.21
  330.9 2.6 collective-permute-done.20
  334.2 0.8 select_select_fusion
  335.0 4.9 %all-to-all-start.1 = ((bf16[16,16,512]{2,1,0:T(8,128)(2,1)}), bf16[16,16,512]{2,1,0:T(8,128)(2,1)S(1)}, u32[]{:S(2)}, u32[]{:S(2)}) async-start(bf16[16,16,512]{2,1,0:T(8,128)(2,1)} %select_select_fusion), calls=%async_computation.1 | async-start | bytes 524288 | tf_op jit(solution)/shard_map/all_to_all | solution.py:695
  340.0 0.7 dynamic_slice.3
  340.6 0.7 reshape.161.dm_ref
  341.4 15.2 %norm_one_back.1 = f32[8,768,512]{2,1,0:T(8,128)} custom-call(bf16[8,768,512]{2,1,0:T(8,128)(2,1)} %get-tuple-element.54.xh_ref.refs_6_, f32[8,768,1]{2,1,0:T(8,128)} %get-tuple-element.89.scale_ref, bf16[8,768,512]{2,1,0:T(8,128)(2,1)} %project_back.1.low_ref, bf16[8,768,512]{2,1,0:T(8,128)(2,1)} %get-tuple-element.91.dr_ref, ...), custom_call_target="tpu_custom_call" | custom-call | flops 62914560 | bytes 34603008 | tf_op jit(solution)/shard_map/norm_one_back/pallas_call | solution.py:525
  356.6 0.6 multiply_subtract_fusion
  357.2 2.4 fusion.6
  (98 shorter events, 5.6 us)
Async XLA Ops:
  7.2 96.1 %all-gather.3.cloned.1.call-start = ((), (), s32[]{:S(2)}) async-start(), calls=%async_computation.2 | async-start | bytes 8650752 | tf_op jit(solution)/shard_map/all_gather | solution.py:642
  9.0 24.1 %all-to-all-start = ((bf16[16,16,512]{2,1,0:T(8,128)(2,1)}), bf16[16,16,512]{2,1,0:T(8,128)(2,1)S(1)}, u32[]{:S(2)}, u32[]{:S(2)}) async-start(bf16[16,16,512]{2,1,0:T(8,128)(2,1)} %bitcast.84), calls=%async_computation | async-start | bytes 524288 | tf_op jit(solution)/shard_map/all_to_all | solution.py:577
  22.0 10.9 %copy-start.10 = (s32[12]{0:T(128)S(1)}, s32[12]{0:T(128)}, u32[]{:S(2)}) copy-start(s32[12]{0:T(128)} %owner.5) | copy-start | bytes 148
  33.8 7.2 %collective-permute-start.2 = (bf16[80,512]{1,0:T(8,128)(2,1)S(1)}, bf16[80,512]{1,0:T(8,128)(2,1)S(1)}, u32[]{:S(2)}, u32[]{:S(2)}) collective-permute-start(bf16[80,512]{1,0:T(8,128)(2,1)S(1)} %get-tuple-element.119), channel_id=1, source_target_pairs={{0,24},{2,26},{4,28},{6,30},{8,16},{10,18},{12,20},{14,22},{16,8},... | collective-permute-start | bytes 245768 | tf_op jit(solution)/shard_map/ppermute | solution.py:549
  37.6 9.3 %collective-permute-start.1 = (bf16[80,512]{1,0:T(8,128)(2,1)S(1)}, bf16[80,512]{1,0:T(8,128)(2,1)S(1)}, u32[]{:S(2)}, u32[]{:S(2)}) collective-permute-start(bf16[80,512]{1,0:T(8,128)(2,1)S(1)} %get-tuple-element.119), channel_id=1, source_target_pairs={{0,16},{2,18},{4,20},{6,22},{8,24},{10,26},{12,28},{14,30},{16,0},... | collective-permute-start | bytes 245768 | tf_op jit(solution)/shard_map/ppermute | solution.py:549
  37.6 9.3 %collective-permute-start = (bf16[80,512]{1,0:T(8,128)(2,1)S(1)}, bf16[80,512]{1,0:T(8,128)(2,1)S(1)}, u32[]{:S(2)}, u32[]{:S(2)}) collective-permute-start(bf16[80,512]{1,0:T(8,128)(2,1)S(1)} %get-tuple-element.119), channel_id=1, source_target_pairs={{0,8},{2,10},{4,12},{6,14},{8,0},{10,2},{12,4},{14,6},{16,24},{18,... | collective-permute-start | bytes 245768 | tf_op jit(solution)/shard_map/ppermute | solution.py:549
  47.0 11.6 %collective-permute-start.5 = (bf16[4,80,512]{2,1,0:T(8,128)(2,1)S(1)}, bf16[4,80,512]{2,1,0:T(8,128)(2,1)S(1)}, u32[]{:S(2)}, u32[]{:S(2)}) collective-permute-start(bf16[4,80,512]{2,1,0:T(8,128)(2,1)S(1)} %get-tuple-element.117), channel_id=1, source_target_pairs={{0,6},{2,4},{4,2},{6,0},{8,14},{10,12},{12,10},{14,8},{16,22},{18,... | collective-permute-start | bytes 983048 | tf_op jit(solution)/shard_map/ppermute | solution.py:549
  49.4 13.7 %collective-permute-start.4 = (bf16[4,80,512]{2,1,0:T(8,128)(2,1)S(1)}, bf16[4,80,512]{2,1,0:T(8,128)(2,1)S(1)}, u32[]{:S(2)}, u32[]{:S(2)}) collective-permute-start(bf16[4,80,512]{2,1,0:T(8,128)(2,1)S(1)} %get-tuple-element.117), channel_id=1, source_target_pairs={{0,4},{2,6},{4,0},{6,2},{8,12},{10,14},{12,8},{14,10},{16,20},{18,... | collective-permute-start | bytes 983048 | tf_op jit(solution)/shard_map/ppermute | solution.py:549
  50.0 13.7 %collective-permute-start.3 = (bf16[4,80,512]{2,1,0:T(8,128)(2,1)S(1)}, bf16[4,80,512]{2,1,0:T(8,128)(2,1)S(1)}, u32[]{:S(2)}, u32[]{:S(2)}) collective-permute-start(bf16[4,80,512]{2,1,0:T(8,128)(2,1)S(1)} %get-tuple-element.117), channel_id=1, source_target_pairs={{0,2},{2,0},{4,6},{6,4},{8,10},{10,8},{12,14},{14,12},{16,18},{18,... | collective-permute-start | bytes 983048 | tf_op jit(solution)/shard_map/ppermute | solution.py:549
  63.9 5.1 %copy-start = (bf16[4,4,80,512]{3,2,1,0:T(8,128)(2,1)}, bf16[4,4,80,512]{3,2,1,0:T(8,128)(2,1)S(1)}, u32[]{:S(2)}) copy-start(bf16[4,4,80,512]{3,2,1,0:T(8,128)(2,1)S(1)} %pad_maximum_fusion) | copy-start | bytes 3932164
  63.9 5.1 %collective-permute-start.6 = (bf16[16,80,512]{2,1,0:T(8,128)(2,1)S(1)}, bf16[16,80,512]{2,1,0:T(8,128)(2,1)}, u32[]{:S(2)}, u32[]{:S(2)}) collective-permute-start(bf16[16,80,512]{2,1,0:T(8,128)(2,1)S(1)} %bitcast.81), channel_id=1, source_target_pairs={{0,1},{1,0},{2,3},{3,2},{4,5},{5,4},{6,7},{7,6},{8,9},{9,8},{10,11... | collective-permute-start | bytes 3932168 | tf_op jit(solution)/shard_map/ppermute | solution.py:549
  213.5 4.8 %collective-permute-start.7 = (bf16[4,4,144,512]{3,2,1,0:T(8,128)(2,1)}, bf16[4,4,144,512]{3,2,1,0:T(8,128)(2,1)S(1)}, u32[]{:S(2)}, u32[]{:S(2)}) collective-permute-start(bf16[4,4,144,512]{3,2,1,0:T(8,128)(2,1)} %get-tuple-element.63), channel_id=1, source_target_pairs={{0,1},{1,0},{2,3},{3,2},{4,5},{5,4},{6,7},{7,6},{8,9},{9,8},{10,11... | collective-permute-start | bytes 7077896 | tf_op jit(solution)/shard_map/ppermute | solution.py:549
  220.9 64.4 %collective-permute-start.10 = (bf16[4,144,512]{2,1,0:T(8,128)(2,1)S(1)}, bf16[4,144,512]{2,1,0:T(8,128)(2,1)}, u32[]{:S(2)}, u32[]{:S(2)}) collective-permute-start(bf16[4,144,512]{2,1,0:T(8,128)(2,1)S(1)} %get-tuple-element.100), channel_id=1, source_target_pairs={{0,6},{2,4},{4,2},{6,0},{8,14},{10,12},{12,10},{14,8},{16,22},{18,... | collective-permute-start | bytes 1769480 | tf_op jit(solution)/shard_map/ppermute | solution.py:549
  221.0 64.3 %collective-permute-start.9 = (bf16[4,144,512]{2,1,0:T(8,128)(2,1)S(1)}, bf16[4,144,512]{2,1,0:T(8,128)(2,1)}, u32[]{:S(2)}, u32[]{:S(2)}) collective-permute-start(bf16[4,144,512]{2,1,0:T(8,128)(2,1)S(1)} %get-tuple-element.101), channel_id=1, source_target_pairs={{0,4},{2,6},{4,0},{6,2},{8,12},{10,14},{12,8},{14,10},{16,20},{18,... | collective-permute-start | bytes 1769480 | tf_op jit(solution)/shard_map/ppermute | solution.py:549
  222.5 62.8 %collective-permute-start.8 = (bf16[4,144,512]{2,1,0:T(8,128)(2,1)S(1)}, bf16[4,144,512]{2,1,0:T(8,128)(2,1)}, u32[]{:S(2)}, u32[]{:S(2)}) collective-permute-start(bf16[4,144,512]{2,1,0:T(8,128)(2,1)S(1)} %get-tuple-element.99), channel_id=1, source_target_pairs={{0,2},{2,0},{4,6},{6,4},{8,10},{10,8},{12,14},{14,12},{16,18},{18,... | collective-permute-start | bytes 1769480 | tf_op jit(solution)/shard_map/ppermute | solution.py:549
  285.3 1.9 copy-start.9
  285.3 1.9 copy-start.8
  285.3 2.4 copy-start.12
  287.1 2.7 copy-start.2
  287.1 2.7 collective-permute-start.11
  287.2 2.3 collective-permute-start.12
  291.2 8.0 %collective-permute-start.18 = (bf16[144,512]{1,0:T(8,128)(2,1)S(1)}, bf16[144,512]{1,0:T(8,128)(2,1)}, u32[]{:S(2)}, u32[]{:S(2)}) collective-permute-start(bf16[144,512]{1,0:T(8,128)(2,1)S(1)} %get-tuple-element.110), channel_id=1, source_target_pairs={{0,24},{2,26},{4,28},{6,30},{8,16},{10,18},{12,20},{14,22},{16,8},... | collective-permute-start | bytes 442376 | tf_op jit(solution)/shard_map/ppermute | solution.py:549
  294.9 27.9 %collective-permute-start.15 = (bf16[352,512]{1,0:T(8,128)(2,1)S(1)}, bf16[352,512]{1,0:T(8,128)(2,1)S(1)}, u32[]{:S(2)}, u32[]{:S(2)}) collective-permute-start(bf16[352,512]{1,0:T(8,128)(2,1)S(1)} %get-tuple-element.125), channel_id=1, source_target_pairs={{0,6},{2,4},{4,2},{6,0},{8,14},{10,12},{12,10},{14,8},{16,22},{18,... | collective-permute-start | bytes 1081352 | tf_op jit(solution)/shard_map/ppermute | solution.py:549
  295.9 26.9 %collective-permute-start.14 = (bf16[352,512]{1,0:T(8,128)(2,1)S(1)}, bf16[352,512]{1,0:T(8,128)(2,1)S(1)}, u32[]{:S(2)}, u32[]{:S(2)}) collective-permute-start(bf16[352,512]{1,0:T(8,128)(2,1)S(1)} %get-tuple-element.124), channel_id=1, source_target_pairs={{0,4},{2,6},{4,0},{6,2},{8,12},{10,14},{12,8},{14,10},{16,20},{18,... | collective-permute-start | bytes 1081352 | tf_op jit(solution)/shard_map/ppermute | solution.py:549
  296.5 26.3 %collective-permute-start.13 = (bf16[352,512]{1,0:T(8,128)(2,1)S(1)}, bf16[352,512]{1,0:T(8,128)(2,1)S(1)}, u32[]{:S(2)}, u32[]{:S(2)}) collective-permute-start(bf16[352,512]{1,0:T(8,128)(2,1)S(1)} %get-tuple-element.123), channel_id=1, source_target_pairs={{0,2},{2,0},{4,6},{6,4},{8,10},{10,8},{12,14},{14,12},{16,18},{18,... | collective-permute-start | bytes 1081352 | tf_op jit(solution)/shard_map/ppermute | solution.py:549
  298.5 23.3 %collective-permute-start.17 = (bf16[144,512]{1,0:T(8,128)(2,1)S(1)}, bf16[144,512]{1,0:T(8,128)(2,1)S(1)}, u32[]{:S(2)}, u32[]{:S(2)}) collective-permute-start(bf16[144,512]{1,0:T(8,128)(2,1)S(1)} %get-tuple-element.111), channel_id=1, source_target_pairs={{0,16},{2,18},{4,20},{6,22},{8,24},{10,26},{12,28},{14,30},{16,0},... | collective-permute-start | bytes 442376 | tf_op jit(solution)/shard_map/ppermute | solution.py:549
  299.2 22.6 %collective-permute-start.16 = (bf16[144,512]{1,0:T(8,128)(2,1)S(1)}, bf16[144,512]{1,0:T(8,128)(2,1)S(1)}, u32[]{:S(2)}, u32[]{:S(2)}) collective-permute-start(bf16[144,512]{1,0:T(8,128)(2,1)S(1)} %get-tuple-element.109), channel_id=1, source_target_pairs={{0,8},{2,10},{4,12},{6,14},{8,0},{10,2},{12,4},{14,6},{16,24},{18,... | collective-permute-start | bytes 442376 | tf_op jit(solution)/shard_map/ppermute | solution.py:549
  322.8 5.0 %copy-start.13 = (s32[16]{0:T(128)S(1)}, s32[16]{0:T(128)}, u32[]{:S(2)}) copy-start(s32[16]{0:T(128)} %get-tuple-element.61) | copy-start | bytes 196
  323.0 11.2 %copy-start.11 = (pred[16]{0:T(512)(128)(4,1)S(1)}, pred[16]{0:T(512)(128)(4,1)}, u32[]{:S(2)}) copy-start(pred[16]{0:T(512)(128)(4,1)} %fusion.25) | copy-start | bytes 52
  323.4 7.5 %collective-permute-start.21 = (bf16[112,512]{1,0:T(8,128)(2,1)S(1)}, bf16[112,512]{1,0:T(8,128)(2,1)S(1)}, u32[]{:S(2)}, u32[]{:S(2)}) collective-permute-start(bf16[112,512]{1,0:T(8,128)(2,1)S(1)} %get-tuple-element.122), channel_id=1, source_target_pairs={{0,24},{2,26},{4,28},{6,30},{8,16},{10,18},{12,20},{14,22},{16,8},... | collective-permute-start | bytes 344072 | tf_op jit(solution)/shard_map/ppermute | solution.py:549
  325.8 7.7 %collective-permute-start.20 = (bf16[112,512]{1,0:T(8,128)(2,1)S(1)}, bf16[112,512]{1,0:T(8,128)(2,1)S(1)}, u32[]{:S(2)}, u32[]{:S(2)}) collective-permute-start(bf16[112,512]{1,0:T(8,128)(2,1)S(1)} %get-tuple-element.121), channel_id=1, source_target_pairs={{0,16},{2,18},{4,20},{6,22},{8,24},{10,26},{12,28},{14,30},{16,0},... | collective-permute-start | bytes 344072 | tf_op jit(solution)/shard_map/ppermute | solution.py:549
  325.8 7.7 %collective-permute-start.19 = (bf16[112,512]{1,0:T(8,128)(2,1)S(1)}, bf16[112,512]{1,0:T(8,128)(2,1)S(1)}, u32[]{:S(2)}, u32[]{:S(2)}) collective-permute-start(bf16[112,512]{1,0:T(8,128)(2,1)S(1)} %get-tuple-element.120), channel_id=1, source_target_pairs={{0,8},{2,10},{4,12},{6,14},{8,0},{10,2},{12,4},{14,6},{16,24},{18,... | collective-permute-start | bytes 344072 | tf_op jit(solution)/shard_map/ppermute | solution.py:549
  335.0 22.2 %all-to-all-start.1 = ((bf16[16,16,512]{2,1,0:T(8,128)(2,1)}), bf16[16,16,512]{2,1,0:T(8,128)(2,1)S(1)}, u32[]{:S(2)}, u32[]{:S(2)}) async-start(bf16[16,16,512]{2,1,0:T(8,128)(2,1)} %select_select_fusion), calls=%async_computation.1 | async-start | bytes 524288 | tf_op jit(solution)/shard_map/all_to_all | solution.py:695
  341.3 15.3 %copy-start.5 = (f32[4608]{0:T(1024)S(1)}, f32[4608]{0:T(1024)}, u32[]{:S(2)}) copy-start(f32[4608]{0:T(1024)} %param.15) | copy-start | bytes 55300
  341.3 15.2 %copy-start.6 = (f32[4608]{0:T(1024)S(1)}, f32[4608]{0:T(1024)}, u32[]{:S(2)}) copy-start(f32[4608]{0:T(1024)} %param.16) | copy-start | bytes 55300
  341.3 15.2 %copy-start.7 = (f32[4608]{0:T(1024)S(1)}, f32[4608]{0:T(1024)}, u32[]{:S(2)}) copy-start(f32[4608]{0:T(1024)} %param.17) | copy-start | bytes 55300
  341.3 15.9 %copy-start.1 = (f32[1,256,512]{2,1,0:T(8,128)S(1)}, f32[1,256,512]{2,1,0:T(8,128)}, u32[]{:S(2)}) copy-start(f32[1,256,512]{2,1,0:T(8,128)} %param.12) | copy-start | bytes 1572868
  341.3 15.9 %copy-start.3 = (f32[1,256,512]{2,1,0:T(8,128)S(1)}, f32[1,256,512]{2,1,0:T(8,128)}, u32[]{:S(2)}) copy-start(f32[1,256,512]{2,1,0:T(8,128)} %param.14) | copy-start | bytes 1572868
  341.4 15.9 %copy-start.4 = (f32[1,256,512]{2,1,0:T(8,128)S(1)}, f32[1,256,512]{2,1,0:T(8,128)}, u32[]{:S(2)}) copy-start(f32[1,256,512]{2,1,0:T(8,128)} %param.13) | copy-start | bytes 1572868
Sparse Core Ops, SparseCore 0:
  10.9 83.1 all-gather.2
